TPU v7x, 512 devices: a whole 4x8x8 slice. The times are simulated.
512 devices in a mesh: rep: 16 (over y, x_lo), fsdp: 32 (over x_hi, z, core).
Axes of the slice: x: 4 (x_hi: 2, x_lo: 2; x = x_hi * 2 + x_lo), y: 8, z: 8, core: 2. Of those that a mesh axis runs over, the one named last changes fastest.
Arguments:
- pseudo_grad: float32 [16, 16384, 256], P('rep', 'fsdp'), may hold values from -6 to 6
- error_buf: float32 [16, 16384, 256], P('rep', 'fsdp'), may hold values from -6 to 6
- momentum: float32 [16384, 256], P('fsdp'), may hold values from -4 to 4
- params: float32 [16384, 256], P('fsdp'), may hold values from -6 to 6
- picks: int32 [16, 256], P('rep', 'fsdp'), may hold values from 0 to 511, as said below
Outputs:
- new_params: float32 [16384, 256], P('fsdp')
- new_momentum: float32 [16384, 256], P('fsdp')
- new_error: float32 [16, 16384, 256], P('rep', 'fsdp')
- gathered: bfloat16 [16384, 256], replicated
Inputs may be any that keep to these rules, and one draw needn't show every extreme that they name: `picks`: entries j of a row with the same j // 8 are distinct.
All inputs are finite; a program needn't handle non-finite values.
Results may differ from a plain program's by a relative error of at most 0.0017.
Values may be sent and summed in bfloat16 or wider, within the bound.
No kernel may reach another device: no remote copies, remote signals or barrier semaphores. Data moves between devices by JAX's collectives and lax.ppermute only.
A program may use at most 64 MiB of HBM per device.

v0:
```python
import jax
import jax.numpy as jnp
from jax import lax
from jax.sharding import PartitionSpec as P

DECAY_RATE = 0.95
MOMENTUM_COEF = 0.9
STEP_SCALE = 0.7


def per_device(pseudo_grad, error_buf, momentum, params, picks):
    shard_blocks = params.shape[0]
    replicas = lax.axis_size("rep")
    accumulated = DECAY_RATE * error_buf[0] + pseudo_grad[0]
    own_picks = picks[0]
    positions = lax.iota(jnp.int32, shard_blocks)
    selector = (own_picks[:, None] == positions[None, :]).astype(jnp.float32)
    chosen_mask = jnp.sum(selector, axis=0)
    new_error = (accumulated * (1.0 - chosen_mask)[:, None])[None]
    chosen_values = jnp.dot(selector, accumulated, precision=lax.Precision.HIGHEST)
    all_values, all_picks = (
        lax.all_gather(chosen_values, "rep", axis=0, tiled=True),
        lax.all_gather(own_picks.astype(jnp.float32), "rep", axis=0, tiled=True),
    )
    spread = (all_picks[:, None] == positions.astype(jnp.float32)[None, :]).astype(jnp.float32)
    summed = lax.dot_general(
        spread, all_values, (((0,), (0,)), ((), ())), precision=lax.Precision.HIGHEST
    )
    delta = summed / replicas
    new_momentum = MOMENTUM_COEF * momentum + delta
    new_params = params - STEP_SCALE * (delta + MOMENTUM_COEF * new_momentum)
    gathered = lax.all_gather(new_params.astype(jnp.bfloat16), "fsdp", axis=0, tiled=True)
    return (new_params, new_momentum, new_error, gathered)


def solution(mesh):
    in_specs = (
        P("rep", "fsdp", None),
        P("rep", "fsdp", None),
        P("fsdp", None),
        P("fsdp", None),
        P("rep", "fsdp"),
    )
    out_specs = (P("fsdp", None), P("fsdp", None), P("rep", "fsdp", None), P())
    return jax.shard_map(
        per_device, mesh=mesh, in_specs=in_specs, out_specs=out_specs, check_vma=False
    )
```

profile of v0, /device:TPU:1, one launch (start us, length us, event | category | flops | bytes accessed | tf_op | source)
XLA Modules:
  0.0 204.7 jit_solution(5294625839869945955)
XLA Ops:
  7.2 0.0 all-gather.2.cloned.1.call-start
  7.2 1.5 fusion
  8.7 28.5 %all_gather.10 = f32[128,256]{1,0:T(8,128)S(1)} all-gather(f32[8,256]{1,0:T(8,128)S(1)} %fusion), channel_id=1, replica_groups=mesh['rep'=16,'fsdp'=32] {'rep'}, dimensions={0}, use_global_device_ids=true | all-gather | bytes 139264 | tf_op jit(solution)/shard_map/all_gather | solution.py:22
  37.2 1.3 dynamic-slice
  39.2 0.8 convert_dynamic-update-slice_fusion
  39.9 23.6 %all-reduce = f32[128]{0:T(128)S(1)} all-reduce(f32[128]{0:T(128)S(1)} %convert_dynamic-update-slice_fusion), channel_id=1, replica_groups=mesh['rep'=16,'fsdp'=32] {'rep'}, use_global_device_ids=true, to_apply=%add | all-reduce | flops 128 | bytes 1024
  63.6 2.8 %fusion.7 = (bf16[512,256]{1,0:T(8,128)(2,1)}, f32[512,256]{1,0:T(8,128)}, f32[512,256]{1,0:T(8,128)}) fusion(f32[512,256]{1,0:T(8,128)} %param.8, f32[512,256]{1,0:T(8,128)} %param.7, f32[128,256]{1,0:T(8,128)S(1)} %all_gather.10, f32[512]{0:T(512)S(1)} %iota_convert_fusion, f32[128]{0:T(128)S(1)} %all-reduce), kind=kOutput, calls=%fused_computation.17 | convolution fusion | flops 202440704 | bytes 2492928 | tf_op jit(solution)/shard_map/dot_general | solution.py:26
  66.3 0.0 all-gather.2.cloned.1.call-update
  66.4 0.7 convert_reduce_fusion
  67.1 2.1 %broadcast_multiply_fusion = f32[1,512,256]{2,1,0:T(8,128)} fusion(f32[512]{0:T(512)S(1)} %broadcast_subtract_fusion, f32[1,512,256]{2,1,0:T(8,128)} %param.5, f32[1,512,256]{2,1,0:T(8,128)} %param.6), kind=kLoop, calls=%fused_computation.6 | loop fusion | flops 393216 | bytes 1574912 | tf_op jit(solution)/shard_map/mul | solution.py:19
  69.2 121.5 %all-gather.2.cloned.1.call-done = bf16[16384,256]{1,0:T(8,128)(2,1)} async-done(((bf16[512,256]{1,0:T(8,128)(2,1)}), bf16[16384,256]{1,0:T(8,128)(2,1)}) %all-gather.2.cloned.1.call-update) | async-done | bytes 8388624 | tf_op jit(solution)/shard_map/all_gather | solution.py:32
  190.7 7.1 %copy.11 = bf16[16384,256]{1,0:T(8,128)(2,1)} copy(bf16[16384,256]{1,0:T(8,128)(2,1)} %all-gather.2.cloned.1.call-done) | data formatting | bytes 16777216
  (3 shorter events, 0.0 us)
Async XLA Ops:
  7.2 183.5 %all-gather.2.cloned.1.call-start = ((), (), s32[]{:S(2)}) async-start(), calls=%async_computation | async-start | bytes 8650752 | tf_op jit(solution)/shard_map/all_gather | solution.py:32
Sparse Core Ops, SparseCore 0:
  66.5 124.1 all-gather.1
where the time goes:
time: 205 us
  waiting for transfers between devices  121 us (59%)
  blocking collectives  52.1 us (25%)
  between operations  14.7 us (7%)
  local copies, waits for them, and re-layouts  8.37 us (4%)
  matrix products  4.29 us (2%)
  other arithmetic  3.63 us (2%)
    all_gather x1, waiting for transfers between devices, per_device(): lax.all_gather(new_params.astype(jnp.bfloat16), 'fsdp', axis=0, tiled=True)  121 us
    all_gather x1, blocking collectives, per_device(): lax.all_gather(chosen_values, 'rep', axis=0, tiled=True)  28.5 us
    unnamed x1, blocking collectives  23.6 us
    unnamed x3, local copies, waits for them, and re-layouts  8.37 us
  transfers between devices with their start and end apart: 1, of which 1 were waited for; matrix products, arithmetic and copies ran while one was open for 1% of the time, Pallas kernels for 0%

commit v1 on v0

v1 whole, which is shorter than its diff:
```python
import jax
import jax.numpy as jnp
from jax import lax
from jax.sharding import PartitionSpec as P

DECAY_RATE = 0.95
MOMENTUM_COEF = 0.9
STEP_SCALE = 0.7
LANES = 128


def per_device(pseudo_grad, error_buf, momentum, params, picks):
    shard_blocks, block = params.shape
    replicas = lax.axis_size("rep")
    own_picks = picks[0].astype(jnp.float32)
    topk = own_picks.shape[0]
    positions = lax.iota(jnp.float32, shard_blocks)
    accumulated = DECAY_RATE * error_buf[0] + pseudo_grad[0]
    selector = (own_picks[:, None] == positions[None, :]).astype(jnp.float32)
    chosen_values = jnp.dot(selector, accumulated, precision=lax.Precision.HIGHEST)
    payload = jnp.concatenate(
        [chosen_values, jnp.broadcast_to(own_picks[:, None], (topk, LANES))], axis=1
    )
    everyone = lax.all_to_all(
        jnp.broadcast_to(payload[None], (replicas, topk, block + LANES)), "rep", 0, 0
    ).reshape(replicas * topk, block + LANES)
    all_values, all_picks = everyone[:, :block], everyone[:, block]
    spread = (all_picks[:, None] == positions[None, :]).astype(jnp.float32)
    summed = lax.dot_general(
        spread, all_values, (((0,), (0,)), ((), ())), precision=lax.Precision.HIGHEST
    )
    delta = summed / replicas
    new_momentum = MOMENTUM_COEF * momentum + delta
    new_params = params - STEP_SCALE * (delta + MOMENTUM_COEF * new_momentum)
    gathered = lax.all_gather(new_params.astype(jnp.bfloat16), "fsdp", axis=0, tiled=True)
    chosen_mask = jnp.sum(selector, axis=0)
    new_error = (accumulated * (1.0 - chosen_mask)[:, None])[None]
    return (new_params, new_momentum, new_error, gathered)


def solution(mesh):
    in_specs = (
        P("rep", "fsdp", None),
        P("rep", "fsdp", None),
        P("fsdp", None),
        P("fsdp", None),
        P("rep", "fsdp"),
    )
    out_specs = (P("fsdp", None), P("fsdp", None), P("rep", "fsdp", None), P())
    return jax.shard_map(
        per_device, mesh=mesh, in_specs=in_specs, out_specs=out_specs, check_vma=False
    )
```

time: 205 us -> 154 us (0.75)
  blocking collectives: 52.1 us -> 17.7 us
  waiting for transfers between devices: 121 us -> 107 us
    all_gather x1 -> x0, blocking collectives: 28.5 us -> none  [per_device(): lax.all_gather(chosen_values, 'rep', axis=0, tiled=True)]
    unnamed x1 -> x0, blocking collectives: 23.6 us -> none
    all_to_all x0 -> x1, blocking collectives: none -> 17.7 us  [per_device(): lax.all_to_all(jnp.broadcast_to(payload[None], (replicas, topk, block + L...]
    all_gather x1, waiting for transfers between devices: 121 us -> 107 us  [per_device(): lax.all_gather(new_params.astype(jnp.bfloat16), 'fsdp', axis=0, tiled=True)]
    unnamed x3 -> x1, local copies, waits for them, and re-layouts: 8.37 us -> 7.1 us
where the time goes in v1:
time: 154 us
  waiting for transfers between devices  107 us (69%)
  blocking collectives  17.7 us (11%)
  between operations  14 us (9%)
  local copies, waits for them, and re-layouts  7.34 us (5%)
  matrix products  4.28 us (3%)
  other arithmetic  2.88 us (2%)
    all_gather x1, waiting for transfers between devices, per_device(): lax.all_gather(new_params.astype(jnp.bfloat16), 'fsdp', axis=0, tiled=True)  107 us
    all_to_all x1, blocking collectives, per_device(): lax.all_to_all(jnp.broadcast_to(payload[None], (replicas, topk, block + L...  17.7 us
    unnamed x1, local copies, waits for them, and re-layouts  7.1 us
  transfers between devices with their start and end apart: 1, of which 1 were waited for; matrix products, arithmetic and copies ran while one was open for 1% of the time, Pallas kernels for 0%

profile of v1, /device:TPU:1, one launch (start us, length us, event | category | flops | bytes accessed | tf_op | source)
XLA Modules:
  0.0 153.6 jit_solution(10624439896315279038)
XLA Ops:
  7.2 0.0 all-gather.2.cloned.1.call-start
  7.2 0.7 convert_bitcast_fusion
  7.9 1.5 fusion
  9.3 0.1 broadcast_in_dim.4
  9.4 0.1 broadcast_in_dim.5
  9.5 17.7 %all_to_all.5 = f32[16,8,384]{2,1,0:T(8,128)S(1)} all-to-all(f32[16,8,384]{2,1,0:T(8,128)S(1)} %broadcast_in_dim.5), channel_id=1, replica_groups=mesh['rep'=16,'fsdp'=32] {'rep'}, dimensions={0} | all-to-all | bytes 393216 | tf_op jit(solution)/shard_map/all_to_all | solution.py:24
  27.2 0.1 slice_reduce_fusion
  27.3 2.8 %fusion.6 = (bf16[512,256]{1,0:T(8,128)(2,1)}, f32[512,256]{1,0:T(8,128)}, f32[512,256]{1,0:T(8,128)}) fusion(f32[512,256]{1,0:T(8,128)} %param.8, f32[512,256]{1,0:T(8,128)} %param.7, f32[128,384]{1,0:T(8,128)S(1)} %bitcast.7, f32[128]{0:T(128)S(1)} %slice_reduce_fusion), kind=kOutput, calls=%fused_computation.18 | convolution fusion | flops 202440704 | bytes 2490880 | tf_op jit(solution)/shard_map/dot_general | solution.py:29
  30.1 0.0 all-gather.2.cloned.1.call-update
  30.2 0.1 convert_reduce_fusion
  30.3 2.1 %broadcast_multiply_fusion = f32[1,512,256]{2,1,0:T(8,128)} fusion(f32[512]{0:T(512)S(1)} %broadcast_subtract_fusion, f32[1,512,256]{2,1,0:T(8,128)} %param.5, f32[1,512,256]{2,1,0:T(8,128)} %param.6), kind=kLoop, calls=%fused_computation.6 | loop fusion | flops 393216 | bytes 1574912 | tf_op jit(solution)/shard_map/mul | solution.py:37
  32.4 107.3 %all-gather.2.cloned.1.call-done = bf16[16384,256]{1,0:T(8,128)(2,1)} async-done(((bf16[512,256]{1,0:T(8,128)(2,1)}), bf16[16384,256]{1,0:T(8,128)(2,1)}) %all-gather.2.cloned.1.call-update) | async-done | bytes 8388624 | tf_op jit(solution)/shard_map/all_gather | solution.py:35
  139.7 7.1 %copy.11 = bf16[16384,256]{1,0:T(8,128)(2,1)} copy(bf16[16384,256]{1,0:T(8,128)(2,1)} %all-gather.2.cloned.1.call-done) | data formatting | bytes 16777216
  (2 shorter events, 0.0 us)
Async XLA Ops:
  7.2 132.5 %all-gather.2.cloned.1.call-start = ((), (), s32[]{:S(2)}) async-start(), calls=%async_computation.1 | async-start | bytes 8650752 | tf_op jit(solution)/shard_map/all_gather | solution.py:35
Sparse Core Ops, SparseCore 0:
  30.3 109.3 all-gather.1

commit v2 on v1

v2 whole, which is shorter than its diff:
```python
import jax
import jax.numpy as jnp
from jax import lax
from jax.experimental import pallas as pl
from jax.experimental.pallas import tpu as pltpu
from jax.sharding import PartitionSpec as P

DECAY_RATE = 0.95
MOMENTUM_COEF = 0.9
STEP_SCALE = 0.7
LANES = 128
AXES = ("rep", "fsdp")
NX, NY, NZ, CORES = 4, 8, 8, 2
CLASSES = 2 * NZ
COLOURS = 4
VMEM_LIMIT = 40 * 1024 * 1024


def device_at(x, y, z, core):
    x, y, z, core = x % NX, y % NY, z % NZ, core % CORES
    return (y * 2 + x % 2) * (2 * NZ * CORES) + (x // 2) * (NZ * CORES) + z * CORES + core


PLACES = [
    (x, y, z, core) for x in range(NX) for y in range(NY) for z in range(NZ) for core in range(CORES)
]


def fetch(value, dx=0, dy=0, dz=0, dcore=0):
    pairs = [
        (device_at(x + dx, y + dy, z + dz, core + dcore), device_at(x, y, z, core))
        for x, y, z, core in PLACES
    ]
    return lax.ppermute(value, AXES, pairs)


def exchange_groups():
    groups = []
    for x in range(NX // 2):
        for y in range(NY):
            for core in range(CORES):
                pair = sorted((x, NX - 1 - x), key=lambda v: v // 2)
                groups.append([device_at(v, y, z, core) for v in pair for z in range(NZ)])
    return groups


def place_of_self():
    rep, shard = lax.axis_index("rep"), lax.axis_index("fsdp")
    x = (shard // (NZ * CORES)) * 2 + rep % 2
    return x, rep // 2, (shard // CORES) % NZ, shard % CORES


def colour_of(x, y, z):
    return (x + y + 2 * z) % COLOURS


def update_kernel(everyone, momentum, params, new_params, new_momentum, send, shard):
    blocks, block = params.shape
    entries = everyone.shape[0]
    values = everyone[:, :block]
    picks = everyone[:, block:]
    lane = lax.broadcasted_iota(jnp.int32, (entries, LANES), 1).astype(jnp.float32)
    spread = jnp.concatenate(
        [(picks == lane + float(at)).astype(jnp.bfloat16) for at in range(0, blocks, LANES)], axis=1
    )
    delta = jnp.zeros((blocks, block), jnp.float32)
    rest = values
    for _ in range(3):
        part = rest.astype(jnp.bfloat16)
        rest = rest - part.astype(jnp.float32)
        delta += lax.dot_general(
            spread, part, (((0,), (0,)), ((), ())), preferred_element_type=jnp.float32
        )
    delta = delta / 16.0
    momentum_now = MOMENTUM_COEF * momentum[...] + delta
    params_now = params[...] - STEP_SCALE * (delta + MOMENTUM_COEF * momentum_now)
    new_momentum[...] = momentum_now
    new_params[...] = params_now
    shard[...] = params_now.astype(jnp.bfloat16)
    x, y, z, core = place_of_self()
    rows = blocks // COLOURS
    for x_hi in range(2):
        x_there = lax.select(x // 2 == x_hi, x, NX - 1 - x)
        for z_there in range(NZ):
            start = pl.multiple_of(colour_of(x_there, y, z_there) * rows, rows)
            send[x_hi * NZ + z_there] = shard[pl.ds(start, rows), :]


def update(everyone, momentum, params):
    blocks, block = params.shape
    vmem = pl.BlockSpec(memory_space=pltpu.VMEM)
    return pl.pallas_call(
        update_kernel,
        out_shape=(
            jax.ShapeDtypeStruct((blocks, block), jnp.float32),
            jax.ShapeDtypeStruct((blocks, block), jnp.float32),
            jax.ShapeDtypeStruct((CLASSES, blocks // COLOURS, block), jnp.bfloat16),
        ),
        in_specs=[vmem] * 3,
        out_specs=(vmem,) * 3,
        scratch_shapes=[pltpu.VMEM((blocks, block), jnp.bfloat16)],
        compiler_params=pltpu.CompilerParams(vmem_limit_bytes=VMEM_LIMIT),
        cost_estimate=pl.CostEstimate(flops=10**8, bytes_accessed=4 * 10**6, transcendentals=0),
    )(everyone, momentum, params)


def put(whole, pieces, shape, dtype):
    arrays = []
    for piece in pieces:
        if not any(piece[0] is a for a in arrays):
            arrays.append(piece[0])
    slots = [next(i for i, a in enumerate(arrays) if a is piece[0]) for piece in pieces]
    given = [] if whole is None else [whole]

    def kernel(*refs):
        sources = refs[len(given) : len(given) + len(arrays)]
        out, sems = refs[-2:]
        x, y, z, core = place_of_self()
        copies = []
        for at, (piece, slot) in enumerate(zip(pieces, slots)):
            _, first, count, cls, other, offset = piece
            copies.append(
                pltpu.make_async_copy(
                    sources[slot].at[pl.ds(first, count)],
                    out.at[
                        pl.ds(cls, count),
                        1 - core if other else core,
                        (colour_of(x, y, z) + offset) % COLOURS,
                    ],
                    sems.at[at],
                )
            )
        for copy in copies:
            copy.start()
        for copy in copies:
            copy.wait()

    moved = sum(a.size for a in arrays) * 4
    return pl.pallas_call(
        kernel,
        out_shape=jax.ShapeDtypeStruct(shape, dtype),
        in_specs=[pl.BlockSpec(memory_space=pl.ANY)] * (len(given) + len(arrays)),
        out_specs=pl.BlockSpec(memory_space=pl.ANY),
        scratch_shapes=[pltpu.SemaphoreType.DMA((len(pieces),))],
        input_output_aliases={0: 0} if given else {},
        cost_estimate=pl.CostEstimate(flops=0, bytes_accessed=moved, transcendentals=0),
    )(*given, *arrays)


def gather_slab(send, rows, block):
    shape = (CLASSES, CORES, COLOURS, rows, block)
    half = CLASSES // 2
    own = lax.all_to_all(send, AXES, 0, 0, axis_index_groups=exchange_groups())
    low, high = own[:half], own[half:]
    first = [
        (fetch(low, dx=1), 0, 1),
        (fetch(high, dy=1), half, 1),
        (fetch(low, dx=-1), 0, -1),
    ]
    second = [
        (fetch(high, dy=-1), half, -1),
        (fetch(low, dz=1), 0, 2),
        (fetch(high, dz=-1), half, 2),
    ]
    own_there = fetch(own, dcore=1)
    whole = put(
        None,
        [(own, 0, CLASSES, 0, False, 0), (own_there, 0, CLASSES, 0, True, 0)],
        shape,
        send.dtype,
    )
    for batch in (first, second):
        joined = jnp.concatenate([piece for piece, _, _ in batch], axis=0)
        there = fetch(joined, dcore=1)
        pieces = [(joined, at * half, half, cls, False, off) for at, (_, cls, off) in enumerate(batch)]
        whole = put(whole, pieces, shape, send.dtype)
        pieces = [(there, at * half, half, cls, True, off) for at, (_, cls, off) in enumerate(batch)]
        whole = put(whole, pieces, shape, send.dtype)
    return whole


def per_device(pseudo_grad, error_buf, momentum, params, picks):
    blocks, block = params.shape
    replicas = lax.axis_size("rep")
    own_picks = picks[0].astype(jnp.float32)
    topk = own_picks.shape[0]
    positions = lax.iota(jnp.float32, blocks)
    accumulated = DECAY_RATE * error_buf[0] + pseudo_grad[0]
    selector = (own_picks[:, None] == positions[None, :]).astype(jnp.float32)
    chosen_values = jnp.dot(selector, accumulated, precision=lax.Precision.HIGHEST)
    payload = jnp.concatenate(
        [chosen_values, jnp.broadcast_to(own_picks[:, None], (topk, LANES))], axis=1
    )
    everyone = lax.all_to_all(
        jnp.broadcast_to(payload[None], (replicas, topk, block + LANES)), "rep", 0, 0
    ).reshape(replicas * topk, block + LANES)
    new_params, new_momentum, send = update(everyone, momentum, params)
    gathered = gather_slab(send, blocks // COLOURS, block)
    chosen_mask = jnp.sum(selector, axis=0)
    new_error = (accumulated * (1.0 - chosen_mask)[:, None])[None]
    return (new_params, new_momentum, new_error, gathered.reshape(-1, block))


def solution(mesh):
    in_specs = (
        P("rep", "fsdp", None),
        P("rep", "fsdp", None),
        P("fsdp", None),
        P("fsdp", None),
        P("rep", "fsdp"),
    )
    out_specs = (P("fsdp", None), P("fsdp", None), P("rep", "fsdp", None), P())
    return jax.shard_map(
        per_device, mesh=mesh, in_specs=in_specs, out_specs=out_specs, check_vma=False
    )
```

time: 154 us -> 358 us (2.32)
  Pallas kernels: 0 us -> 261 us
  waiting for transfers between devices: 107 us -> 1.75 us
  blocking collectives: 17.7 us -> 53.5 us
  starting transfers between devices: 0.04 us -> 34 us
  between operations: 14 us -> 0.88 us
  local copies, waits for them, and re-layouts: 7.34 us -> 2.91 us
    pallas_call x0 -> x6, Pallas kernels: none -> 261 us  [the longest x5 260 us: put(): pl.pallas_call(kernel, out_shape=jax.ShapeDtypeStruct(shape, dtype), in_s...]
    all_gather x1 -> x0, waiting for transfers between devices: 107 us -> none  [per_device(): lax.all_gather(new_params.astype(jnp.bfloat16), 'fsdp', axis=0, tiled=True)]
    all_to_all x0 -> x1, blocking collectives: none -> 35.7 us  [gather_slab(): own = lax.all_to_all(send, AXES, 0, 0, axis_index_groups=exchange_groups())]
    ppermute x0 -> x9, starting transfers between devices: none -> 34 us  [fetch(): return lax.ppermute(value, AXES, pairs)]
    unnamed x1 -> x16, local copies, waits for them, and re-layouts: 7.1 us -> 1.8 us
  transfers between devices with their start and end apart: 1 -> 9, of which waited for: 1 -> 1; matrix products, arithmetic and copies ran while one was open for 1% -> 1% of each run, Pallas kernels for 0% -> 59%
where the time goes in v2:
time: 358 us
  Pallas kernels  261 us (73%)
  blocking collectives  53.5 us (15%)
  starting transfers between devices  34 us (9%)
    pallas_call x5, Pallas kernels, put(): pl.pallas_call(kernel, out_shape=jax.ShapeDtypeStruct(shape, dtype), in_s...  260 us
    all_to_all x1, blocking collectives, gather_slab(): own = lax.all_to_all(send, AXES, 0, 0, axis_index_groups=exchange_groups())  35.7 us
    ppermute x9, starting transfers between devices, fetch(): return lax.ppermute(value, AXES, pairs)  34 us
    all_to_all x1, blocking collectives, per_device(): lax.all_to_all(jnp.broadcast_to(payload[None], (replicas, topk, block + L...  17.7 us
  transfers between devices with their start and end apart: 9, of which 1 were waited for; matrix products, arithmetic and copies ran while one was open for 1% of the time, Pallas kernels for 59%

profile of v2, /device:TPU:1, one launch (start us, length us, event | category | flops | bytes accessed | tf_op | source)
XLA Modules:
  0.0 357.6 jit_solution(3922607579674790294)
XLA Ops:
  0.6 0.0 copy-start
  0.6 0.0 copy-start.1
  0.7 0.7 convert_bitcast_fusion
  1.4 1.5 fusion
  2.9 0.1 broadcast_in_dim.4
  2.9 0.1 broadcast_in_dim.5
  3.0 17.7 %all_to_all.10 = f32[16,8,384]{2,1,0:T(8,128)S(1)} all-to-all(f32[16,8,384]{2,1,0:T(8,128)S(1)} %broadcast_in_dim.5), channel_id=1, replica_groups=mesh['rep'=16,'fsdp'=32] {'rep'}, dimensions={0} | all-to-all | bytes 393216 | tf_op jit(solution)/shard_map/all_to_all | solution.py:194
  20.8 0.0 copy-done
  20.8 0.0 copy-done.1
  20.8 1.5 shard_map.84
  22.2 35.7 %all_to_all.11.refs_0_ = bf16[16,128,256]{2,1,0:T(8,128)(2,1)S(1)} all-to-all(bf16[16,128,256]{2,1,0:T(8,128)(2,1)S(1)} %get-tuple-element.9), channel_id=1, replica_groups={{0,2,4,6,8,10,12,14,48,50,52,54,56,58,60,62},{1,3,5,7,9,11,13,15,49,51,..., dimensions={0} | all-to-all | bytes 2097152 | tf_op jit(solution)/shard_map/all_to_all | solution.py:153
  58.0 0.0 copy-start.2
  58.0 0.1 fusion.4
  58.1 2.0 collective-permute-start.1
  60.0 2.3 collective-permute-start.2
  62.4 3.2 collective-permute-start.3
  65.6 3.0 collective-permute-start.5
  68.7 2.8 collective-permute-start.6
  71.5 0.0 collective-permute-done.1
  71.5 2.6 collective-permute-start.7
  74.1 0.8 constant_dynamic-update-slice_fusion.2
  75.0 0.0 collective-permute-done.2
  75.0 0.9 constant_dynamic-update-slice_fusion.1
  75.8 0.0 collective-permute-done.3
  75.8 0.8 constant_dynamic-update-slice_fusion.refs_1_
  76.7 0.0 copy-start.4
  76.7 0.0 copy-start.5
  76.7 8.5 %collective-permute-start.4 = (bf16[24,128,256]{2,1,0:T(8,128)(2,1)}, bf16[24,128,256]{2,1,0:T(8,128)(2,1)}, u32[]{:S(2)}, u32[]{:S(2)}) collective-permute-start(bf16[24,128,256]{2,1,0:T(8,128)(2,1)} %constant_dynamic-update-slice_fusion.refs_1_), channel_id=1, source_target_pairs={{1,0},{0,1},{3,2},{2,3},{5,4},{4,5},{7,6},{6,7},{9,8},{8,9},{11,10... | collective-permute-start | bytes 4718600 | tf_op jit(solution)/shard_map/ppermute | solution.py:34
  85.2 0.0 collective-permute-done.5
  85.3 0.0 collective-permute-done.6
  85.4 0.0 collective-permute-done.7
  85.4 0.0 copy-start.3
  85.4 7.5 %collective-permute-start.8 = (bf16[24,128,256]{2,1,0:T(8,128)(2,1)S(1)}, bf16[24,128,256]{2,1,0:T(8,128)(2,1)}, u32[]{:S(2)}, u32[]{:S(2)}) collective-permute-start(bf16[24,128,256]{2,1,0:T(8,128)(2,1)S(1)} %constant_dynamic-update-slice_fusion.3.refs_1_), channel_id=1, source_target_pairs={{1,0},{0,1},{3,2},{2,3},{5,4},{4,5},{7,6},{6,7},{9,8},{8,9},{11,10... | collective-permute-start | bytes 4718600 | tf_op jit(solution)/shard_map/ppermute | solution.py:34
  93.0 0.0 copy-done.2
  93.0 1.9 collective-permute-start
  94.9 0.1 convert_reduce_fusion
  95.0 0.0 copy-done.4
  95.0 0.0 copy-done.5
  95.0 0.9 broadcast_multiply_fusion
  95.9 1.7 collective-permute-done.refs_1_
  97.7 64.6 %shard_map.85.refs_0_ = bf16[16,2,4,128,256]{4,3,2,1,0:T(8,128)(2,1)} custom-call(bf16[16,128,256]{2,1,0:T(8,128)(2,1)} %copy-done.2, bf16[16,128,256]{2,1,0:T(8,128)(2,1)} %collective-permute-done.refs_1_), custom_call_target="tpu_custom_call" | custom-call | bytes 4194304 | tf_op jit(solution)/shard_map/pallas_call | solution.py:139
  162.3 0.0 copy-done.3
  162.3 48.8 %shard_map.86.refs_0_ = bf16[16,2,4,128,256]{4,3,2,1,0:T(8,128)(2,1)} custom-call(bf16[16,2,4,128,256]{4,3,2,1,0:T(8,128)(2,1)} %shard_map.85.refs_0_, bf16[24,128,256]{2,1,0:T(8,128)(2,1)} %constant_dynamic-update-slice_fusion.refs_1_), custom_call_target="tpu_custom_call", output_to_operand_aliasing={{}: (0, {})} | custom-call | bytes 3145728 | tf_op jit(solution)/shard_map/pallas_call | solution.py:139
  211.1 0.0 collective-permute-done.4.refs_1_
  211.2 48.8 %shard_map.87.refs_0_ = bf16[16,2,4,128,256]{4,3,2,1,0:T(8,128)(2,1)} custom-call(bf16[16,2,4,128,256]{4,3,2,1,0:T(8,128)(2,1)} %shard_map.86.refs_0_, bf16[24,128,256]{2,1,0:T(8,128)(2,1)} %collective-permute-done.4.refs_1_), custom_call_target="tpu_custom_call", output_to_operand_aliasing={{}: (0, {})} | custom-call | bytes 3145728 | tf_op jit(solution)/shard_map/pallas_call | solution.py:139
  260.0 48.8 %shard_map.88.refs_0_ = bf16[16,2,4,128,256]{4,3,2,1,0:T(8,128)(2,1)} custom-call(bf16[16,2,4,128,256]{4,3,2,1,0:T(8,128)(2,1)} %shard_map.87.refs_0_, bf16[24,128,256]{2,1,0:T(8,128)(2,1)} %copy-done.3), custom_call_target="tpu_custom_call", output_to_operand_aliasing={{}: (0, {})} | custom-call | bytes 3145728 | tf_op jit(solution)/shard_map/pallas_call | solution.py:139
  308.8 0.0 collective-permute-done.8.refs_1_
  308.8 48.8 %shard_map.89 = bf16[16,2,4,128,256]{4,3,2,1,0:T(8,128)(2,1)} custom-call(bf16[16,2,4,128,256]{4,3,2,1,0:T(8,128)(2,1)} %shard_map.88.refs_0_, bf16[24,128,256]{2,1,0:T(8,128)(2,1)} %collective-permute-done.8.refs_1_), custom_call_target="tpu_custom_call", output_to_operand_aliasing={{}: (0, {})} | custom-call | bytes 3145728 | tf_op jit(solution)/shard_map/pallas_call | solution.py:139
  (5 shorter events, 0.1 us)
Async XLA Ops:
  0.6 20.1 %copy-start = (f32[512,256]{1,0:T(8,128)S(1)}, f32[512,256]{1,0:T(8,128)}, u32[]{:S(2)}) copy-start(f32[512,256]{1,0:T(8,128)} %momentum.1) | copy-start | bytes 1572868
  0.6 20.1 %copy-start.1 = (f32[512,256]{1,0:T(8,128)S(1)}, f32[512,256]{1,0:T(8,128)}, u32[]{:S(2)}) copy-start(f32[512,256]{1,0:T(8,128)} %params.1) | copy-start | bytes 1572868
  58.0 35.0 %copy-start.2 = (bf16[16,128,256]{2,1,0:T(8,128)(2,1)}, bf16[16,128,256]{2,1,0:T(8,128)(2,1)S(1)}, u32[]{:S(2)}) copy-start(bf16[16,128,256]{2,1,0:T(8,128)(2,1)S(1)} %all_to_all.11.refs_0_) | copy-start | bytes 3145732
  58.1 13.4 %collective-permute-start.1 = (bf16[8,128,256]{2,1,0:T(8,128)(2,1)S(1)}, bf16[8,128,256]{2,1,0:T(8,128)(2,1)S(1)}, u32[]{:S(2)}, u32[]{:S(2)}) collective-permute-start(bf16[8,128,256]{2,1,0:T(8,128)(2,1)S(1)} %get-tuple-element.11), channel_id=1, source_target_pairs={{32,0},{33,1},{34,2},{35,3},{36,4},{37,5},{38,6},{39,7},{40,8},{41... | collective-permute-start | bytes 1572872 | tf_op jit(solution)/shard_map/ppermute | solution.py:34
  60.0 14.9 %collective-permute-start.2 = (bf16[8,128,256]{2,1,0:T(8,128)(2,1)S(1)}, bf16[8,128,256]{2,1,0:T(8,128)(2,1)S(1)}, u32[]{:S(2)}, u32[]{:S(2)}) collective-permute-start(bf16[8,128,256]{2,1,0:T(8,128)(2,1)S(1)} %get-tuple-element.10), channel_id=1, source_target_pairs={{64,0},{65,1},{66,2},{67,3},{68,4},{69,5},{70,6},{71,7},{72,8},{73... | collective-permute-start | bytes 1572872 | tf_op jit(solution)/shard_map/ppermute | solution.py:34
  62.4 13.4 %collective-permute-start.3 = (bf16[8,128,256]{2,1,0:T(8,128)(2,1)S(1)}, bf16[8,128,256]{2,1,0:T(8,128)(2,1)S(1)}, u32[]{:S(2)}, u32[]{:S(2)}) collective-permute-start(bf16[8,128,256]{2,1,0:T(8,128)(2,1)S(1)} %get-tuple-element.11), channel_id=1, source_target_pairs={{48,0},{49,1},{50,2},{51,3},{52,4},{53,5},{54,6},{55,7},{56,8},{57... | collective-permute-start | bytes 1572872 | tf_op jit(solution)/shard_map/ppermute | solution.py:34
  65.6 19.6 %collective-permute-start.5 = (bf16[8,128,256]{2,1,0:T(8,128)(2,1)S(1)}, bf16[8,128,256]{2,1,0:T(8,128)(2,1)S(1)}, u32[]{:S(2)}, u32[]{:S(2)}) collective-permute-start(bf16[8,128,256]{2,1,0:T(8,128)(2,1)S(1)} %get-tuple-element.10), channel_id=1, source_target_pairs={{448,0},{449,1},{450,2},{451,3},{452,4},{453,5},{454,6},{455,7},{4... | collective-permute-start | bytes 1572872 | tf_op jit(solution)/shard_map/ppermute | solution.py:34
  68.7 16.6 %collective-permute-start.6 = (bf16[8,128,256]{2,1,0:T(8,128)(2,1)S(1)}, bf16[8,128,256]{2,1,0:T(8,128)(2,1)S(1)}, u32[]{:S(2)}, u32[]{:S(2)}) collective-permute-start(bf16[8,128,256]{2,1,0:T(8,128)(2,1)S(1)} %get-tuple-element.11), channel_id=1, source_target_pairs={{2,0},{3,1},{4,2},{5,3},{6,4},{7,5},{8,6},{9,7},{10,8},{11,9},{12,... | collective-permute-start | bytes 1572872 | tf_op jit(solution)/shard_map/ppermute | solution.py:34
  71.5 13.9 %collective-permute-start.7 = (bf16[8,128,256]{2,1,0:T(8,128)(2,1)S(1)}, bf16[8,128,256]{2,1,0:T(8,128)(2,1)S(1)}, u32[]{:S(2)}, u32[]{:S(2)}) collective-permute-start(bf16[8,128,256]{2,1,0:T(8,128)(2,1)S(1)} %get-tuple-element.10), channel_id=1, source_target_pairs={{14,0},{15,1},{0,2},{1,3},{2,4},{3,5},{4,6},{5,7},{6,8},{7,9},{8,1... | collective-permute-start | bytes 1572872 | tf_op jit(solution)/shard_map/ppermute | solution.py:34
  76.7 18.3 %copy-start.4 = (f32[1,512,256]{2,1,0:T(8,128)S(1)}, f32[1,512,256]{2,1,0:T(8,128)}, u32[]{:S(2)}) copy-start(f32[1,512,256]{2,1,0:T(8,128)} %param.5) | copy-start | bytes 1572868
  76.7 18.3 %copy-start.5 = (f32[1,512,256]{2,1,0:T(8,128)S(1)}, f32[1,512,256]{2,1,0:T(8,128)}, u32[]{:S(2)}) copy-start(f32[1,512,256]{2,1,0:T(8,128)} %param.6) | copy-start | bytes 1572868
  76.7 134.5 %collective-permute-start.4 = (bf16[24,128,256]{2,1,0:T(8,128)(2,1)}, bf16[24,128,256]{2,1,0:T(8,128)(2,1)}, u32[]{:S(2)}, u32[]{:S(2)}) collective-permute-start(bf16[24,128,256]{2,1,0:T(8,128)(2,1)} %constant_dynamic-update-slice_fusion.refs_1_), channel_id=1, source_target_pairs={{1,0},{0,1},{3,2},{2,3},{5,4},{4,5},{7,6},{6,7},{9,8},{8,9},{11,10... | collective-permute-start | bytes 4718600 | tf_op jit(solution)/shard_map/ppermute | solution.py:34
  85.4 76.9 %copy-start.3 = (bf16[24,128,256]{2,1,0:T(8,128)(2,1)}, bf16[24,128,256]{2,1,0:T(8,128)(2,1)S(1)}, u32[]{:S(2)}) copy-start(bf16[24,128,256]{2,1,0:T(8,128)(2,1)S(1)} %constant_dynamic-update-slice_fusion.3.refs_1_) | copy-start | bytes 4718596
  85.4 223.4 %collective-permute-start.8 = (bf16[24,128,256]{2,1,0:T(8,128)(2,1)S(1)}, bf16[24,128,256]{2,1,0:T(8,128)(2,1)}, u32[]{:S(2)}, u32[]{:S(2)}) collective-permute-start(bf16[24,128,256]{2,1,0:T(8,128)(2,1)S(1)} %constant_dynamic-update-slice_fusion.3.refs_1_), channel_id=1, source_target_pairs={{1,0},{0,1},{3,2},{2,3},{5,4},{4,5},{7,6},{6,7},{9,8},{8,9},{11,10... | collective-permute-start | bytes 4718600 | tf_op jit(solution)/shard_map/ppermute | solution.py:34
  93.0 4.7 %collective-permute-start = (bf16[16,128,256]{2,1,0:T(8,128)(2,1)S(1)}, bf16[16,128,256]{2,1,0:T(8,128)(2,1)}, u32[]{:S(2)}, u32[]{:S(2)}) collective-permute-start(bf16[16,128,256]{2,1,0:T(8,128)(2,1)S(1)} %all_to_all.11.refs_0_), channel_id=1, source_target_pairs={{1,0},{0,1},{3,2},{2,3},{5,4},{4,5},{7,6},{6,7},{9,8},{8,9},{11,10... | collective-permute-start | bytes 3145736 | tf_op jit(solution)/shard_map/ppermute | solution.py:34

commit v3 on v2

--- a/solution.py
+++ b/solution.py
@@ -117,65 +117,64 @@
         out, sems = refs[-2:]
         x, y, z, core = place_of_self()
         copies = []
-        for at, (piece, slot) in enumerate(zip(pieces, slots)):
+        for piece, slot in zip(pieces, slots):
             _, first, count, cls, other, offset = piece
-            copies.append(
-                pltpu.make_async_copy(
-                    sources[slot].at[pl.ds(first, count)],
-                    out.at[
-                        pl.ds(cls, count),
-                        1 - core if other else core,
-                        (colour_of(x, y, z) + offset) % COLOURS,
-                    ],
-                    sems.at[at],
+            there = 1 - core if other else core
+            colour = (colour_of(x, y, z) + offset) % COLOURS
+            for at in range(count):
+                copies.append(
+                    pltpu.make_async_copy(
+                        sources[slot].at[first + at],
+                        out.at[cls + at, there, colour],
+                        sems.at[len(copies)],
+                    )
                 )
-            )
         for copy in copies:
             copy.start()
         for copy in copies:
             copy.wait()
 
-    moved = sum(a.size for a in arrays) * 4
+    total = sum(piece[2] for piece in pieces)
+    moved = 4 * total * pieces[0][0][0].size
     return pl.pallas_call(
         kernel,
         out_shape=jax.ShapeDtypeStruct(shape, dtype),
         in_specs=[pl.BlockSpec(memory_space=pl.ANY)] * (len(given) + len(arrays)),
         out_specs=pl.BlockSpec(memory_space=pl.ANY),
-        scratch_shapes=[pltpu.SemaphoreType.DMA((len(pieces),))],
+        scratch_shapes=[pltpu.SemaphoreType.DMA((total,))],
         input_output_aliases={0: 0} if given else {},
         cost_estimate=pl.CostEstimate(flops=0, bytes_accessed=moved, transcendentals=0),
     )(*given, *arrays)
 
 
+PERMUTES = (
+    (dict(dx=1), 1, (0, 11)),
+    (dict(dy=-1), -1, (0, 10)),
+    (dict(dz=1), 2, (0, 9)),
+    (dict(dz=-1), 2, (9, 16)),
+    (dict(dx=-1), -1, (10, 16)),
+    (dict(dy=1), 1, (11, 16)),
+)
+BATCHES = ((0, 1), (2, 3), (4, 5))
+
+
 def gather_slab(send, rows, block):
     shape = (CLASSES, CORES, COLOURS, rows, block)
-    half = CLASSES // 2
     own = lax.all_to_all(send, AXES, 0, 0, axis_index_groups=exchange_groups())
-    low, high = own[:half], own[half:]
-    first = [
-        (fetch(low, dx=1), 0, 1),
-        (fetch(high, dy=1), half, 1),
-        (fetch(low, dx=-1), 0, -1),
-    ]
-    second = [
-        (fetch(high, dy=-1), half, -1),
-        (fetch(low, dz=1), 0, 2),
-        (fetch(high, dz=-1), half, 2),
-    ]
+    arrived = [fetch(own[lo:hi], **where) for where, _, (lo, hi) in PERMUTES]
     own_there = fetch(own, dcore=1)
-    whole = put(
-        None,
-        [(own, 0, CLASSES, 0, False, 0), (own_there, 0, CLASSES, 0, True, 0)],
-        shape,
-        send.dtype,
-    )
-    for batch in (first, second):
-        joined = jnp.concatenate([piece for piece, _, _ in batch], axis=0)
+    whole = put(None, [(own, 0, CLASSES, 0, False, 0)], shape, send.dtype)
+    whole = put(whole, [(own_there, 0, CLASSES, 0, True, 0)], shape, send.dtype)
+    for batch in BATCHES:
+        joined = jnp.concatenate([arrived[i] for i in batch], axis=0)
         there = fetch(joined, dcore=1)
-        pieces = [(joined, at * half, half, cls, False, off) for at, (_, cls, off) in enumerate(batch)]
-        whole = put(whole, pieces, shape, send.dtype)
-        pieces = [(there, at * half, half, cls, True, off) for at, (_, cls, off) in enumerate(batch)]
-        whole = put(whole, pieces, shape, send.dtype)
+        for array, other in ((joined, False), (there, True)):
+            pieces, first = [], 0
+            for i in batch:
+                _, offset, (lo, hi) = PERMUTES[i]
+                pieces.append((array, first, hi - lo, lo, other, offset))
+                first += hi - lo
+            whole = put(whole, pieces, shape, send.dtype)
     return whole
 
 

time: 358 us -> 369 us (1.031)
  waiting for transfers between devices: 1.75 us -> 7.58 us
  Pallas kernels: 261 us -> 266 us
    ppermute x9 -> x10, waiting for transfers between devices: 1.75 us -> 7.58 us  [fetch(): return lax.ppermute(value, AXES, pairs)]
    pallas_call x5 -> x8, Pallas kernels: 260 us -> 264 us  [put(): pl.pallas_call(kernel, out_shape=jax.ShapeDtypeStruct(shape, dtype), in_s...]
    ppermute x9 -> x10, starting transfers between devices: 34 us -> 32.7 us  [fetch(): return lax.ppermute(value, AXES, pairs)]
  transfers between devices with their start and end apart: 9 -> 10, of which waited for: 1 -> 3; matrix products, arithmetic and copies ran while one was open for 1% -> 1% of each run, Pallas kernels for 59% -> 66%
where the time goes in v3:
time: 369 us; the launch traced here: 368 us
  Pallas kernels  266 us (72%)
  blocking collectives  53.6 us (15%)
  starting transfers between devices  32.7 us (9%)
  waiting for transfers between devices  7.58 us (2%)
  local copies, waits for them, and re-layouts  4.17 us (1%)
    pallas_call x8, Pallas kernels, put(): pl.pallas_call(kernel, out_shape=jax.ShapeDtypeStruct(shape, dtype), in_s...  264 us
    all_to_all x1, blocking collectives, gather_slab(): own = lax.all_to_all(send, AXES, 0, 0, axis_index_groups=exchange_groups())  35.7 us
    ppermute x10, starting transfers between devices, fetch(): return lax.ppermute(value, AXES, pairs)  32.7 us
    all_to_all x1, blocking collectives, per_device(): lax.all_to_all(jnp.broadcast_to(payload[None], (replicas, topk, block + L...  17.9 us
    ppermute x10, waiting for transfers between devices, fetch(): return lax.ppermute(value, AXES, pairs)  7.58 us
  transfers between devices with their start and end apart: 10, of which 3 were waited for; matrix products, arithmetic and copies ran while one was open for 1% of the time, Pallas kernels for 66%

profile of v3, /device:TPU:1, one launch (start us, length us, event | category | flops | bytes accessed | tf_op | source)
XLA Modules:
  0.0 368.1 jit_solution(3632887028785418918)
XLA Ops:
  0.6 0.7 convert_bitcast_fusion
  1.3 0.0 copy-start.6
  1.3 1.5 fusion
  2.8 0.0 copy-start.5
  2.8 0.1 broadcast_in_dim.4
  3.0 17.9 %all_to_all.10 = f32[16,8,384]{2,1,0:T(8,128)S(1)} all-to-all(f32[16,8,384]{2,1,0:T(8,128)S(1)} %broadcast_in_dim.5), channel_id=1, replica_groups=mesh['rep'=16,'fsdp'=32] {'rep'}, dimensions={0} | all-to-all | bytes 393216 | tf_op jit(solution)/shard_map/all_to_all | solution.py:193
  20.9 0.0 copy-start
  20.9 1.0 copy-done
  21.9 0.0 copy-start.1
  21.9 1.0 copy-done.1
  22.9 1.5 shard_map.84
  24.4 35.7 %all_to_all.11.refs_0_ = bf16[16,128,256]{2,1,0:T(8,128)(2,1)S(1)} all-to-all(bf16[16,128,256]{2,1,0:T(8,128)(2,1)S(1)} %get-tuple-element.9), channel_id=1, replica_groups={{0,2,4,6,8,10,12,14,48,50,52,54,56,58,60,62},{1,3,5,7,9,11,13,15,49,51,..., dimensions={0} | all-to-all | bytes 2097152 | tf_op jit(solution)/shard_map/all_to_all | solution.py:163
  60.1 0.0 copy-start.2
  60.2 2.0 collective-permute-start.1
  62.2 2.8 collective-permute-start.2
  65.1 4.0 %collective-permute-start.4 = (bf16[9,128,256]{2,1,0:T(8,128)(2,1)S(1)}, bf16[9,128,256]{2,1,0:T(8,128)(2,1)S(1)}, u32[]{:S(2)}, u32[]{:S(2)}) collective-permute-start(bf16[9,128,256]{2,1,0:T(8,128)(2,1)S(1)} %slice.26), channel_id=1, source_target_pairs={{2,0},{3,1},{4,2},{5,3},{6,4},{7,5},{8,6},{9,7},{10,8},{11,9},{12,... | collective-permute-start | bytes 1769480 | tf_op jit(solution)/shard_map/ppermute | solution.py:34
  69.1 3.4 collective-permute-start.5
  72.5 2.7 collective-permute-done.1
  75.3 0.9 collective-permute-done.2
  76.2 0.0 copy-start.3
  76.3 8.2 %collective-permute-start.3 = (bf16[21,128,256]{2,1,0:T(8,128)(2,1)S(1)}, bf16[21,128,256]{2,1,0:T(8,128)(2,1)}, u32[]{:S(2)}, u32[]{:S(2)}) collective-permute-start(bf16[21,128,256]{2,1,0:T(8,128)(2,1)S(1)} %constant_dynamic-update-slice_fusion.refs_1_), channel_id=1, source_target_pairs={{1,0},{0,1},{3,2},{2,3},{5,4},{4,5},{7,6},{6,7},{9,8},{8,9},{11,10... | collective-permute-start | bytes 4128776 | tf_op jit(solution)/shard_map/ppermute | solution.py:34
  84.5 3.3 collective-permute-start.7
  87.8 2.0 collective-permute-start.8
  89.8 0.0 collective-permute-done.4
  89.8 2.5 collective-permute-start
  92.4 0.0 collective-permute-done.5
  92.4 0.0 copy-start.4
  92.4 1.9 collective-permute-start.6
  94.4 3.9 %collective-permute-done.7 = bf16[6,128,256]{2,1,0:T(8,128)(2,1)S(1)} collective-permute-done((bf16[6,128,256]{2,1,0:T(8,128)(2,1)S(1)}, bf16[6,128,256]{2,1,0:T(8,128)(2,1)S(1)}, u32[]{:S(2)}, u32[]{:S(2)}) %collective-permute-start.7) | collective-permute-done | bytes 393248 | tf_op jit(solution)/shard_map/ppermute | solution.py:34
  98.3 0.8 constant_dynamic-update-slice_fusion.5
  99.1 0.0 collective-permute-done.8
  99.1 0.8 constant_dynamic-update-slice_fusion.4.refs_1_
  99.9 2.7 collective-permute-start.9
  102.6 0.1 convert_reduce_fusion
  102.7 0.0 copy-done.6
  102.7 0.0 copy-done.5
  102.7 0.9 broadcast_multiply_fusion
  103.6 0.0 copy-done.2
  103.6 33.0 %shard_map.85.refs_0_ = bf16[16,2,4,128,256]{4,3,2,1,0:T(8,128)(2,1)} custom-call(bf16[16,128,256]{2,1,0:T(8,128)(2,1)} %copy-done.2), custom_call_target="tpu_custom_call" | custom-call | bytes 2097152 | tf_op jit(solution)/shard_map/pallas_call | solution.py:139
  136.6 0.0 collective-permute-done.refs_1_
  136.6 33.0 %shard_map.86.refs_0_ = bf16[16,2,4,128,256]{4,3,2,1,0:T(8,128)(2,1)} custom-call(bf16[16,2,4,128,256]{4,3,2,1,0:T(8,128)(2,1)} %shard_map.85.refs_0_, bf16[16,128,256]{2,1,0:T(8,128)(2,1)} %collective-permute-done.refs_1_), custom_call_target="tpu_custom_call", output_to_operand_aliasing={{}: (0, {})} | custom-call | bytes 2097152 | tf_op jit(solution)/shard_map/pallas_call | solution.py:139
  169.7 0.0 copy-done.3
  169.7 0.0 copy-done.4
  169.7 43.0 %shard_map.87.refs_0_ = bf16[16,2,4,128,256]{4,3,2,1,0:T(8,128)(2,1)} custom-call(bf16[16,2,4,128,256]{4,3,2,1,0:T(8,128)(2,1)} %shard_map.86.refs_0_, bf16[21,128,256]{2,1,0:T(8,128)(2,1)} %copy-done.3), custom_call_target="tpu_custom_call", output_to_operand_aliasing={{}: (0, {})} | custom-call | bytes 2752512 | tf_op jit(solution)/shard_map/pallas_call | solution.py:139
  212.7 0.0 collective-permute-done.3.refs_1_
  212.8 43.0 %shard_map.88.refs_0_ = bf16[16,2,4,128,256]{4,3,2,1,0:T(8,128)(2,1)} custom-call(bf16[16,2,4,128,256]{4,3,2,1,0:T(8,128)(2,1)} %shard_map.87.refs_0_, bf16[21,128,256]{2,1,0:T(8,128)(2,1)} %collective-permute-done.3.refs_1_), custom_call_target="tpu_custom_call", output_to_operand_aliasing={{}: (0, {})} | custom-call | bytes 2752512 | tf_op jit(solution)/shard_map/pallas_call | solution.py:139
  255.8 33.0 %shard_map.89.refs_0_ = bf16[16,2,4,128,256]{4,3,2,1,0:T(8,128)(2,1)} custom-call(bf16[16,2,4,128,256]{4,3,2,1,0:T(8,128)(2,1)} %shard_map.88.refs_0_, bf16[16,128,256]{2,1,0:T(8,128)(2,1)} %copy-done.4), custom_call_target="tpu_custom_call", output_to_operand_aliasing={{}: (0, {})} | custom-call | bytes 2097152 | tf_op jit(solution)/shard_map/pallas_call | solution.py:139
  288.8 0.0 collective-permute-done.6.refs_1_
  288.9 33.0 %shard_map.90.refs_0_ = bf16[16,2,4,128,256]{4,3,2,1,0:T(8,128)(2,1)} custom-call(bf16[16,2,4,128,256]{4,3,2,1,0:T(8,128)(2,1)} %shard_map.89.refs_0_, bf16[16,128,256]{2,1,0:T(8,128)(2,1)} %collective-permute-done.6.refs_1_), custom_call_target="tpu_custom_call", output_to_operand_aliasing={{}: (0, {})} | custom-call | bytes 2097152 | tf_op jit(solution)/shard_map/pallas_call | solution.py:139
  321.9 23.1 %shard_map.91.refs_0_ = bf16[16,2,4,128,256]{4,3,2,1,0:T(8,128)(2,1)} custom-call(bf16[16,2,4,128,256]{4,3,2,1,0:T(8,128)(2,1)} %shard_map.90.refs_0_, bf16[11,128,256]{2,1,0:T(8,128)(2,1)} %constant_dynamic-update-slice_fusion.4.refs_1_), custom_call_target="tpu_custom_call", output_to_operand_aliasing={{}: (0, {})} | custom-call | bytes 1441792 | tf_op jit(solution)/shard_map/pallas_call | solution.py:139
  345.0 0.0 collective-permute-done.9.refs_1_
  345.0 23.1 %shard_map.92 = bf16[16,2,4,128,256]{4,3,2,1,0:T(8,128)(2,1)} custom-call(bf16[16,2,4,128,256]{4,3,2,1,0:T(8,128)(2,1)} %shard_map.91.refs_0_, bf16[11,128,256]{2,1,0:T(8,128)(2,1)} %collective-permute-done.9.refs_1_), custom_call_target="tpu_custom_call", output_to_operand_aliasing={{}: (0, {})} | custom-call | bytes 1441792 | tf_op jit(solution)/shard_map/pallas_call | solution.py:139
  (13 shorter events, 0.4 us)
Async XLA Ops:
  1.3 101.4 %copy-start.6 = (f32[1,512,256]{2,1,0:T(8,128)S(1)}, f32[1,512,256]{2,1,0:T(8,128)}, u32[]{:S(2)}) copy-start(f32[1,512,256]{2,1,0:T(8,128)} %param.6) | copy-start | bytes 1572868
  2.8 99.9 %copy-start.5 = (f32[1,512,256]{2,1,0:T(8,128)S(1)}, f32[1,512,256]{2,1,0:T(8,128)}, u32[]{:S(2)}) copy-start(f32[1,512,256]{2,1,0:T(8,128)} %param.5) | copy-start | bytes 1572868
  20.9 1.0 copy-start
  21.9 1.0 copy-start.1
  60.1 43.5 %copy-start.2 = (bf16[16,128,256]{2,1,0:T(8,128)(2,1)}, bf16[16,128,256]{2,1,0:T(8,128)(2,1)S(1)}, u32[]{:S(2)}) copy-start(bf16[16,128,256]{2,1,0:T(8,128)(2,1)S(1)} %all_to_all.11.refs_0_) | copy-start | bytes 3145732
  60.2 15.0 %collective-permute-start.1 = (bf16[11,128,256]{2,1,0:T(8,128)(2,1)S(1)}, bf16[11,128,256]{2,1,0:T(8,128)(2,1)S(1)}, u32[]{:S(2)}, u32[]{:S(2)}) collective-permute-start(bf16[11,128,256]{2,1,0:T(8,128)(2,1)S(1)} %slice.24), channel_id=1, source_target_pairs={{32,0},{33,1},{34,2},{35,3},{36,4},{37,5},{38,6},{39,7},{40,8},{41... | collective-permute-start | bytes 2162696 | tf_op jit(solution)/shard_map/ppermute | solution.py:34
  62.2 14.0 %collective-permute-start.2 = (bf16[10,128,256]{2,1,0:T(8,128)(2,1)S(1)}, bf16[10,128,256]{2,1,0:T(8,128)(2,1)S(1)}, u32[]{:S(2)}, u32[]{:S(2)}) collective-permute-start(bf16[10,128,256]{2,1,0:T(8,128)(2,1)S(1)} %slice.25), channel_id=1, source_target_pairs={{448,0},{449,1},{450,2},{451,3},{452,4},{453,5},{454,6},{455,7},{4... | collective-permute-start | bytes 1966088 | tf_op jit(solution)/shard_map/ppermute | solution.py:34
  65.1 24.8 %collective-permute-start.4 = (bf16[9,128,256]{2,1,0:T(8,128)(2,1)S(1)}, bf16[9,128,256]{2,1,0:T(8,128)(2,1)S(1)}, u32[]{:S(2)}, u32[]{:S(2)}) collective-permute-start(bf16[9,128,256]{2,1,0:T(8,128)(2,1)S(1)} %slice.26), channel_id=1, source_target_pairs={{2,0},{3,1},{4,2},{5,3},{6,4},{7,5},{8,6},{9,7},{10,8},{11,9},{12,... | collective-permute-start | bytes 1769480 | tf_op jit(solution)/shard_map/ppermute | solution.py:34
  69.1 23.3 %collective-permute-start.5 = (bf16[7,128,256]{2,1,0:T(8,128)(2,1)S(1)}, bf16[7,128,256]{2,1,0:T(8,128)(2,1)S(1)}, u32[]{:S(2)}, u32[]{:S(2)}) collective-permute-start(bf16[7,128,256]{2,1,0:T(8,128)(2,1)S(1)} %slice.27), channel_id=1, source_target_pairs={{14,0},{15,1},{0,2},{1,3},{2,4},{3,5},{4,6},{5,7},{6,8},{7,9},{8,1... | collective-permute-start | bytes 1376264 | tf_op jit(solution)/shard_map/ppermute | solution.py:34
  76.2 93.5 %copy-start.3 = (bf16[21,128,256]{2,1,0:T(8,128)(2,1)}, bf16[21,128,256]{2,1,0:T(8,128)(2,1)S(1)}, u32[]{:S(2)}) copy-start(bf16[21,128,256]{2,1,0:T(8,128)(2,1)S(1)} %constant_dynamic-update-slice_fusion.refs_1_) | copy-start | bytes 4128772
  76.3 136.5 %collective-permute-start.3 = (bf16[21,128,256]{2,1,0:T(8,128)(2,1)S(1)}, bf16[21,128,256]{2,1,0:T(8,128)(2,1)}, u32[]{:S(2)}, u32[]{:S(2)}) collective-permute-start(bf16[21,128,256]{2,1,0:T(8,128)(2,1)S(1)} %constant_dynamic-update-slice_fusion.refs_1_), channel_id=1, source_target_pairs={{1,0},{0,1},{3,2},{2,3},{5,4},{4,5},{7,6},{6,7},{9,8},{8,9},{11,10... | collective-permute-start | bytes 4128776 | tf_op jit(solution)/shard_map/ppermute | solution.py:34
  84.5 13.8 %collective-permute-start.7 = (bf16[6,128,256]{2,1,0:T(8,128)(2,1)S(1)}, bf16[6,128,256]{2,1,0:T(8,128)(2,1)S(1)}, u32[]{:S(2)}, u32[]{:S(2)}) collective-permute-start(bf16[6,128,256]{2,1,0:T(8,128)(2,1)S(1)} %slice.28), channel_id=1, source_target_pairs={{48,0},{49,1},{50,2},{51,3},{52,4},{53,5},{54,6},{55,7},{56,8},{57... | collective-permute-start | bytes 1179656 | tf_op jit(solution)/shard_map/ppermute | solution.py:34
  87.8 11.3 %collective-permute-start.8 = (bf16[5,128,256]{2,1,0:T(8,128)(2,1)S(1)}, bf16[5,128,256]{2,1,0:T(8,128)(2,1)S(1)}, u32[]{:S(2)}, u32[]{:S(2)}) collective-permute-start(bf16[5,128,256]{2,1,0:T(8,128)(2,1)S(1)} %slice.29), channel_id=1, source_target_pairs={{64,0},{65,1},{66,2},{67,3},{68,4},{69,5},{70,6},{71,7},{72,8},{73... | collective-permute-start | bytes 983048 | tf_op jit(solution)/shard_map/ppermute | solution.py:34
  89.8 46.8 %collective-permute-start = (bf16[16,128,256]{2,1,0:T(8,128)(2,1)S(1)}, bf16[16,128,256]{2,1,0:T(8,128)(2,1)}, u32[]{:S(2)}, u32[]{:S(2)}) collective-permute-start(bf16[16,128,256]{2,1,0:T(8,128)(2,1)S(1)} %all_to_all.11.refs_0_), channel_id=1, source_target_pairs={{1,0},{0,1},{3,2},{2,3},{5,4},{4,5},{7,6},{6,7},{9,8},{8,9},{11,10... | collective-permute-start | bytes 3145736 | tf_op jit(solution)/shard_map/ppermute | solution.py:34
  92.4 77.3 %copy-start.4 = (bf16[16,128,256]{2,1,0:T(8,128)(2,1)}, bf16[16,128,256]{2,1,0:T(8,128)(2,1)S(1)}, u32[]{:S(2)}) copy-start(bf16[16,128,256]{2,1,0:T(8,128)(2,1)S(1)} %constant_dynamic-update-slice_fusion.2.refs_1_) | copy-start | bytes 3145732
  92.4 196.4 %collective-permute-start.6 = (bf16[16,128,256]{2,1,0:T(8,128)(2,1)S(1)}, bf16[16,128,256]{2,1,0:T(8,128)(2,1)}, u32[]{:S(2)}, u32[]{:S(2)}) collective-permute-start(bf16[16,128,256]{2,1,0:T(8,128)(2,1)S(1)} %constant_dynamic-update-slice_fusion.2.refs_1_), channel_id=1, source_target_pairs={{1,0},{0,1},{3,2},{2,3},{5,4},{4,5},{7,6},{6,7},{9,8},{8,9},{11,10... | collective-permute-start | bytes 3145736 | tf_op jit(solution)/shard_map/ppermute | solution.py:34
  99.9 245.1 %collective-permute-start.9 = (bf16[11,128,256]{2,1,0:T(8,128)(2,1)}, bf16[11,128,256]{2,1,0:T(8,128)(2,1)}, u32[]{:S(2)}, u32[]{:S(2)}) collective-permute-start(bf16[11,128,256]{2,1,0:T(8,128)(2,1)} %constant_dynamic-update-slice_fusion.4.refs_1_), channel_id=1, source_target_pairs={{1,0},{0,1},{3,2},{2,3},{5,4},{4,5},{7,6},{6,7},{9,8},{8,9},{11,10... | collective-permute-start | bytes 2162696 | tf_op jit(solution)/shard_map/ppermute | solution.py:34

commit v4 on v3

--- a/solution.py
+++ b/solution.py
@@ -54,8 +54,16 @@
     return (x + y + 2 * z) % COLOURS
 
 
-def update_kernel(everyone, momentum, params, new_params, new_momentum, send, shard):
+def update_kernel(
+    everyone, momentum_hbm, params_hbm, new_params, new_momentum, send, momentum, params, shard, sems
+):
     blocks, block = params.shape
+    loads = [
+        pltpu.make_async_copy(momentum_hbm, momentum, sems.at[0]),
+        pltpu.make_async_copy(params_hbm, params, sems.at[1]),
+    ]
+    for load in loads:
+        load.start()
     entries = everyone.shape[0]
     values = everyone[:, :block]
     picks = everyone[:, block:]
@@ -72,6 +80,8 @@
             spread, part, (((0,), (0,)), ((), ())), preferred_element_type=jnp.float32
         )
     delta = delta / 16.0
+    for load in loads:
+        load.wait()
     momentum_now = MOMENTUM_COEF * momentum[...] + delta
     params_now = params[...] - STEP_SCALE * (delta + MOMENTUM_COEF * momentum_now)
     new_momentum[...] = momentum_now
@@ -89,6 +99,7 @@
 def update(everyone, momentum, params):
     blocks, block = params.shape
     vmem = pl.BlockSpec(memory_space=pltpu.VMEM)
+    hbm = pl.BlockSpec(memory_space=pltpu.HBM)
     return pl.pallas_call(
         update_kernel,
         out_shape=(
@@ -96,9 +107,14 @@
             jax.ShapeDtypeStruct((blocks, block), jnp.float32),
             jax.ShapeDtypeStruct((CLASSES, blocks // COLOURS, block), jnp.bfloat16),
         ),
-        in_specs=[vmem] * 3,
+        in_specs=[vmem, hbm, hbm],
         out_specs=(vmem,) * 3,
-        scratch_shapes=[pltpu.VMEM((blocks, block), jnp.bfloat16)],
+        scratch_shapes=[
+            pltpu.VMEM((blocks, block), jnp.float32),
+            pltpu.VMEM((blocks, block), jnp.float32),
+            pltpu.VMEM((blocks, block), jnp.bfloat16),
+            pltpu.SemaphoreType.DMA((2,)),
+        ],
         compiler_params=pltpu.CompilerParams(vmem_limit_bytes=VMEM_LIMIT),
         cost_estimate=pl.CostEstimate(flops=10**8, bytes_accessed=4 * 10**6, transcendentals=0),
     )(everyone, momentum, params)
@@ -139,39 +155,39 @@
     return pl.pallas_call(
         kernel,
         out_shape=jax.ShapeDtypeStruct(shape, dtype),
-        in_specs=[pl.BlockSpec(memory_space=pl.ANY)] * (len(given) + len(arrays)),
-        out_specs=pl.BlockSpec(memory_space=pl.ANY),
+        in_specs=[pl.BlockSpec(memory_space=pltpu.HBM)] * len(given)
+        + [pl.BlockSpec(memory_space=pltpu.VMEM)] * len(arrays),
+        out_specs=pl.BlockSpec(memory_space=pltpu.HBM),
         scratch_shapes=[pltpu.SemaphoreType.DMA((total,))],
         input_output_aliases={0: 0} if given else {},
+        compiler_params=pltpu.CompilerParams(vmem_limit_bytes=VMEM_LIMIT),
         cost_estimate=pl.CostEstimate(flops=0, bytes_accessed=moved, transcendentals=0),
     )(*given, *arrays)
 
 
 PERMUTES = (
-    (dict(dx=1), 1, (0, 11)),
-    (dict(dy=-1), -1, (0, 10)),
-    (dict(dz=1), 2, (0, 9)),
-    (dict(dz=-1), 2, (9, 16)),
-    (dict(dx=-1), -1, (10, 16)),
-    (dict(dy=1), 1, (11, 16)),
+    (dict(dz=1), 2, (0, 16)),
+    (dict(dx=1), 1, (0, 10)),
+    (dict(dx=-1), -1, (0, 10)),
+    (dict(dy=1), 1, (10, 16)),
+    (dict(dy=-1), -1, (10, 16)),
 )
-BATCHES = ((0, 1), (2, 3), (4, 5))
+BATCHES = ((1, 3), (2, 4), (0,))
 
 
 def gather_slab(send, rows, block):
     shape = (CLASSES, CORES, COLOURS, rows, block)
     own = lax.all_to_all(send, AXES, 0, 0, axis_index_groups=exchange_groups())
     arrived = [fetch(own[lo:hi], **where) for where, _, (lo, hi) in PERMUTES]
-    own_there = fetch(own, dcore=1)
-    whole = put(None, [(own, 0, CLASSES, 0, False, 0)], shape, send.dtype)
-    whole = put(whole, [(own_there, 0, CLASSES, 0, True, 0)], shape, send.dtype)
-    for batch in BATCHES:
-        joined = jnp.concatenate([arrived[i] for i in batch], axis=0)
+    whole = None
+    for at, batch in enumerate(BATCHES):
+        parts = [(own, 0, (0, CLASSES))] if at == 0 else []
+        parts += [(arrived[i], *PERMUTES[i][1:]) for i in batch]
+        joined = jnp.concatenate([part[0] for part in parts], axis=0) if len(parts) > 1 else parts[0][0]
         there = fetch(joined, dcore=1)
         for array, other in ((joined, False), (there, True)):
             pieces, first = [], 0
-            for i in batch:
-                _, offset, (lo, hi) = PERMUTES[i]
+            for _, offset, (lo, hi) in parts:
                 pieces.append((array, first, hi - lo, lo, other, offset))
                 first += hi - lo
             whole = put(whole, pieces, shape, send.dtype)

time: 369 us -> 120 us (0.33)
  Pallas kernels: 266 us -> 9.45 us
  waiting for transfers between devices: 7.58 us -> 25.5 us
  starting transfers between devices: 32.7 us -> 24.5 us
    pallas_call x8 -> x6, Pallas kernels: 264 us -> 7.69 us  [put(): pl.pallas_call(kernel, out_shape=jax.ShapeDtypeStruct(shape, dtype), in_s...]
    ppermute x10 -> x8, waiting for transfers between devices: 7.58 us -> 25.5 us  [fetch(): return lax.ppermute(value, AXES, pairs)]
    ppermute x10 -> x8, starting transfers between devices: 32.7 us -> 24.5 us  [fetch(): return lax.ppermute(value, AXES, pairs)]
  transfers between devices with their start and end apart: 10 -> 8, of which waited for: 3 -> 3; matrix products, arithmetic and copies ran while one was open for 1% -> 1% of each run, Pallas kernels for 66% -> 5%
where the time goes in v4:
time: 120 us
  blocking collectives  53.5 us (45%)
  waiting for transfers between devices  25.5 us (21%)
  starting transfers between devices  24.5 us (20%)
  Pallas kernels  9.45 us (8%)
  local copies, waits for them, and re-layouts  2.53 us (2%)
  other arithmetic  1.68 us (1%)
  matrix products  1.47 us (1%)
    all_to_all x1, blocking collectives, gather_slab(): own = lax.all_to_all(send, AXES, 0, 0, axis_index_groups=exchange_groups())  35.8 us
    ppermute x8, waiting for transfers between devices, fetch(): return lax.ppermute(value, AXES, pairs)  25.5 us
    ppermute x8, starting transfers between devices, fetch(): return lax.ppermute(value, AXES, pairs)  24.5 us
    all_to_all x1, blocking collectives, per_device(): lax.all_to_all(jnp.broadcast_to(payload[None], (replicas, topk, block + L...  17.7 us
    pallas_call x6, Pallas kernels, put(): pl.pallas_call(kernel, out_shape=jax.ShapeDtypeStruct(shape, dtype), in_s...  7.69 us
  transfers between devices with their start and end apart: 8, of which 3 were waited for; matrix products, arithmetic and copies ran while one was open for 1% of the time, Pallas kernels for 5%

profile of v4, /device:TPU:1, one launch (start us, length us, event | category | flops | bytes accessed | tf_op | source)
XLA Modules:
  0.0 119.5 jit_solution(9916940546744257526)
XLA Ops:
  0.6 0.7 convert_bitcast_fusion
  1.3 1.5 %fusion = f32[8,256]{1,0:T(8,128)S(1)} fusion(f32[1,512,256]{2,1,0:T(8,128)} %param.5, f32[1,512,256]{2,1,0:T(8,128)} %param.6, f32[8]{0:T(128)S(1)} %convert_bitcast_fusion), kind=kOutput, calls=%fused_computation | convolution fusion | flops 12849152 | bytes 1056800 | tf_op jit(solution)/shard_map/dot_general | solution.py:205
  2.8 0.1 broadcast_in_dim.4
  2.8 0.1 broadcast_in_dim.5
  2.9 17.7 %all_to_all.10 = f32[16,8,384]{2,1,0:T(8,128)S(1)} all-to-all(f32[16,8,384]{2,1,0:T(8,128)S(1)} %broadcast_in_dim.5), channel_id=1, replica_groups=mesh['rep'=16,'fsdp'=32] {'rep'}, dimensions={0} | all-to-all | bytes 393216 | tf_op jit(solution)/shard_map/all_to_all | solution.py:209
  20.7 0.0 copy-start
  20.7 1.0 copy-done
  21.7 0.0 copy-start.1
  21.7 1.0 copy-done.1
  22.7 1.8 %shard_map.84 = (f32[512,256]{1,0:T(8,128)}, f32[512,256]{1,0:T(8,128)}, bf16[16,128,256]{2,1,0:T(8,128)(2,1)S(1)}) custom-call(f32[128,384]{1,0:T(8,128)S(1)} %bitcast.7, f32[512,256]{1,0:T(8,128)S(1)} %copy-done, f32[512,256]{1,0:T(8,128)S(1)} %copy-done.1), custom_call_target="tpu_custom_call" | custom-call | flops 100000000 | bytes 4000000 | tf_op jit(solution)/shard_map/pallas_call | solution.py:103
  24.5 35.8 %all_to_all.11 = bf16[16,128,256]{2,1,0:T(8,128)(2,1)S(1)} all-to-all(bf16[16,128,256]{2,1,0:T(8,128)(2,1)S(1)} %get-tuple-element.9), channel_id=1, replica_groups={{0,2,4,6,8,10,12,14,48,50,52,54,56,58,60,62},{1,3,5,7,9,11,13,15,49,51,..., dimensions={0} | all-to-all | bytes 2097152 | tf_op jit(solution)/shard_map/all_to_all | solution.py:180
  60.3 2.0 %collective-permute-start = (bf16[10,128,256]{2,1,0:T(8,128)(2,1)S(1)}, bf16[10,128,256]{2,1,0:T(8,128)(2,1)S(1)}, u32[]{:S(2)}, u32[]{:S(2)}) collective-permute-start(bf16[10,128,256]{2,1,0:T(8,128)(2,1)S(1)} %slice.10), channel_id=1, source_target_pairs={{32,0},{33,1},{34,2},{35,3},{36,4},{37,5},{38,6},{39,7},{40,8},{41... | collective-permute-start | bytes 1966088 | tf_op jit(solution)/shard_map/ppermute | solution.py:34
  62.3 2.3 %collective-permute-start.1 = (bf16[6,128,256]{2,1,0:T(8,128)(2,1)S(1)}, bf16[6,128,256]{2,1,0:T(8,128)(2,1)S(1)}, u32[]{:S(2)}, u32[]{:S(2)}) collective-permute-start(bf16[6,128,256]{2,1,0:T(8,128)(2,1)S(1)} %slice.11), channel_id=1, source_target_pairs={{64,0},{65,1},{66,2},{67,3},{68,4},{69,5},{70,6},{71,7},{72,8},{73... | collective-permute-start | bytes 1179656 | tf_op jit(solution)/shard_map/ppermute | solution.py:34
  64.7 0.1 constant_dynamic-update-slice_fusion.2
  64.8 0.0 copy-start.2
  64.8 0.0 copy-start.3
  64.8 9.2 %collective-permute-done = bf16[10,128,256]{2,1,0:T(8,128)(2,1)S(1)} collective-permute-done((bf16[10,128,256]{2,1,0:T(8,128)(2,1)S(1)}, bf16[10,128,256]{2,1,0:T(8,128)(2,1)S(1)}, u32[]{:S(2)}, u32[]{:S(2)}) %collective-permute-start) | collective-permute-done | bytes 655392 | tf_op jit(solution)/shard_map/ppermute | solution.py:34
  74.0 0.0 collective-permute-done.1
  74.1 7.3 %collective-permute-start.2 = (bf16[32,128,256]{2,1,0:T(8,128)(2,1)S(1)}, bf16[32,128,256]{2,1,0:T(8,128)(2,1)S(1)}, u32[]{:S(2)}, u32[]{:S(2)}) collective-permute-start(bf16[32,128,256]{2,1,0:T(8,128)(2,1)S(1)} %constant_dynamic-update-slice_fusion.refs_0_), channel_id=1, source_target_pairs={{1,0},{0,1},{3,2},{2,3},{5,4},{4,5},{7,6},{6,7},{9,8},{8,9},{11,10... | collective-permute-start | bytes 6291464 | tf_op jit(solution)/shard_map/ppermute | solution.py:34
  81.4 2.5 %collective-permute-start.6 = (bf16[16,128,256]{2,1,0:T(8,128)(2,1)S(1)}, bf16[16,128,256]{2,1,0:T(8,128)(2,1)S(1)}, u32[]{:S(2)}, u32[]{:S(2)}) collective-permute-start(bf16[16,128,256]{2,1,0:T(8,128)(2,1)S(1)} %all_to_all.11), channel_id=1, source_target_pairs={{2,0},{3,1},{4,2},{5,3},{6,4},{7,5},{8,6},{9,7},{10,8},{11,9},{12,... | collective-permute-start | bytes 3145736 | tf_op jit(solution)/shard_map/ppermute | solution.py:34
  83.8 2.3 %collective-permute-start.3 = (bf16[10,128,256]{2,1,0:T(8,128)(2,1)S(1)}, bf16[10,128,256]{2,1,0:T(8,128)(2,1)S(1)}, u32[]{:S(2)}, u32[]{:S(2)}) collective-permute-start(bf16[10,128,256]{2,1,0:T(8,128)(2,1)S(1)} %slice.10), channel_id=1, source_target_pairs={{48,0},{49,1},{50,2},{51,3},{52,4},{53,5},{54,6},{55,7},{56,8},{57... | collective-permute-start | bytes 1966088 | tf_op jit(solution)/shard_map/ppermute | solution.py:34
  86.2 2.7 %collective-permute-start.4 = (bf16[6,128,256]{2,1,0:T(8,128)(2,1)S(1)}, bf16[6,128,256]{2,1,0:T(8,128)(2,1)S(1)}, u32[]{:S(2)}, u32[]{:S(2)}) collective-permute-start(bf16[6,128,256]{2,1,0:T(8,128)(2,1)S(1)} %slice.11), channel_id=1, source_target_pairs={{448,0},{449,1},{450,2},{451,3},{452,4},{453,5},{454,6},{455,7},{4... | collective-permute-start | bytes 1179656 | tf_op jit(solution)/shard_map/ppermute | solution.py:34
  88.9 14.7 %collective-permute-done.3 = bf16[10,128,256]{2,1,0:T(8,128)(2,1)S(1)} collective-permute-done((bf16[10,128,256]{2,1,0:T(8,128)(2,1)S(1)}, bf16[10,128,256]{2,1,0:T(8,128)(2,1)S(1)}, u32[]{:S(2)}, u32[]{:S(2)}) %collective-permute-start.3) | collective-permute-done | bytes 655392 | tf_op jit(solution)/shard_map/ppermute | solution.py:34
  103.7 0.0 collective-permute-done.4
  103.8 2.7 %collective-permute-start.5 = (bf16[16,128,256]{2,1,0:T(8,128)(2,1)S(1)}, bf16[16,128,256]{2,1,0:T(8,128)(2,1)S(1)}, u32[]{:S(2)}, u32[]{:S(2)}) collective-permute-start(bf16[16,128,256]{2,1,0:T(8,128)(2,1)S(1)} %constant_dynamic-update-slice_fusion.3.refs_1_), channel_id=1, source_target_pairs={{1,0},{0,1},{3,2},{2,3},{5,4},{4,5},{7,6},{6,7},{9,8},{8,9},{11,10... | collective-permute-start | bytes 3145736 | tf_op jit(solution)/shard_map/ppermute | solution.py:34
  106.5 1.6 %collective-permute-done.6.refs_1_ = bf16[16,128,256]{2,1,0:T(8,128)(2,1)S(1)} collective-permute-done((bf16[16,128,256]{2,1,0:T(8,128)(2,1)S(1)}, bf16[16,128,256]{2,1,0:T(8,128)(2,1)S(1)}, u32[]{:S(2)}, u32[]{:S(2)}) %collective-permute-start.6) | collective-permute-done | bytes 1048608 | tf_op jit(solution)/shard_map/ppermute | solution.py:34
  108.0 2.7 %collective-permute-start.7 = (bf16[16,128,256]{2,1,0:T(8,128)(2,1)S(1)}, bf16[16,128,256]{2,1,0:T(8,128)(2,1)S(1)}, u32[]{:S(2)}, u32[]{:S(2)}) collective-permute-start(bf16[16,128,256]{2,1,0:T(8,128)(2,1)S(1)} %collective-permute-done.6.refs_1_), channel_id=1, source_target_pairs={{1,0},{0,1},{3,2},{2,3},{5,4},{4,5},{7,6},{6,7},{9,8},{8,9},{11,10... | collective-permute-start | bytes 3145736 | tf_op jit(solution)/shard_map/ppermute | solution.py:34
  110.7 0.1 convert_reduce_fusion
  110.8 0.0 copy-done.2
  110.8 0.0 copy-done.3
  110.9 0.9 broadcast_multiply_fusion
  111.8 1.6 %shard_map.85.refs_0_ = bf16[16,2,4,128,256]{4,3,2,1,0:T(8,128)(2,1)} custom-call(bf16[32,128,256]{2,1,0:T(8,128)(2,1)S(1)} %constant_dynamic-update-slice_fusion.refs_0_), custom_call_target="tpu_custom_call" | custom-call | bytes 4194304 | tf_op jit(solution)/shard_map/pallas_call | solution.py:155
  113.4 0.0 collective-permute-done.2.refs_1_
  113.4 1.6 %shard_map.86.refs_0_ = bf16[16,2,4,128,256]{4,3,2,1,0:T(8,128)(2,1)} custom-call(bf16[16,2,4,128,256]{4,3,2,1,0:T(8,128)(2,1)} %shard_map.85.refs_0_, bf16[32,128,256]{2,1,0:T(8,128)(2,1)S(1)} %collective-permute-done.2.refs_1_), custom_call_target="tpu_custom_call", output_to_operand_aliasing={{}: (0, {})} | custom-call | bytes 4194304 | tf_op jit(solution)/shard_map/pallas_call | solution.py:155
  115.0 1.1 shard_map.87.refs_0_
  116.1 0.0 collective-permute-done.5.refs_1_
  116.1 1.1 shard_map.88.refs_0_
  117.3 1.1 shard_map.89.refs_0_
  118.4 0.0 collective-permute-done.7.refs_1_
  118.4 1.1 shard_map.90
  (8 shorter events, 0.2 us)
Async XLA Ops:
  20.7 1.0 copy-start
  21.7 1.0 copy-start.1
  60.3 13.6 %collective-permute-start = (bf16[10,128,256]{2,1,0:T(8,128)(2,1)S(1)}, bf16[10,128,256]{2,1,0:T(8,128)(2,1)S(1)}, u32[]{:S(2)}, u32[]{:S(2)}) collective-permute-start(bf16[10,128,256]{2,1,0:T(8,128)(2,1)S(1)} %slice.10), channel_id=1, source_target_pairs={{32,0},{33,1},{34,2},{35,3},{36,4},{37,5},{38,6},{39,7},{40,8},{41... | collective-permute-start | bytes 1966088 | tf_op jit(solution)/shard_map/ppermute | solution.py:34
  62.3 11.7 %collective-permute-start.1 = (bf16[6,128,256]{2,1,0:T(8,128)(2,1)S(1)}, bf16[6,128,256]{2,1,0:T(8,128)(2,1)S(1)}, u32[]{:S(2)}, u32[]{:S(2)}) collective-permute-start(bf16[6,128,256]{2,1,0:T(8,128)(2,1)S(1)} %slice.11), channel_id=1, source_target_pairs={{64,0},{65,1},{66,2},{67,3},{68,4},{69,5},{70,6},{71,7},{72,8},{73... | collective-permute-start | bytes 1179656 | tf_op jit(solution)/shard_map/ppermute | solution.py:34
  64.8 46.1 %copy-start.2 = (f32[1,512,256]{2,1,0:T(8,128)S(1)}, f32[1,512,256]{2,1,0:T(8,128)}, u32[]{:S(2)}) copy-start(f32[1,512,256]{2,1,0:T(8,128)} %param.5) | copy-start | bytes 1572868
  64.8 46.1 %copy-start.3 = (f32[1,512,256]{2,1,0:T(8,128)S(1)}, f32[1,512,256]{2,1,0:T(8,128)}, u32[]{:S(2)}) copy-start(f32[1,512,256]{2,1,0:T(8,128)} %param.6) | copy-start | bytes 1572868
  74.1 39.3 %collective-permute-start.2 = (bf16[32,128,256]{2,1,0:T(8,128)(2,1)S(1)}, bf16[32,128,256]{2,1,0:T(8,128)(2,1)S(1)}, u32[]{:S(2)}, u32[]{:S(2)}) collective-permute-start(bf16[32,128,256]{2,1,0:T(8,128)(2,1)S(1)} %constant_dynamic-update-slice_fusion.refs_0_), channel_id=1, source_target_pairs={{1,0},{0,1},{3,2},{2,3},{5,4},{4,5},{7,6},{6,7},{9,8},{8,9},{11,10... | collective-permute-start | bytes 6291464 | tf_op jit(solution)/shard_map/ppermute | solution.py:34
  81.4 26.7 %collective-permute-start.6 = (bf16[16,128,256]{2,1,0:T(8,128)(2,1)S(1)}, bf16[16,128,256]{2,1,0:T(8,128)(2,1)S(1)}, u32[]{:S(2)}, u32[]{:S(2)}) collective-permute-start(bf16[16,128,256]{2,1,0:T(8,128)(2,1)S(1)} %all_to_all.11), channel_id=1, source_target_pairs={{2,0},{3,1},{4,2},{5,3},{6,4},{7,5},{8,6},{9,7},{10,8},{11,9},{12,... | collective-permute-start | bytes 3145736 | tf_op jit(solution)/shard_map/ppermute | solution.py:34
  83.8 19.8 %collective-permute-start.3 = (bf16[10,128,256]{2,1,0:T(8,128)(2,1)S(1)}, bf16[10,128,256]{2,1,0:T(8,128)(2,1)S(1)}, u32[]{:S(2)}, u32[]{:S(2)}) collective-permute-start(bf16[10,128,256]{2,1,0:T(8,128)(2,1)S(1)} %slice.10), channel_id=1, source_target_pairs={{48,0},{49,1},{50,2},{51,3},{52,4},{53,5},{54,6},{55,7},{56,8},{57... | collective-permute-start | bytes 1966088 | tf_op jit(solution)/shard_map/ppermute | solution.py:34
  86.2 17.5 %collective-permute-start.4 = (bf16[6,128,256]{2,1,0:T(8,128)(2,1)S(1)}, bf16[6,128,256]{2,1,0:T(8,128)(2,1)S(1)}, u32[]{:S(2)}, u32[]{:S(2)}) collective-permute-start(bf16[6,128,256]{2,1,0:T(8,128)(2,1)S(1)} %slice.11), channel_id=1, source_target_pairs={{448,0},{449,1},{450,2},{451,3},{452,4},{453,5},{454,6},{455,7},{4... | collective-permute-start | bytes 1179656 | tf_op jit(solution)/shard_map/ppermute | solution.py:34
  103.8 12.4 %collective-permute-start.5 = (bf16[16,128,256]{2,1,0:T(8,128)(2,1)S(1)}, bf16[16,128,256]{2,1,0:T(8,128)(2,1)S(1)}, u32[]{:S(2)}, u32[]{:S(2)}) collective-permute-start(bf16[16,128,256]{2,1,0:T(8,128)(2,1)S(1)} %constant_dynamic-update-slice_fusion.3.refs_1_), channel_id=1, source_target_pairs={{1,0},{0,1},{3,2},{2,3},{5,4},{4,5},{7,6},{6,7},{9,8},{8,9},{11,10... | collective-permute-start | bytes 3145736 | tf_op jit(solution)/shard_map/ppermute | solution.py:34
  108.0 10.4 %collective-permute-start.7 = (bf16[16,128,256]{2,1,0:T(8,128)(2,1)S(1)}, bf16[16,128,256]{2,1,0:T(8,128)(2,1)S(1)}, u32[]{:S(2)}, u32[]{:S(2)}) collective-permute-start(bf16[16,128,256]{2,1,0:T(8,128)(2,1)S(1)} %collective-permute-done.6.refs_1_), channel_id=1, source_target_pairs={{1,0},{0,1},{3,2},{2,3},{5,4},{4,5},{7,6},{6,7},{9,8},{8,9},{11,10... | collective-permute-start | bytes 3145736 | tf_op jit(solution)/shard_map/ppermute | solution.py:34

commit v5 on v3

--- a/solution.py
+++ b/solution.py
@@ -52,6 +52,66 @@
 
 def colour_of(x, y, z):
     return (x + y + 2 * z) % COLOURS
+
+
+def choose_kernel(picks, error, grad, momentum, params, payload, momentum_near, params_near, rows, sems):
+    topk, block = payload.shape[1], error.shape[1]
+    loads = []
+    for at in range(topk):
+        first = pl.multiple_of((picks[at] // 8) * 8, 8)
+        for which, array in enumerate((error, grad)):
+            slot = 2 * at + which
+            loads.append(
+                pltpu.make_async_copy(array.at[pl.ds(first, 8)], rows.at[slot], sems.at[slot])
+            )
+    staged = [
+        pltpu.make_async_copy(momentum, momentum_near, sems.at[2 * topk]),
+        pltpu.make_async_copy(params, params_near, sems.at[2 * topk + 1]),
+    ]
+    for copy in loads + staged:
+        copy.start()
+    row_of = lax.broadcasted_iota(jnp.int32, (8, block), 0)
+    pick_row = lax.broadcasted_iota(jnp.int32, (topk, LANES), 0)
+    values = jnp.zeros((topk, block), jnp.float32)
+    names = jnp.zeros((topk, LANES), jnp.float32)
+    for copy in loads:
+        copy.wait()
+    for at in range(topk):
+        group = DECAY_RATE * rows[2 * at] + rows[2 * at + 1]
+        one = jnp.sum(jnp.where(row_of == picks[at] % 8, group, 0.0), axis=0, keepdims=True)
+        values = jnp.where(row_of == at, one, values)
+        names = jnp.where(pick_row == at, picks[at].astype(jnp.float32), names)
+    for replica in range(payload.shape[0]):
+        payload[replica, :, :block] = values
+        payload[replica, :, block:] = names
+    for copy in staged:
+        copy.wait()
+
+
+def choose(picks, error, grad, momentum, params, replicas):
+    blocks, block = params.shape
+    topk = picks.shape[0]
+    vmem = pl.BlockSpec(memory_space=pltpu.VMEM)
+    hbm = pl.BlockSpec(memory_space=pltpu.HBM)
+    error, grad, momentum, params = (
+        pltpu.with_memory_space_constraint(array, pltpu.HBM) for array in (error, grad, momentum, params)
+    )
+    return pl.pallas_call(
+        choose_kernel,
+        out_shape=(
+            jax.ShapeDtypeStruct((replicas, topk, block + LANES), jnp.float32),
+            jax.ShapeDtypeStruct((blocks, block), jnp.float32),
+            jax.ShapeDtypeStruct((blocks, block), jnp.float32),
+        ),
+        in_specs=[pl.BlockSpec(memory_space=pltpu.SMEM)] + [hbm] * 4,
+        out_specs=(vmem,) * 3,
+        scratch_shapes=[
+            pltpu.VMEM((2 * topk, 8, block), jnp.float32),
+            pltpu.SemaphoreType.DMA((2 * topk + 2,)),
+        ],
+        compiler_params=pltpu.CompilerParams(vmem_limit_bytes=VMEM_LIMIT),
+        cost_estimate=pl.CostEstimate(flops=10**5, bytes_accessed=2 * 10**6, transcendentals=0),
+    )(picks, error, grad, momentum, params)
 
 
 def update_kernel(everyone, momentum, params, new_params, new_momentum, send, shard):
@@ -139,23 +199,24 @@
     return pl.pallas_call(
         kernel,
         out_shape=jax.ShapeDtypeStruct(shape, dtype),
-        in_specs=[pl.BlockSpec(memory_space=pl.ANY)] * (len(given) + len(arrays)),
-        out_specs=pl.BlockSpec(memory_space=pl.ANY),
+        in_specs=[pl.BlockSpec(memory_space=pltpu.HBM)] * len(given)
+        + [pl.BlockSpec(memory_space=pltpu.VMEM)] * len(arrays),
+        out_specs=pl.BlockSpec(memory_space=pltpu.HBM),
         scratch_shapes=[pltpu.SemaphoreType.DMA((total,))],
         input_output_aliases={0: 0} if given else {},
+        compiler_params=pltpu.CompilerParams(vmem_limit_bytes=VMEM_LIMIT),
         cost_estimate=pl.CostEstimate(flops=0, bytes_accessed=moved, transcendentals=0),
     )(*given, *arrays)
 
 
 PERMUTES = (
-    (dict(dx=1), 1, (0, 11)),
-    (dict(dy=-1), -1, (0, 10)),
-    (dict(dz=1), 2, (0, 9)),
-    (dict(dz=-1), 2, (9, 16)),
-    (dict(dx=-1), -1, (10, 16)),
-    (dict(dy=1), 1, (11, 16)),
+    (dict(dz=1), 2, (0, 16)),
+    (dict(dx=1), 1, (0, 10)),
+    (dict(dx=-1), -1, (0, 10)),
+    (dict(dy=1), 1, (10, 16)),
+    (dict(dy=-1), -1, (10, 16)),
 )
-BATCHES = ((0, 1), (2, 3), (4, 5))
+BATCHES = ((1, 3, 2, 4), (0,))
 
 
 def gather_slab(send, rows, block):
@@ -165,38 +226,35 @@
     own_there = fetch(own, dcore=1)
     whole = put(None, [(own, 0, CLASSES, 0, False, 0)], shape, send.dtype)
     whole = put(whole, [(own_there, 0, CLASSES, 0, True, 0)], shape, send.dtype)
+    *arrived, whole = lax.optimization_barrier((*arrived, whole))
+    here, there = [], []
     for batch in BATCHES:
-        joined = jnp.concatenate([arrived[i] for i in batch], axis=0)
-        there = fetch(joined, dcore=1)
-        for array, other in ((joined, False), (there, True)):
-            pieces, first = [], 0
-            for i in batch:
-                _, offset, (lo, hi) = PERMUTES[i]
-                pieces.append((array, first, hi - lo, lo, other, offset))
+        parts = [(arrived[i], *PERMUTES[i][1:]) for i in batch]
+        joined = jnp.concatenate([part[0] for part in parts], axis=0) if len(parts) > 1 else parts[0][0]
+        for array, other, pieces in ((joined, False, here), (fetch(joined, dcore=1), True, there)):
+            batch_pieces, first = [], 0
+            for _, offset, (lo, hi) in parts:
+                batch_pieces.append((array, first, hi - lo, lo, other, offset))
                 first += hi - lo
-            whole = put(whole, pieces, shape, send.dtype)
+            pieces.append(batch_pieces)
+    for batch_pieces in here + there:
+        whole = put(whole, batch_pieces, shape, send.dtype)
     return whole
 
 
 def per_device(pseudo_grad, error_buf, momentum, params, picks):
     blocks, block = params.shape
     replicas = lax.axis_size("rep")
-    own_picks = picks[0].astype(jnp.float32)
-    topk = own_picks.shape[0]
-    positions = lax.iota(jnp.float32, blocks)
+    own_picks = picks[0]
+    payload, momentum_near, params_near = choose(
+        own_picks, error_buf[0], pseudo_grad[0], momentum, params, replicas
+    )
+    everyone = lax.all_to_all(payload, "rep", 0, 0).reshape(-1, payload.shape[-1])
+    new_params, new_momentum, send = update(everyone, momentum_near, params_near)
+    gathered = gather_slab(send, blocks // COLOURS, block)
     accumulated = DECAY_RATE * error_buf[0] + pseudo_grad[0]
-    selector = (own_picks[:, None] == positions[None, :]).astype(jnp.float32)
-    chosen_values = jnp.dot(selector, accumulated, precision=lax.Precision.HIGHEST)
-    payload = jnp.concatenate(
-        [chosen_values, jnp.broadcast_to(own_picks[:, None], (topk, LANES))], axis=1
-    )
-    everyone = lax.all_to_all(
-        jnp.broadcast_to(payload[None], (replicas, topk, block + LANES)), "rep", 0, 0
-    ).reshape(replicas * topk, block + LANES)
-    new_params, new_momentum, send = update(everyone, momentum, params)
-    gathered = gather_slab(send, blocks // COLOURS, block)
-    chosen_mask = jnp.sum(selector, axis=0)
-    new_error = (accumulated * (1.0 - chosen_mask)[:, None])[None]
+    chosen = jnp.any(own_picks[:, None] == lax.iota(jnp.int32, blocks)[None, :], axis=0)
+    new_error = jnp.where(chosen[:, None], 0.0, accumulated)[None]
     return (new_params, new_momentum, new_error, gathered.reshape(-1, block))
 
 

time: 369 us -> 103 us (0.28)
  Pallas kernels: 266 us -> 11.3 us
  starting transfers between devices: 32.7 us -> 25.7 us
    pallas_call x8 -> x6, Pallas kernels: 264 us -> 7.69 us  [put(): pl.pallas_call(kernel, out_shape=jax.ShapeDtypeStruct(shape, dtype), in_s...]
    ppermute x10 -> x8, starting transfers between devices: 32.7 us -> 25.7 us  [fetch(): return lax.ppermute(value, AXES, pairs)]
    ppermute x10 -> x8, waiting for transfers between devices: 7.58 us -> 9.57 us  [fetch(): return lax.ppermute(value, AXES, pairs)]
  transfers between devices with their start and end apart: 10 -> 8, of which waited for: 3 -> 4; matrix products, arithmetic and copies ran while one was open for 1% -> 1% of each run, Pallas kernels for 66% -> 6%
where the time goes in v5:
time: 103 us
  blocking collectives  53.5 us (52%)
  starting transfers between devices  25.7 us (25%)
  Pallas kernels  11.3 us (11%)
  waiting for transfers between devices  9.57 us (9%)
  other arithmetic  1.05 us (1%)
    all_to_all x1, blocking collectives, gather_slab(): own = lax.all_to_all(send, AXES, 0, 0, axis_index_groups=exchange_groups())  35.7 us
    ppermute x8, starting transfers between devices, fetch(): return lax.ppermute(value, AXES, pairs)  25.7 us
    all_to_all x1, blocking collectives, per_device(): lax.all_to_all(payload, 'rep', 0, 0).reshape(-1, payload.shape[-1])  17.7 us
    ppermute x8, waiting for transfers between devices, fetch(): return lax.ppermute(value, AXES, pairs)  9.57 us
    pallas_call x6, Pallas kernels, put(): pl.pallas_call(kernel, out_shape=jax.ShapeDtypeStruct(shape, dtype), in_s...  7.69 us
    pallas_call x1, Pallas kernels, choose(): pl.pallas_call(choose_kernel, out_shape=(jax.ShapeDtypeStruct((replicas,...  2.1 us
  transfers between devices with their start and end apart: 8, of which 4 were waited for; matrix products, arithmetic and copies ran while one was open for 1% of the time, Pallas kernels for 6%

profile of v5, /device:TPU:1, one launch (start us, length us, event | category | flops | bytes accessed | tf_op | source)
XLA Modules:
  0.0 102.8 jit_solution(4451625387386917845)
XLA Ops:
  0.6 0.0 copy-start
  0.6 0.6 copy-done
  1.3 2.1 %shard_map.84 = (f32[16,8,384]{2,1,0:T(8,128)S(1)}, f32[512,256]{1,0:T(8,128)S(1)}, f32[512,256]{1,0:T(8,128)S(1)}) custom-call(s32[8]{0:T(128)S(1)} %bitcast.6, f32[512,256]{1,0:T(8,128)} %bitcast.9, f32[512,256]{1,0:T(8,128)} %bitcast.10, f32[512,256]{1,0:T(8,128)} %momentum.1, f32[512,256]{1,0:T(8,128)} %params.1), custom_call_target="tpu_custom_call" | custom-call | flops 100000 | bytes 2000000 | tf_op jit(solution)/shard_map/pallas_call | solution.py:99
  3.4 17.7 %all_to_all.10 = f32[16,8,384]{2,1,0:T(8,128)S(1)} all-to-all(f32[16,8,384]{2,1,0:T(8,128)S(1)} %get-tuple-element.16), channel_id=1, replica_groups=mesh['rep'=16,'fsdp'=32] {'rep'}, dimensions={0} | all-to-all | bytes 393216 | tf_op jit(solution)/shard_map/all_to_all | solution.py:252
  21.1 1.5 %shard_map.85 = (f32[512,256]{1,0:T(8,128)}, f32[512,256]{1,0:T(8,128)}, bf16[16,128,256]{2,1,0:T(8,128)(2,1)S(1)}) custom-call(f32[128,384]{1,0:T(8,128)S(1)} %bitcast.5, f32[512,256]{1,0:T(8,128)S(1)} %get-tuple-element.17.momentum, f32[512,256]{1,0:T(8,128)S(1)} %get-tuple-element.18.params), custom_call_target="tpu_custom_call" | custom-call | flops 100000000 | bytes 4000000 | tf_op jit(solution)/shard_map/pallas_call | solution.py:152
  22.6 35.7 %all_to_all.11.refs_0_ = bf16[16,128,256]{2,1,0:T(8,128)(2,1)S(1)} all-to-all(bf16[16,128,256]{2,1,0:T(8,128)(2,1)S(1)} %get-tuple-element.21), channel_id=1, replica_groups={{0,2,4,6,8,10,12,14,48,50,52,54,56,58,60,62},{1,3,5,7,9,11,13,15,49,51,..., dimensions={0} | all-to-all | bytes 2097152 | tf_op jit(solution)/shard_map/all_to_all | solution.py:224
  58.4 6.4 %collective-permute-start.5 = (bf16[16,128,256]{2,1,0:T(8,128)(2,1)S(1)}, bf16[16,128,256]{2,1,0:T(8,128)(2,1)S(1)}, u32[]{:S(2)}, u32[]{:S(2)}) collective-permute-start(bf16[16,128,256]{2,1,0:T(8,128)(2,1)S(1)} %all_to_all.11.refs_0_), channel_id=1, source_target_pairs={{1,0},{0,1},{3,2},{2,3},{5,4},{4,5},{7,6},{6,7},{9,8},{8,9},{11,10... | collective-permute-start | bytes 3145736 | tf_op jit(solution)/shard_map/ppermute | solution.py:34
  64.7 4.1 %collective-permute-start = (bf16[16,128,256]{2,1,0:T(8,128)(2,1)S(1)}, bf16[16,128,256]{2,1,0:T(8,128)(2,1)S(1)}, u32[]{:S(2)}, u32[]{:S(2)}) collective-permute-start(bf16[16,128,256]{2,1,0:T(8,128)(2,1)S(1)} %all_to_all.11.refs_0_), channel_id=1, source_target_pairs={{2,0},{3,1},{4,2},{5,3},{6,4},{7,5},{8,6},{9,7},{10,8},{11,9},{12,... | collective-permute-start | bytes 3145736 | tf_op jit(solution)/shard_map/ppermute | solution.py:34
  68.9 2.5 %collective-permute-start.1 = (bf16[10,128,256]{2,1,0:T(8,128)(2,1)S(1)}, bf16[10,128,256]{2,1,0:T(8,128)(2,1)S(1)}, u32[]{:S(2)}, u32[]{:S(2)}) collective-permute-start(bf16[10,128,256]{2,1,0:T(8,128)(2,1)S(1)} %slice.10), channel_id=1, source_target_pairs={{32,0},{33,1},{34,2},{35,3},{36,4},{37,5},{38,6},{39,7},{40,8},{41... | collective-permute-start | bytes 1966088 | tf_op jit(solution)/shard_map/ppermute | solution.py:34
  71.5 2.7 %collective-permute-start.2 = (bf16[10,128,256]{2,1,0:T(8,128)(2,1)S(1)}, bf16[10,128,256]{2,1,0:T(8,128)(2,1)S(1)}, u32[]{:S(2)}, u32[]{:S(2)}) collective-permute-start(bf16[10,128,256]{2,1,0:T(8,128)(2,1)S(1)} %slice.10), channel_id=1, source_target_pairs={{48,0},{49,1},{50,2},{51,3},{52,4},{53,5},{54,6},{55,7},{56,8},{57... | collective-permute-start | bytes 1966088 | tf_op jit(solution)/shard_map/ppermute | solution.py:34
  74.3 2.1 %collective-permute-start.3 = (bf16[6,128,256]{2,1,0:T(8,128)(2,1)S(1)}, bf16[6,128,256]{2,1,0:T(8,128)(2,1)S(1)}, u32[]{:S(2)}, u32[]{:S(2)}) collective-permute-start(bf16[6,128,256]{2,1,0:T(8,128)(2,1)S(1)} %slice.11), channel_id=1, source_target_pairs={{64,0},{65,1},{66,2},{67,3},{68,4},{69,5},{70,6},{71,7},{72,8},{73... | collective-permute-start | bytes 1179656 | tf_op jit(solution)/shard_map/ppermute | solution.py:34
  76.3 0.0 collective-permute-done.5.refs_1_
  76.4 3.2 %collective-permute-start.4 = (bf16[6,128,256]{2,1,0:T(8,128)(2,1)S(1)}, bf16[6,128,256]{2,1,0:T(8,128)(2,1)S(1)}, u32[]{:S(2)}, u32[]{:S(2)}) collective-permute-start(bf16[6,128,256]{2,1,0:T(8,128)(2,1)S(1)} %slice.11), channel_id=1, source_target_pairs={{448,0},{449,1},{450,2},{451,3},{452,4},{453,5},{454,6},{455,7},{4... | collective-permute-start | bytes 1179656 | tf_op jit(solution)/shard_map/ppermute | solution.py:34
  79.6 1.1 %shard_map.86.refs_0_ = bf16[16,2,4,128,256]{4,3,2,1,0:T(8,128)(2,1)} custom-call(bf16[16,128,256]{2,1,0:T(8,128)(2,1)S(1)} %all_to_all.11.refs_0_), custom_call_target="tpu_custom_call" | custom-call | bytes 2097152 | tf_op jit(solution)/shard_map/pallas_call | solution.py:199
  80.7 1.1 %shard_map.87.refs_0_ = bf16[16,2,4,128,256]{4,3,2,1,0:T(8,128)(2,1)} custom-call(bf16[16,2,4,128,256]{4,3,2,1,0:T(8,128)(2,1)} %shard_map.86.refs_0_, bf16[16,128,256]{2,1,0:T(8,128)(2,1)S(1)} %collective-permute-done.5.refs_1_), custom_call_target="tpu_custom_call", output_to_operand_aliasing={{}: (0, {})} | custom-call | bytes 2097152 | tf_op jit(solution)/shard_map/pallas_call | solution.py:199
  81.9 0.0 copy-start.1
  81.9 0.0 copy-start.2
  81.9 4.1 %collective-permute-done.3 = bf16[6,128,256]{2,1,0:T(8,128)(2,1)S(1)} collective-permute-done((bf16[6,128,256]{2,1,0:T(8,128)(2,1)S(1)}, bf16[6,128,256]{2,1,0:T(8,128)(2,1)S(1)}, u32[]{:S(2)}, u32[]{:S(2)}) %collective-permute-start.3) | collective-permute-done | bytes 393248 | tf_op jit(solution)/shard_map/ppermute | solution.py:34
  85.9 3.0 %collective-permute-done.4 = bf16[6,128,256]{2,1,0:T(8,128)(2,1)S(1)} collective-permute-done((bf16[6,128,256]{2,1,0:T(8,128)(2,1)S(1)}, bf16[6,128,256]{2,1,0:T(8,128)(2,1)S(1)}, u32[]{:S(2)}, u32[]{:S(2)}) %collective-permute-start.4) | collective-permute-done | bytes 393248 | tf_op jit(solution)/shard_map/ppermute | solution.py:34
  88.9 0.0 collective-permute-done.1
  88.9 1.4 %collective-permute-done.2 = bf16[10,128,256]{2,1,0:T(8,128)(2,1)S(1)} collective-permute-done((bf16[10,128,256]{2,1,0:T(8,128)(2,1)S(1)}, bf16[10,128,256]{2,1,0:T(8,128)(2,1)S(1)}, u32[]{:S(2)}, u32[]{:S(2)}) %collective-permute-start.2) | collective-permute-done | bytes 655392 | tf_op jit(solution)/shard_map/ppermute | solution.py:34
  90.3 1.1 %collective-permute-done.refs_1_ = bf16[16,128,256]{2,1,0:T(8,128)(2,1)S(1)} collective-permute-done((bf16[16,128,256]{2,1,0:T(8,128)(2,1)S(1)}, bf16[16,128,256]{2,1,0:T(8,128)(2,1)S(1)}, u32[]{:S(2)}, u32[]{:S(2)}) %collective-permute-start) | collective-permute-done | bytes 1048608 | tf_op jit(solution)/shard_map/ppermute | solution.py:34
  91.6 2.7 %collective-permute-start.6 = (bf16[32,128,256]{2,1,0:T(8,128)(2,1)S(1)}, bf16[32,128,256]{2,1,0:T(8,128)(2,1)S(1)}, u32[]{:S(2)}, u32[]{:S(2)}) collective-permute-start(bf16[32,128,256]{2,1,0:T(8,128)(2,1)S(1)} %constant_dynamic-update-slice_fusion.refs_1_), channel_id=1, source_target_pairs={{1,0},{0,1},{3,2},{2,3},{5,4},{4,5},{7,6},{6,7},{9,8},{8,9},{11,10... | collective-permute-start | bytes 6291464 | tf_op jit(solution)/shard_map/ppermute | solution.py:34
  94.3 1.9 %collective-permute-start.7 = (bf16[16,128,256]{2,1,0:T(8,128)(2,1)S(1)}, bf16[16,128,256]{2,1,0:T(8,128)(2,1)S(1)}, u32[]{:S(2)}, u32[]{:S(2)}) collective-permute-start(bf16[16,128,256]{2,1,0:T(8,128)(2,1)S(1)} %collective-permute-done.refs_1_), channel_id=1, source_target_pairs={{1,0},{0,1},{3,2},{2,3},{5,4},{4,5},{7,6},{6,7},{9,8},{8,9},{11,10... | collective-permute-start | bytes 3145736 | tf_op jit(solution)/shard_map/ppermute | solution.py:34
  96.3 0.1 fusion
  96.3 0.0 copy-done.1
  96.4 0.0 copy-done.2
  96.4 1.0 add_select_fusion
  97.3 1.6 %shard_map.88.refs_0_ = bf16[16,2,4,128,256]{4,3,2,1,0:T(8,128)(2,1)} custom-call(bf16[16,2,4,128,256]{4,3,2,1,0:T(8,128)(2,1)} %shard_map.87.refs_0_, bf16[32,128,256]{2,1,0:T(8,128)(2,1)S(1)} %constant_dynamic-update-slice_fusion.refs_1_), custom_call_target="tpu_custom_call", output_to_operand_aliasing={{}: (0, {})} | custom-call | bytes 4194304 | tf_op jit(solution)/shard_map/pallas_call | solution.py:199
  98.9 1.1 %shard_map.89.refs_0_ = bf16[16,2,4,128,256]{4,3,2,1,0:T(8,128)(2,1)} custom-call(bf16[16,2,4,128,256]{4,3,2,1,0:T(8,128)(2,1)} %shard_map.88.refs_0_, bf16[16,128,256]{2,1,0:T(8,128)(2,1)S(1)} %collective-permute-done.refs_1_), custom_call_target="tpu_custom_call", output_to_operand_aliasing={{}: (0, {})} | custom-call | bytes 2097152 | tf_op jit(solution)/shard_map/pallas_call | solution.py:199
  100.0 0.0 collective-permute-done.6.refs_1_
  100.0 1.6 %shard_map.90.refs_0_ = bf16[16,2,4,128,256]{4,3,2,1,0:T(8,128)(2,1)} custom-call(bf16[16,2,4,128,256]{4,3,2,1,0:T(8,128)(2,1)} %shard_map.89.refs_0_, bf16[32,128,256]{2,1,0:T(8,128)(2,1)S(1)} %collective-permute-done.6.refs_1_), custom_call_target="tpu_custom_call", output_to_operand_aliasing={{}: (0, {})} | custom-call | bytes 4194304 | tf_op jit(solution)/shard_map/pallas_call | solution.py:199
  101.7 0.0 collective-permute-done.7.refs_1_
  101.7 1.1 %shard_map.91 = bf16[16,2,4,128,256]{4,3,2,1,0:T(8,128)(2,1)} custom-call(bf16[16,2,4,128,256]{4,3,2,1,0:T(8,128)(2,1)} %shard_map.90.refs_0_, bf16[16,128,256]{2,1,0:T(8,128)(2,1)S(1)} %collective-permute-done.7.refs_1_), custom_call_target="tpu_custom_call", output_to_operand_aliasing={{}: (0, {})} | custom-call | bytes 2097152 | tf_op jit(solution)/shard_map/pallas_call | solution.py:199
  (6 shorter events, 0.2 us)
Async XLA Ops:
  0.6 0.7 copy-start
  58.4 18.0 %collective-permute-start.5 = (bf16[16,128,256]{2,1,0:T(8,128)(2,1)S(1)}, bf16[16,128,256]{2,1,0:T(8,128)(2,1)S(1)}, u32[]{:S(2)}, u32[]{:S(2)}) collective-permute-start(bf16[16,128,256]{2,1,0:T(8,128)(2,1)S(1)} %all_to_all.11.refs_0_), channel_id=1, source_target_pairs={{1,0},{0,1},{3,2},{2,3},{5,4},{4,5},{7,6},{6,7},{9,8},{8,9},{11,10... | collective-permute-start | bytes 3145736 | tf_op jit(solution)/shard_map/ppermute | solution.py:34
  64.7 26.7 %collective-permute-start = (bf16[16,128,256]{2,1,0:T(8,128)(2,1)S(1)}, bf16[16,128,256]{2,1,0:T(8,128)(2,1)S(1)}, u32[]{:S(2)}, u32[]{:S(2)}) collective-permute-start(bf16[16,128,256]{2,1,0:T(8,128)(2,1)S(1)} %all_to_all.11.refs_0_), channel_id=1, source_target_pairs={{2,0},{3,1},{4,2},{5,3},{6,4},{7,5},{8,6},{9,7},{10,8},{11,9},{12,... | collective-permute-start | bytes 3145736 | tf_op jit(solution)/shard_map/ppermute | solution.py:34
  68.9 20.0 %collective-permute-start.1 = (bf16[10,128,256]{2,1,0:T(8,128)(2,1)S(1)}, bf16[10,128,256]{2,1,0:T(8,128)(2,1)S(1)}, u32[]{:S(2)}, u32[]{:S(2)}) collective-permute-start(bf16[10,128,256]{2,1,0:T(8,128)(2,1)S(1)} %slice.10), channel_id=1, source_target_pairs={{32,0},{33,1},{34,2},{35,3},{36,4},{37,5},{38,6},{39,7},{40,8},{41... | collective-permute-start | bytes 1966088 | tf_op jit(solution)/shard_map/ppermute | solution.py:34
  71.5 18.8 %collective-permute-start.2 = (bf16[10,128,256]{2,1,0:T(8,128)(2,1)S(1)}, bf16[10,128,256]{2,1,0:T(8,128)(2,1)S(1)}, u32[]{:S(2)}, u32[]{:S(2)}) collective-permute-start(bf16[10,128,256]{2,1,0:T(8,128)(2,1)S(1)} %slice.10), channel_id=1, source_target_pairs={{48,0},{49,1},{50,2},{51,3},{52,4},{53,5},{54,6},{55,7},{56,8},{57... | collective-permute-start | bytes 1966088 | tf_op jit(solution)/shard_map/ppermute | solution.py:34
  74.3 11.7 %collective-permute-start.3 = (bf16[6,128,256]{2,1,0:T(8,128)(2,1)S(1)}, bf16[6,128,256]{2,1,0:T(8,128)(2,1)S(1)}, u32[]{:S(2)}, u32[]{:S(2)}) collective-permute-start(bf16[6,128,256]{2,1,0:T(8,128)(2,1)S(1)} %slice.11), channel_id=1, source_target_pairs={{64,0},{65,1},{66,2},{67,3},{68,4},{69,5},{70,6},{71,7},{72,8},{73... | collective-permute-start | bytes 1179656 | tf_op jit(solution)/shard_map/ppermute | solution.py:34
  76.4 12.6 %collective-permute-start.4 = (bf16[6,128,256]{2,1,0:T(8,128)(2,1)S(1)}, bf16[6,128,256]{2,1,0:T(8,128)(2,1)S(1)}, u32[]{:S(2)}, u32[]{:S(2)}) collective-permute-start(bf16[6,128,256]{2,1,0:T(8,128)(2,1)S(1)} %slice.11), channel_id=1, source_target_pairs={{448,0},{449,1},{450,2},{451,3},{452,4},{453,5},{454,6},{455,7},{4... | collective-permute-start | bytes 1179656 | tf_op jit(solution)/shard_map/ppermute | solution.py:34
  81.9 14.5 %copy-start.1 = (f32[1,512,256]{2,1,0:T(8,128)S(1)}, f32[1,512,256]{2,1,0:T(8,128)}, u32[]{:S(2)}) copy-start(f32[1,512,256]{2,1,0:T(8,128)} %param.6) | copy-start | bytes 1572868
  81.9 14.5 %copy-start.2 = (f32[1,512,256]{2,1,0:T(8,128)S(1)}, f32[1,512,256]{2,1,0:T(8,128)}, u32[]{:S(2)}) copy-start(f32[1,512,256]{2,1,0:T(8,128)} %param.5) | copy-start | bytes 1572868
  91.6 8.4 %collective-permute-start.6 = (bf16[32,128,256]{2,1,0:T(8,128)(2,1)S(1)}, bf16[32,128,256]{2,1,0:T(8,128)(2,1)S(1)}, u32[]{:S(2)}, u32[]{:S(2)}) collective-permute-start(bf16[32,128,256]{2,1,0:T(8,128)(2,1)S(1)} %constant_dynamic-update-slice_fusion.refs_1_), channel_id=1, source_target_pairs={{1,0},{0,1},{3,2},{2,3},{5,4},{4,5},{7,6},{6,7},{9,8},{8,9},{11,10... | collective-permute-start | bytes 6291464 | tf_op jit(solution)/shard_map/ppermute | solution.py:34
  94.3 7.3 %collective-permute-start.7 = (bf16[16,128,256]{2,1,0:T(8,128)(2,1)S(1)}, bf16[16,128,256]{2,1,0:T(8,128)(2,1)S(1)}, u32[]{:S(2)}, u32[]{:S(2)}) collective-permute-start(bf16[16,128,256]{2,1,0:T(8,128)(2,1)S(1)} %collective-permute-done.refs_1_), channel_id=1, source_target_pairs={{1,0},{0,1},{3,2},{2,3},{5,4},{4,5},{7,6},{6,7},{9,8},{8,9},{11,10... | collective-permute-start | bytes 3145736 | tf_op jit(solution)/shard_map/ppermute | solution.py:34

commit v6 on v5

--- a/solution.py
+++ b/solution.py
@@ -12,7 +12,8 @@
 AXES = ("rep", "fsdp")
 NX, NY, NZ, CORES = 4, 8, 8, 2
 CLASSES = 2 * NZ
-COLOURS = 4
+COLOURS = 8
+SHIFTS = (1, 3)
 VMEM_LIMIT = 40 * 1024 * 1024
 
 
@@ -34,14 +35,13 @@
     return lax.ppermute(value, AXES, pairs)
 
 
-def exchange_groups():
-    groups = []
-    for x in range(NX // 2):
-        for y in range(NY):
-            for core in range(CORES):
-                pair = sorted((x, NX - 1 - x), key=lambda v: v // 2)
-                groups.append([device_at(v, y, z, core) for v in pair for z in range(NZ)])
-    return groups
+def collect(shard, partner):
+    pairs = []
+    for x, y, z, core in PLACES:
+        x_there = NX - 1 - x if partner else x
+        z_there = colour_of(x, y, z) + SHIFTS[x_there // 2]
+        pairs.append((device_at(x_there, y, z_there, core), device_at(x, y, z, core)))
+    return lax.ppermute(shard, AXES, pairs)
 
 
 def place_of_self():
@@ -51,7 +51,7 @@
 
 
 def colour_of(x, y, z):
-    return (x + y + 2 * z) % COLOURS
+    return (2 * x + y + 5 * z) % COLOURS
 
 
 def choose_kernel(picks, error, grad, momentum, params, payload, momentum_near, params_near, rows, sems):
@@ -114,7 +114,7 @@
     )(picks, error, grad, momentum, params)
 
 
-def update_kernel(everyone, momentum, params, new_params, new_momentum, send, shard):
+def update_kernel(everyone, momentum, params, new_params, new_momentum, shard):
     blocks, block = params.shape
     entries = everyone.shape[0]
     values = everyone[:, :block]
@@ -137,13 +137,6 @@
     new_momentum[...] = momentum_now
     new_params[...] = params_now
     shard[...] = params_now.astype(jnp.bfloat16)
-    x, y, z, core = place_of_self()
-    rows = blocks // COLOURS
-    for x_hi in range(2):
-        x_there = lax.select(x // 2 == x_hi, x, NX - 1 - x)
-        for z_there in range(NZ):
-            start = pl.multiple_of(colour_of(x_there, y, z_there) * rows, rows)
-            send[x_hi * NZ + z_there] = shard[pl.ds(start, rows), :]
 
 
 def update(everyone, momentum, params):
@@ -154,11 +147,10 @@
         out_shape=(
             jax.ShapeDtypeStruct((blocks, block), jnp.float32),
             jax.ShapeDtypeStruct((blocks, block), jnp.float32),
-            jax.ShapeDtypeStruct((CLASSES, blocks // COLOURS, block), jnp.bfloat16),
+            jax.ShapeDtypeStruct((blocks, block), jnp.bfloat16),
         ),
         in_specs=[vmem] * 3,
         out_specs=(vmem,) * 3,
-        scratch_shapes=[pltpu.VMEM((blocks, block), jnp.bfloat16)],
         compiler_params=pltpu.CompilerParams(vmem_limit_bytes=VMEM_LIMIT),
         cost_estimate=pl.CostEstimate(flops=10**8, bytes_accessed=4 * 10**6, transcendentals=0),
     )(everyone, momentum, params)
@@ -177,15 +169,18 @@
         out, sems = refs[-2:]
         x, y, z, core = place_of_self()
         copies = []
-        for piece, slot in zip(pieces, slots):
-            _, first, count, cls, other, offset = piece
-            there = 1 - core if other else core
-            colour = (colour_of(x, y, z) + offset) % COLOURS
-            for at in range(count):
+        for (_, first, offset, other), slot in zip(pieces, slots):
+            x_there = (x + offset.get("dx", 0) + NX) % NX
+            y_there = y + offset.get("dy", 0) + NY
+            z_there = z + offset.get("dz", 0) + NZ
+            colour = colour_of(x_there, y_there, z_there)
+            own = x_there // 2
+            for at, x_hi in enumerate((own, 1 - own)):
+                shift = SHIFTS[0] + (SHIFTS[1] - SHIFTS[0]) * x_hi
                 copies.append(
                     pltpu.make_async_copy(
                         sources[slot].at[first + at],
-                        out.at[cls + at, there, colour],
+                        out.at[x_hi * NZ + (colour + shift) % NZ, 1 - core if other else core],
                         sems.at[len(copies)],
                     )
                 )
@@ -194,8 +189,7 @@
         for copy in copies:
             copy.wait()
 
-    total = sum(piece[2] for piece in pieces)
-    moved = 4 * total * pieces[0][0][0].size
+    total = 2 * len(pieces)
     return pl.pallas_call(
         kernel,
         out_shape=jax.ShapeDtypeStruct(shape, dtype),
@@ -205,40 +199,40 @@
         scratch_shapes=[pltpu.SemaphoreType.DMA((total,))],
         input_output_aliases={0: 0} if given else {},
         compiler_params=pltpu.CompilerParams(vmem_limit_bytes=VMEM_LIMIT),
-        cost_estimate=pl.CostEstimate(flops=0, bytes_accessed=moved, transcendentals=0),
+        cost_estimate=pl.CostEstimate(
+            flops=0, bytes_accessed=4 * total * shape[2] * shape[3], transcendentals=0
+        ),
     )(*given, *arrays)
 
 
-PERMUTES = (
-    (dict(dz=1), 2, (0, 16)),
-    (dict(dx=1), 1, (0, 10)),
-    (dict(dx=-1), -1, (0, 10)),
-    (dict(dy=1), 1, (10, 16)),
-    (dict(dy=-1), -1, (10, 16)),
+OTHERS = (
+    dict(dy=1, dz=-1),
+    dict(dx=1),
+    dict(dx=-1),
+    dict(dy=-1),
+    dict(dz=1),
+    dict(dy=1),
+    dict(dz=-1),
 )
-BATCHES = ((1, 3, 2, 4), (0,))
-
-
-def gather_slab(send, rows, block):
-    shape = (CLASSES, CORES, COLOURS, rows, block)
-    own = lax.all_to_all(send, AXES, 0, 0, axis_index_groups=exchange_groups())
-    arrived = [fetch(own[lo:hi], **where) for where, _, (lo, hi) in PERMUTES]
-    own_there = fetch(own, dcore=1)
-    whole = put(None, [(own, 0, CLASSES, 0, False, 0)], shape, send.dtype)
-    whole = put(whole, [(own_there, 0, CLASSES, 0, True, 0)], shape, send.dtype)
+BATCHES = ((0, 1, 2, 3), (4, 5, 6))
+
+
+def gather_slab(shard):
+    shape = (CLASSES, CORES, *shard.shape)
+    portion = jnp.stack([collect(shard, partner=False), collect(shard, partner=True)])
+    arrived = [fetch(portion, **offset) for offset in OTHERS]
+    portion_there = fetch(portion, dcore=1)
+    whole = put(None, [(portion, 0, {}, False)], shape, shard.dtype)
+    whole = put(whole, [(portion_there, 0, {}, True)], shape, shard.dtype)
     *arrived, whole = lax.optimization_barrier((*arrived, whole))
     here, there = [], []
     for batch in BATCHES:
-        parts = [(arrived[i], *PERMUTES[i][1:]) for i in batch]
-        joined = jnp.concatenate([part[0] for part in parts], axis=0) if len(parts) > 1 else parts[0][0]
-        for array, other, pieces in ((joined, False, here), (fetch(joined, dcore=1), True, there)):
-            batch_pieces, first = [], 0
-            for _, offset, (lo, hi) in parts:
-                batch_pieces.append((array, first, hi - lo, lo, other, offset))
-                first += hi - lo
-            pieces.append(batch_pieces)
-    for batch_pieces in here + there:
-        whole = put(whole, batch_pieces, shape, send.dtype)
+        joined = jnp.concatenate([arrived[i] for i in batch], axis=0)
+        joined_there = fetch(joined, dcore=1)
+        here.append([(joined, 2 * at, OTHERS[i], False) for at, i in enumerate(batch)])
+        there.append([(joined_there, 2 * at, OTHERS[i], True) for at, i in enumerate(batch)])
+    for pieces in here + there:
+        whole = put(whole, pieces, shape, shard.dtype)
     return whole
 
 
@@ -250,8 +244,8 @@
         own_picks, error_buf[0], pseudo_grad[0], momentum, params, replicas
     )
     everyone = lax.all_to_all(payload, "rep", 0, 0).reshape(-1, payload.shape[-1])
-    new_params, new_momentum, send = update(everyone, momentum_near, params_near)
-    gathered = gather_slab(send, blocks // COLOURS, block)
+    new_params, new_momentum, shard = update(everyone, momentum_near, params_near)
+    gathered = gather_slab(shard)
     accumulated = DECAY_RATE * error_buf[0] + pseudo_grad[0]
     chosen = jnp.any(own_picks[:, None] == lax.iota(jnp.int32, blocks)[None, :], axis=0)
     new_error = jnp.where(chosen[:, None], 0.0, accumulated)[None]

time: 103 us -> 105 us (1.019)
  the two profiles are of different devices: /device:TPU:1 before, /device:TPU:17 now
where the time goes in v6:
time: 105 us; the launch traced here: 104 us
  starting transfers between devices  55.1 us (52%)
  waiting for transfers between devices  19.8 us (19%)
  blocking collectives  16 us (15%)
  Pallas kernels  10.5 us (10%)
  other arithmetic  1.07 us (1%)
    ppermute x10, starting transfers between devices, fetch(): return lax.ppermute(value, AXES, pairs)  44.4 us
    all_to_all x1, blocking collectives, per_device(): lax.all_to_all(payload, 'rep', 0, 0).reshape(-1, payload.shape[-1])  16 us
    ppermute x10, waiting for transfers between devices, fetch(): return lax.ppermute(value, AXES, pairs)  11.8 us
    ppermute x2, starting transfers between devices, collect(): return lax.ppermute(shard, AXES, pairs)  10.7 us
    ppermute x2, waiting for transfers between devices, collect(): return lax.ppermute(shard, AXES, pairs)  8.01 us
    pallas_call x6, Pallas kernels, put(): pl.pallas_call(kernel, out_shape=jax.ShapeDtypeStruct(shape, dtype), in_s...  6.97 us
  transfers between devices with their start and end apart: 12, of which 5 were waited for; matrix products, arithmetic and copies ran while one was open for 1% of the time, Pallas kernels for 6%

profile of v6, /device:TPU:17, one launch (start us, length us, event | category | flops | bytes accessed | tf_op | source)
XLA Modules:
  0.0 104.2 jit_solution(2180953610975892189)
XLA Ops:
  0.6 0.0 copy-start
  0.6 0.6 copy-done
  1.3 2.1 %shard_map.84 = (f32[16,8,384]{2,1,0:T(8,128)S(1)}, f32[512,256]{1,0:T(8,128)S(1)}, f32[512,256]{1,0:T(8,128)S(1)}) custom-call(s32[8]{0:T(128)S(1)} %bitcast.8, f32[512,256]{1,0:T(8,128)} %bitcast.11, f32[512,256]{1,0:T(8,128)} %bitcast.12, f32[512,256]{1,0:T(8,128)} %momentum.1, f32[512,256]{1,0:T(8,128)} %params.1), custom_call_target="tpu_custom_call" | custom-call | flops 100000 | bytes 2000000 | tf_op jit(solution)/shard_map/pallas_call | solution.py:99
  3.4 16.0 %all_to_all.5 = f32[16,8,384]{2,1,0:T(8,128)S(1)} all-to-all(f32[16,8,384]{2,1,0:T(8,128)S(1)} %get-tuple-element.18), channel_id=1, replica_groups=mesh['rep'=16,'fsdp'=32] {'rep'}, dimensions={0} | all-to-all | bytes 393216 | tf_op jit(solution)/shard_map/all_to_all | solution.py:246
  19.4 1.4 %shard_map.85 = (f32[512,256]{1,0:T(8,128)}, f32[512,256]{1,0:T(8,128)}, bf16[512,256]{1,0:T(8,128)(2,1)S(1)}) custom-call(f32[128,384]{1,0:T(8,128)S(1)} %bitcast.7, f32[512,256]{1,0:T(8,128)S(1)} %get-tuple-element.19.momentum, f32[512,256]{1,0:T(8,128)S(1)} %get-tuple-element.20.params), custom_call_target="tpu_custom_call" | custom-call | flops 100000000 | bytes 4000000 | tf_op jit(solution)/shard_map/pallas_call | solution.py:145
  20.7 4.0 %collective-permute-start = (bf16[512,256]{1,0:T(8,128)(2,1)S(1)}, bf16[512,256]{1,0:T(8,128)(2,1)S(1)}, u32[]{:S(2)}, u32[]{:S(2)}) collective-permute-start(bf16[512,256]{1,0:T(8,128)(2,1)S(1)} %get-tuple-element.23), channel_id=1, source_target_pairs={{2,0},{3,1},{12,2},{13,3},{6,4},{7,5},{0,6},{1,7},{10,8},{11,9},{4... | collective-permute-start | bytes 786440 | tf_op jit(solution)/shard_map/ppermute | solution.py:44
  24.8 6.7 %collective-permute-start.1 = (bf16[512,256]{1,0:T(8,128)(2,1)S(1)}, bf16[512,256]{1,0:T(8,128)(2,1)S(1)}, u32[]{:S(2)}, u32[]{:S(2)}) collective-permute-start(bf16[512,256]{1,0:T(8,128)(2,1)S(1)} %get-tuple-element.23), channel_id=1, source_target_pairs={{54,0},{55,1},{48,2},{49,3},{58,4},{59,5},{52,6},{53,7},{62,8},{63... | collective-permute-start | bytes 786440 | tf_op jit(solution)/shard_map/ppermute | solution.py:44
  31.4 1.8 %collective-permute-done = bf16[512,256]{1,0:T(8,128)(2,1)S(1)} collective-permute-done((bf16[512,256]{1,0:T(8,128)(2,1)S(1)}, bf16[512,256]{1,0:T(8,128)(2,1)S(1)}, u32[]{:S(2)}, u32[]{:S(2)}) %collective-permute-start) | collective-permute-done | bytes 262176 | tf_op jit(solution)/shard_map/ppermute | solution.py:44
  33.2 6.2 %collective-permute-done.1 = bf16[512,256]{1,0:T(8,128)(2,1)S(1)} collective-permute-done((bf16[512,256]{1,0:T(8,128)(2,1)S(1)}, bf16[512,256]{1,0:T(8,128)(2,1)S(1)}, u32[]{:S(2)}, u32[]{:S(2)}) %collective-permute-start.1) | collective-permute-done | bytes 262176 | tf_op jit(solution)/shard_map/ppermute | solution.py:44
  39.4 0.1 pad_maximum_fusion.refs_0_
  39.5 4.4 %collective-permute-start.9 = (bf16[2,512,256]{2,1,0:T(8,128)(2,1)S(1)}, bf16[2,512,256]{2,1,0:T(8,128)(2,1)S(1)}, u32[]{:S(2)}, u32[]{:S(2)}) collective-permute-start(bf16[2,512,256]{2,1,0:T(8,128)(2,1)S(1)} %pad_maximum_fusion.refs_0_), channel_id=1, source_target_pairs={{1,0},{0,1},{3,2},{2,3},{5,4},{4,5},{7,6},{6,7},{9,8},{8,9},{11,10... | collective-permute-start | bytes 1572872 | tf_op jit(solution)/shard_map/ppermute | solution.py:35
  43.9 7.8 %collective-permute-start.2 = (bf16[2,512,256]{2,1,0:T(8,128)(2,1)S(1)}, bf16[2,512,256]{2,1,0:T(8,128)(2,1)S(1)}, u32[]{:S(2)}, u32[]{:S(2)}) collective-permute-start(bf16[2,512,256]{2,1,0:T(8,128)(2,1)S(1)} %pad_maximum_fusion.refs_0_), channel_id=1, source_target_pairs={{78,0},{79,1},{64,2},{65,3},{66,4},{67,5},{68,6},{69,7},{70,8},{71... | collective-permute-start | bytes 1572872 | tf_op jit(solution)/shard_map/ppermute | solution.py:35
  51.7 5.3 %collective-permute-start.3 = (bf16[2,512,256]{2,1,0:T(8,128)(2,1)S(1)}, bf16[2,512,256]{2,1,0:T(8,128)(2,1)S(1)}, u32[]{:S(2)}, u32[]{:S(2)}) collective-permute-start(bf16[2,512,256]{2,1,0:T(8,128)(2,1)S(1)} %pad_maximum_fusion.refs_0_), channel_id=1, source_target_pairs={{32,0},{33,1},{34,2},{35,3},{36,4},{37,5},{38,6},{39,7},{40,8},{41... | collective-permute-start | bytes 1572872 | tf_op jit(solution)/shard_map/ppermute | solution.py:35
  57.0 3.9 %collective-permute-start.4 = (bf16[2,512,256]{2,1,0:T(8,128)(2,1)S(1)}, bf16[2,512,256]{2,1,0:T(8,128)(2,1)S(1)}, u32[]{:S(2)}, u32[]{:S(2)}) collective-permute-start(bf16[2,512,256]{2,1,0:T(8,128)(2,1)S(1)} %pad_maximum_fusion.refs_0_), channel_id=1, source_target_pairs={{48,0},{49,1},{50,2},{51,3},{52,4},{53,5},{54,6},{55,7},{56,8},{57... | collective-permute-start | bytes 1572872 | tf_op jit(solution)/shard_map/ppermute | solution.py:35
  60.9 3.7 %collective-permute-start.5 = (bf16[2,512,256]{2,1,0:T(8,128)(2,1)S(1)}, bf16[2,512,256]{2,1,0:T(8,128)(2,1)S(1)}, u32[]{:S(2)}, u32[]{:S(2)}) collective-permute-start(bf16[2,512,256]{2,1,0:T(8,128)(2,1)S(1)} %pad_maximum_fusion.refs_0_), channel_id=1, source_target_pairs={{448,0},{449,1},{450,2},{451,3},{452,4},{453,5},{454,6},{455,7},{4... | collective-permute-start | bytes 1572872 | tf_op jit(solution)/shard_map/ppermute | solution.py:35
  64.7 0.0 collective-permute-done.9.refs_1_
  64.7 5.4 %collective-permute-start.6 = (bf16[2,512,256]{2,1,0:T(8,128)(2,1)S(1)}, bf16[2,512,256]{2,1,0:T(8,128)(2,1)S(1)}, u32[]{:S(2)}, u32[]{:S(2)}) collective-permute-start(bf16[2,512,256]{2,1,0:T(8,128)(2,1)S(1)} %pad_maximum_fusion.refs_0_), channel_id=1, source_target_pairs={{2,0},{3,1},{4,2},{5,3},{6,4},{7,5},{8,6},{9,7},{10,8},{11,9},{12,... | collective-permute-start | bytes 1572872 | tf_op jit(solution)/shard_map/ppermute | solution.py:35
  70.1 0.0 collective-permute-done.2
  70.1 6.0 %collective-permute-start.7 = (bf16[2,512,256]{2,1,0:T(8,128)(2,1)S(1)}, bf16[2,512,256]{2,1,0:T(8,128)(2,1)S(1)}, u32[]{:S(2)}, u32[]{:S(2)}) collective-permute-start(bf16[2,512,256]{2,1,0:T(8,128)(2,1)S(1)} %pad_maximum_fusion.refs_0_), channel_id=1, source_target_pairs={{64,0},{65,1},{66,2},{67,3},{68,4},{69,5},{70,6},{71,7},{72,8},{73... | collective-permute-start | bytes 1572872 | tf_op jit(solution)/shard_map/ppermute | solution.py:35
  76.1 0.0 collective-permute-done.3
  76.1 1.9 %collective-permute-start.8 = (bf16[2,512,256]{2,1,0:T(8,128)(2,1)S(1)}, bf16[2,512,256]{2,1,0:T(8,128)(2,1)S(1)}, u32[]{:S(2)}, u32[]{:S(2)}) collective-permute-start(bf16[2,512,256]{2,1,0:T(8,128)(2,1)S(1)} %pad_maximum_fusion.refs_0_), channel_id=1, source_target_pairs={{14,0},{15,1},{0,2},{1,3},{2,4},{3,5},{4,6},{5,7},{6,8},{7,9},{8,1... | collective-permute-start | bytes 1572872 | tf_op jit(solution)/shard_map/ppermute | solution.py:35
  78.0 0.8 shard_map.86.refs_0_
  78.9 0.9 shard_map.87.refs_0_
  79.7 0.0 collective-permute-done.4
  79.8 0.0 collective-permute-done.5
  79.8 0.7 collective-permute-done.6
  80.5 6.1 %collective-permute-done.7 = bf16[2,512,256]{2,1,0:T(8,128)(2,1)S(1)} collective-permute-done((bf16[2,512,256]{2,1,0:T(8,128)(2,1)S(1)}, bf16[2,512,256]{2,1,0:T(8,128)(2,1)S(1)}, u32[]{:S(2)}, u32[]{:S(2)}) %collective-permute-start.7) | collective-permute-done | bytes 524320 | tf_op jit(solution)/shard_map/ppermute | solution.py:35
  86.5 5.0 %collective-permute-done.8 = bf16[2,512,256]{2,1,0:T(8,128)(2,1)S(1)} collective-permute-done((bf16[2,512,256]{2,1,0:T(8,128)(2,1)S(1)}, bf16[2,512,256]{2,1,0:T(8,128)(2,1)S(1)}, u32[]{:S(2)}, u32[]{:S(2)}) %collective-permute-start.8) | collective-permute-done | bytes 524320 | tf_op jit(solution)/shard_map/ppermute | solution.py:35
  91.7 0.0 copy-start.1
  91.7 0.0 copy-start.2
  91.7 4.0 %collective-permute-start.10 = (bf16[8,512,256]{2,1,0:T(8,128)(2,1)S(1)}, bf16[8,512,256]{2,1,0:T(8,128)(2,1)S(1)}, u32[]{:S(2)}, u32[]{:S(2)}) collective-permute-start(bf16[8,512,256]{2,1,0:T(8,128)(2,1)S(1)} %constant_dynamic-update-slice_fusion.refs_1_), channel_id=1, source_target_pairs={{1,0},{0,1},{3,2},{2,3},{5,4},{4,5},{7,6},{6,7},{9,8},{8,9},{11,10... | collective-permute-start | bytes 6291464 | tf_op jit(solution)/shard_map/ppermute | solution.py:35
  95.9 1.9 %collective-permute-start.11 = (bf16[6,512,256]{2,1,0:T(8,128)(2,1)S(1)}, bf16[6,512,256]{2,1,0:T(8,128)(2,1)S(1)}, u32[]{:S(2)}, u32[]{:S(2)}) collective-permute-start(bf16[6,512,256]{2,1,0:T(8,128)(2,1)S(1)} %constant_dynamic-update-slice_fusion.4.refs_1_), channel_id=1, source_target_pairs={{1,0},{0,1},{3,2},{2,3},{5,4},{4,5},{7,6},{6,7},{9,8},{8,9},{11,10... | collective-permute-start | bytes 4718600 | tf_op jit(solution)/shard_map/ppermute | solution.py:35
  97.9 0.1 fusion
  97.9 0.0 copy-done.1
  97.9 0.0 copy-done.2
  97.9 0.9 add_select_fusion
  98.9 1.4 %shard_map.88.refs_0_ = bf16[16,2,512,256]{3,2,1,0:T(8,128)(2,1)} custom-call(bf16[16,2,512,256]{3,2,1,0:T(8,128)(2,1)} %shard_map.87.refs_0_, bf16[8,512,256]{2,1,0:T(8,128)(2,1)S(1)} %constant_dynamic-update-slice_fusion.refs_1_), custom_call_target="tpu_custom_call", output_to_operand_aliasing={{}: (0, {})} | custom-call | bytes 4194304 | tf_op jit(solution)/shard_map/pallas_call | solution.py:193
  100.3 1.2 %shard_map.89.refs_0_ = bf16[16,2,512,256]{3,2,1,0:T(8,128)(2,1)} custom-call(bf16[16,2,512,256]{3,2,1,0:T(8,128)(2,1)} %shard_map.88.refs_0_, bf16[6,512,256]{2,1,0:T(8,128)(2,1)S(1)} %constant_dynamic-update-slice_fusion.4.refs_1_), custom_call_target="tpu_custom_call", output_to_operand_aliasing={{}: (0, {})} | custom-call | bytes 3145728 | tf_op jit(solution)/shard_map/pallas_call | solution.py:193
  101.5 0.0 collective-permute-done.10.refs_1_
  101.5 1.4 %shard_map.90.refs_0_ = bf16[16,2,512,256]{3,2,1,0:T(8,128)(2,1)} custom-call(bf16[16,2,512,256]{3,2,1,0:T(8,128)(2,1)} %shard_map.89.refs_0_, bf16[8,512,256]{2,1,0:T(8,128)(2,1)S(1)} %collective-permute-done.10.refs_1_), custom_call_target="tpu_custom_call", output_to_operand_aliasing={{}: (0, {})} | custom-call | bytes 4194304 | tf_op jit(solution)/shard_map/pallas_call | solution.py:193
  102.9 0.0 collective-permute-done.11.refs_1_
  103.0 1.2 %shard_map.91 = bf16[16,2,512,256]{3,2,1,0:T(8,128)(2,1)} custom-call(bf16[16,2,512,256]{3,2,1,0:T(8,128)(2,1)} %shard_map.90.refs_0_, bf16[6,512,256]{2,1,0:T(8,128)(2,1)S(1)} %collective-permute-done.11.refs_1_), custom_call_target="tpu_custom_call", output_to_operand_aliasing={{}: (0, {})} | custom-call | bytes 3145728 | tf_op jit(solution)/shard_map/pallas_call | solution.py:193
  (7 shorter events, 0.3 us)
Async XLA Ops:
  0.6 0.7 copy-start
  20.7 12.5 %collective-permute-start = (bf16[512,256]{1,0:T(8,128)(2,1)S(1)}, bf16[512,256]{1,0:T(8,128)(2,1)S(1)}, u32[]{:S(2)}, u32[]{:S(2)}) collective-permute-start(bf16[512,256]{1,0:T(8,128)(2,1)S(1)} %get-tuple-element.23), channel_id=1, source_target_pairs={{2,0},{3,1},{12,2},{13,3},{6,4},{7,5},{0,6},{1,7},{10,8},{11,9},{4... | collective-permute-start | bytes 786440 | tf_op jit(solution)/shard_map/ppermute | solution.py:44
  24.8 14.7 %collective-permute-start.1 = (bf16[512,256]{1,0:T(8,128)(2,1)S(1)}, bf16[512,256]{1,0:T(8,128)(2,1)S(1)}, u32[]{:S(2)}, u32[]{:S(2)}) collective-permute-start(bf16[512,256]{1,0:T(8,128)(2,1)S(1)} %get-tuple-element.23), channel_id=1, source_target_pairs={{54,0},{55,1},{48,2},{49,3},{58,4},{59,5},{52,6},{53,7},{62,8},{63... | collective-permute-start | bytes 786440 | tf_op jit(solution)/shard_map/ppermute | solution.py:44
  39.5 25.2 %collective-permute-start.9 = (bf16[2,512,256]{2,1,0:T(8,128)(2,1)S(1)}, bf16[2,512,256]{2,1,0:T(8,128)(2,1)S(1)}, u32[]{:S(2)}, u32[]{:S(2)}) collective-permute-start(bf16[2,512,256]{2,1,0:T(8,128)(2,1)S(1)} %pad_maximum_fusion.refs_0_), channel_id=1, source_target_pairs={{1,0},{0,1},{3,2},{2,3},{5,4},{4,5},{7,6},{6,7},{9,8},{8,9},{11,10... | collective-permute-start | bytes 1572872 | tf_op jit(solution)/shard_map/ppermute | solution.py:35
  43.9 26.2 %collective-permute-start.2 = (bf16[2,512,256]{2,1,0:T(8,128)(2,1)S(1)}, bf16[2,512,256]{2,1,0:T(8,128)(2,1)S(1)}, u32[]{:S(2)}, u32[]{:S(2)}) collective-permute-start(bf16[2,512,256]{2,1,0:T(8,128)(2,1)S(1)} %pad_maximum_fusion.refs_0_), channel_id=1, source_target_pairs={{78,0},{79,1},{64,2},{65,3},{66,4},{67,5},{68,6},{69,7},{70,8},{71... | collective-permute-start | bytes 1572872 | tf_op jit(solution)/shard_map/ppermute | solution.py:35
  51.7 24.4 %collective-permute-start.3 = (bf16[2,512,256]{2,1,0:T(8,128)(2,1)S(1)}, bf16[2,512,256]{2,1,0:T(8,128)(2,1)S(1)}, u32[]{:S(2)}, u32[]{:S(2)}) collective-permute-start(bf16[2,512,256]{2,1,0:T(8,128)(2,1)S(1)} %pad_maximum_fusion.refs_0_), channel_id=1, source_target_pairs={{32,0},{33,1},{34,2},{35,3},{36,4},{37,5},{38,6},{39,7},{40,8},{41... | collective-permute-start | bytes 1572872 | tf_op jit(solution)/shard_map/ppermute | solution.py:35
  57.0 22.7 %collective-permute-start.4 = (bf16[2,512,256]{2,1,0:T(8,128)(2,1)S(1)}, bf16[2,512,256]{2,1,0:T(8,128)(2,1)S(1)}, u32[]{:S(2)}, u32[]{:S(2)}) collective-permute-start(bf16[2,512,256]{2,1,0:T(8,128)(2,1)S(1)} %pad_maximum_fusion.refs_0_), channel_id=1, source_target_pairs={{48,0},{49,1},{50,2},{51,3},{52,4},{53,5},{54,6},{55,7},{56,8},{57... | collective-permute-start | bytes 1572872 | tf_op jit(solution)/shard_map/ppermute | solution.py:35
  60.9 18.8 %collective-permute-start.5 = (bf16[2,512,256]{2,1,0:T(8,128)(2,1)S(1)}, bf16[2,512,256]{2,1,0:T(8,128)(2,1)S(1)}, u32[]{:S(2)}, u32[]{:S(2)}) collective-permute-start(bf16[2,512,256]{2,1,0:T(8,128)(2,1)S(1)} %pad_maximum_fusion.refs_0_), channel_id=1, source_target_pairs={{448,0},{449,1},{450,2},{451,3},{452,4},{453,5},{454,6},{455,7},{4... | collective-permute-start | bytes 1572872 | tf_op jit(solution)/shard_map/ppermute | solution.py:35
  64.7 15.8 %collective-permute-start.6 = (bf16[2,512,256]{2,1,0:T(8,128)(2,1)S(1)}, bf16[2,512,256]{2,1,0:T(8,128)(2,1)S(1)}, u32[]{:S(2)}, u32[]{:S(2)}) collective-permute-start(bf16[2,512,256]{2,1,0:T(8,128)(2,1)S(1)} %pad_maximum_fusion.refs_0_), channel_id=1, source_target_pairs={{2,0},{3,1},{4,2},{5,3},{6,4},{7,5},{8,6},{9,7},{10,8},{11,9},{12,... | collective-permute-start | bytes 1572872 | tf_op jit(solution)/shard_map/ppermute | solution.py:35
  70.1 16.4 %collective-permute-start.7 = (bf16[2,512,256]{2,1,0:T(8,128)(2,1)S(1)}, bf16[2,512,256]{2,1,0:T(8,128)(2,1)S(1)}, u32[]{:S(2)}, u32[]{:S(2)}) collective-permute-start(bf16[2,512,256]{2,1,0:T(8,128)(2,1)S(1)} %pad_maximum_fusion.refs_0_), channel_id=1, source_target_pairs={{64,0},{65,1},{66,2},{67,3},{68,4},{69,5},{70,6},{71,7},{72,8},{73... | collective-permute-start | bytes 1572872 | tf_op jit(solution)/shard_map/ppermute | solution.py:35
  76.1 15.4 %collective-permute-start.8 = (bf16[2,512,256]{2,1,0:T(8,128)(2,1)S(1)}, bf16[2,512,256]{2,1,0:T(8,128)(2,1)S(1)}, u32[]{:S(2)}, u32[]{:S(2)}) collective-permute-start(bf16[2,512,256]{2,1,0:T(8,128)(2,1)S(1)} %pad_maximum_fusion.refs_0_), channel_id=1, source_target_pairs={{14,0},{15,1},{0,2},{1,3},{2,4},{3,5},{4,6},{5,7},{6,8},{7,9},{8,1... | collective-permute-start | bytes 1572872 | tf_op jit(solution)/shard_map/ppermute | solution.py:35
  91.7 6.3 %copy-start.1 = (f32[1,512,256]{2,1,0:T(8,128)S(1)}, f32[1,512,256]{2,1,0:T(8,128)}, u32[]{:S(2)}) copy-start(f32[1,512,256]{2,1,0:T(8,128)} %param.6) | copy-start | bytes 1572868
  91.7 6.3 %copy-start.2 = (f32[1,512,256]{2,1,0:T(8,128)S(1)}, f32[1,512,256]{2,1,0:T(8,128)}, u32[]{:S(2)}) copy-start(f32[1,512,256]{2,1,0:T(8,128)} %param.5) | copy-start | bytes 1572868
  91.7 9.8 %collective-permute-start.10 = (bf16[8,512,256]{2,1,0:T(8,128)(2,1)S(1)}, bf16[8,512,256]{2,1,0:T(8,128)(2,1)S(1)}, u32[]{:S(2)}, u32[]{:S(2)}) collective-permute-start(bf16[8,512,256]{2,1,0:T(8,128)(2,1)S(1)} %constant_dynamic-update-slice_fusion.refs_1_), channel_id=1, source_target_pairs={{1,0},{0,1},{3,2},{2,3},{5,4},{4,5},{7,6},{6,7},{9,8},{8,9},{11,10... | collective-permute-start | bytes 6291464 | tf_op jit(solution)/shard_map/ppermute | solution.py:35
  95.9 7.0 %collective-permute-start.11 = (bf16[6,512,256]{2,1,0:T(8,128)(2,1)S(1)}, bf16[6,512,256]{2,1,0:T(8,128)(2,1)S(1)}, u32[]{:S(2)}, u32[]{:S(2)}) collective-permute-start(bf16[6,512,256]{2,1,0:T(8,128)(2,1)S(1)} %constant_dynamic-update-slice_fusion.4.refs_1_), channel_id=1, source_target_pairs={{1,0},{0,1},{3,2},{2,3},{5,4},{4,5},{7,6},{6,7},{9,8},{8,9},{11,10... | collective-permute-start | bytes 4718600 | tf_op jit(solution)/shard_map/ppermute | solution.py:35

commit v7 on v6

--- a/solution.py
+++ b/solution.py
@@ -27,11 +27,16 @@
 ]
 
 
-def fetch(value, dx=0, dy=0, dz=0, dcore=0):
-    pairs = [
-        (device_at(x + dx, y + dy, z + dz, core + dcore), device_at(x, y, z, core))
-        for x, y, z, core in PLACES
-    ]
+def fetch(value, offsets):
+    pairs = []
+    for x, y, z, core in PLACES:
+        dx, dy, dz = offsets[core]
+        pairs.append((device_at(x + dx, y + dy, z + dz, core), device_at(x, y, z, core)))
+    return lax.ppermute(value, AXES, pairs)
+
+
+def swap(value):
+    pairs = [(device_at(x, y, z, 1 - core), device_at(x, y, z, core)) for x, y, z, core in PLACES]
     return lax.ppermute(value, AXES, pairs)
 
 
@@ -169,18 +174,19 @@
         out, sems = refs[-2:]
         x, y, z, core = place_of_self()
         copies = []
-        for (_, first, offset, other), slot in zip(pieces, slots):
-            x_there = (x + offset.get("dx", 0) + NX) % NX
-            y_there = y + offset.get("dy", 0) + NY
-            z_there = z + offset.get("dz", 0) + NZ
-            colour = colour_of(x_there, y_there, z_there)
+        for (_, first, count, offsets, other), slot in zip(pieces, slots):
+            by = 1 - core if other else core
+            dx, dy, dz = (one + (two - one) * by for one, two in zip(*offsets))
+            x_there = (x + dx + NX) % NX
+            colour = colour_of(x_there, y + dy + NY, z + dz + NZ)
             own = x_there // 2
-            for at, x_hi in enumerate((own, 1 - own)):
+            for at in range(count):
+                x_hi = 1 - own if at % 2 else own
                 shift = SHIFTS[0] + (SHIFTS[1] - SHIFTS[0]) * x_hi
                 copies.append(
                     pltpu.make_async_copy(
                         sources[slot].at[first + at],
-                        out.at[x_hi * NZ + (colour + shift) % NZ, 1 - core if other else core],
+                        out.at[x_hi * NZ + (colour + shift) % NZ, 1 - by if at >= 2 else by],
                         sems.at[len(copies)],
                     )
                 )
@@ -189,7 +195,7 @@
         for copy in copies:
             copy.wait()
 
-    total = 2 * len(pieces)
+    total = sum(piece[2] for piece in pieces)
     return pl.pallas_call(
         kernel,
         out_shape=jax.ShapeDtypeStruct(shape, dtype),
@@ -205,32 +211,34 @@
     )(*given, *arrays)
 
 
-OTHERS = (
-    dict(dy=1, dz=-1),
-    dict(dx=1),
-    dict(dx=-1),
-    dict(dy=-1),
-    dict(dz=1),
-    dict(dy=1),
-    dict(dz=-1),
+HERE = ((0, 0, 0), (0, 0, 0))
+OPPOSITE = ((0, 1, -1), (0, -1, 1))
+NEIGHBOURS = (
+    ((1, 0, 0), (-1, 0, 0)),
+    ((0, 1, 0), (0, -1, 0)),
+    ((0, 0, 1), (0, 0, -1)),
 )
-BATCHES = ((0, 1, 2, 3), (4, 5, 6))
 
 
 def gather_slab(shard):
     shape = (CLASSES, CORES, *shard.shape)
-    portion = jnp.stack([collect(shard, partner=False), collect(shard, partner=True)])
-    arrived = [fetch(portion, **offset) for offset in OTHERS]
-    portion_there = fetch(portion, dcore=1)
-    whole = put(None, [(portion, 0, {}, False)], shape, shard.dtype)
-    whole = put(whole, [(portion_there, 0, {}, True)], shape, shard.dtype)
-    *arrived, whole = lax.optimization_barrier((*arrived, whole))
+    half = jnp.stack([collect(shard, partner=False), collect(shard, partner=True)])
+    opposite = fetch(half, OPPOSITE)
+    portion = jnp.concatenate([half, swap(half)], axis=0)
+    arrived = [fetch(portion, offsets) for offsets in NEIGHBOURS]
+    whole = put(None, [(portion, 0, 4, HERE, False)], shape, shard.dtype)
+    opposite, *arrived, whole = lax.optimization_barrier((opposite, *arrived, whole))
+    batches = (
+        ((arrived[0], 4, NEIGHBOURS[0]), (arrived[1], 4, NEIGHBOURS[1])),
+        ((arrived[2], 4, NEIGHBOURS[2]), (opposite, 2, OPPOSITE)),
+    )
     here, there = [], []
-    for batch in BATCHES:
-        joined = jnp.concatenate([arrived[i] for i in batch], axis=0)
-        joined_there = fetch(joined, dcore=1)
-        here.append([(joined, 2 * at, OTHERS[i], False) for at, i in enumerate(batch)])
-        there.append([(joined_there, 2 * at, OTHERS[i], True) for at, i in enumerate(batch)])
+    for batch in batches:
+        joined = jnp.concatenate([array for array, _, _ in batch], axis=0)
+        joined_there = swap(joined)
+        firsts = (0, batch[0][1])
+        here.append([(joined, at, n, off, False) for at, (_, n, off) in zip(firsts, batch)])
+        there.append([(joined_there, at, n, off, True) for at, (_, n, off) in zip(firsts, batch)])
     for pieces in here + there:
         whole = put(whole, pieces, shape, shard.dtype)
     return whole

time: 105 us -> 98 us (0.933)
  the two profiles are of different devices: /device:TPU:17 before, /device:TPU:1 now
where the time goes in v7:
time: 98 us; the launch traced here: 97.5 us
  starting transfers between devices  43.6 us (44%)
  waiting for transfers between devices  23.5 us (24%)
  blocking collectives  17.7 us (18%)
  Pallas kernels  9.8 us (10%)
  other arithmetic  1.17 us (1%)
    ppermute x4, starting transfers between devices, fetch(): return lax.ppermute(value, AXES, pairs)  18.9 us
    all_to_all x1, blocking collectives, per_device(): lax.all_to_all(payload, 'rep', 0, 0).reshape(-1, payload.shape[-1])  17.7 us
    ppermute x4, waiting for transfers between devices, fetch(): return lax.ppermute(value, AXES, pairs)  15.1 us
    ppermute x2, starting transfers between devices, collect(): return lax.ppermute(shard, AXES, pairs)  14.1 us
    ppermute x3, starting transfers between devices, swap(): return lax.ppermute(value, AXES, pairs)  10.7 us
    ppermute x2, waiting for transfers between devices, collect(): return lax.ppermute(shard, AXES, pairs)  6.86 us
    pallas_call x5, Pallas kernels, put(): pl.pallas_call(kernel, out_shape=jax.ShapeDtypeStruct(shape, dtype), in_s...  6.31 us
    pallas_call x1, Pallas kernels, choose(): pl.pallas_call(choose_kernel, out_shape=(jax.ShapeDtypeStruct((replicas,...  2.1 us
  transfers between devices with their start and end apart: 9, of which 4 were waited for; matrix products, arithmetic and copies ran while one was open for 1% of the time, Pallas kernels for 5%

profile of v7, /device:TPU:1, one launch (start us, length us, event | category | flops | bytes accessed | tf_op | source)
XLA Modules:
  0.0 97.5 jit_solution(12367617344536618014)
XLA Ops:
  0.6 0.0 copy-start
  0.6 0.6 copy-done
  1.3 2.1 %shard_map.84 = (f32[16,8,384]{2,1,0:T(8,128)S(1)}, f32[512,256]{1,0:T(8,128)S(1)}, f32[512,256]{1,0:T(8,128)S(1)}) custom-call(s32[8]{0:T(128)S(1)} %bitcast.8, f32[512,256]{1,0:T(8,128)} %bitcast.11, f32[512,256]{1,0:T(8,128)} %bitcast.12, f32[512,256]{1,0:T(8,128)} %momentum.1, f32[512,256]{1,0:T(8,128)} %params.1), custom_call_target="tpu_custom_call" | custom-call | flops 100000 | bytes 2000000 | tf_op jit(solution)/shard_map/pallas_call | solution.py:104
  3.4 17.7 %all_to_all.5 = f32[16,8,384]{2,1,0:T(8,128)S(1)} all-to-all(f32[16,8,384]{2,1,0:T(8,128)S(1)} %get-tuple-element.15), channel_id=1, replica_groups=mesh['rep'=16,'fsdp'=32] {'rep'}, dimensions={0} | all-to-all | bytes 393216 | tf_op jit(solution)/shard_map/all_to_all | solution.py:254
  21.1 1.4 %shard_map.85 = (f32[512,256]{1,0:T(8,128)}, f32[512,256]{1,0:T(8,128)}, bf16[512,256]{1,0:T(8,128)(2,1)S(1)}) custom-call(f32[128,384]{1,0:T(8,128)S(1)} %bitcast.7, f32[512,256]{1,0:T(8,128)S(1)} %get-tuple-element.16.momentum, f32[512,256]{1,0:T(8,128)S(1)} %get-tuple-element.17.params), custom_call_target="tpu_custom_call" | custom-call | flops 100000000 | bytes 4000000 | tf_op jit(solution)/shard_map/pallas_call | solution.py:150
  22.5 7.6 %collective-permute-start = (bf16[512,256]{1,0:T(8,128)(2,1)S(1)}, bf16[512,256]{1,0:T(8,128)(2,1)S(1)}, u32[]{:S(2)}, u32[]{:S(2)}) collective-permute-start(bf16[512,256]{1,0:T(8,128)(2,1)S(1)} %get-tuple-element.20), channel_id=1, source_target_pairs={{2,0},{3,1},{12,2},{13,3},{6,4},{7,5},{0,6},{1,7},{10,8},{11,9},{4... | collective-permute-start | bytes 786440 | tf_op jit(solution)/shard_map/ppermute | solution.py:49
  30.1 6.5 %collective-permute-start.1 = (bf16[512,256]{1,0:T(8,128)(2,1)S(1)}, bf16[512,256]{1,0:T(8,128)(2,1)S(1)}, u32[]{:S(2)}, u32[]{:S(2)}) collective-permute-start(bf16[512,256]{1,0:T(8,128)(2,1)S(1)} %get-tuple-element.20), channel_id=1, source_target_pairs={{54,0},{55,1},{48,2},{49,3},{58,4},{59,5},{52,6},{53,7},{62,8},{63... | collective-permute-start | bytes 786440 | tf_op jit(solution)/shard_map/ppermute | solution.py:49
  36.6 0.0 collective-permute-done
  36.6 6.9 %collective-permute-done.1 = bf16[512,256]{1,0:T(8,128)(2,1)S(1)} collective-permute-done((bf16[512,256]{1,0:T(8,128)(2,1)S(1)}, bf16[512,256]{1,0:T(8,128)(2,1)S(1)}, u32[]{:S(2)}, u32[]{:S(2)}) %collective-permute-start.1) | collective-permute-done | bytes 262176 | tf_op jit(solution)/shard_map/ppermute | solution.py:49
  43.5 0.1 pad_maximum_fusion.1
  43.5 6.2 %collective-permute-start.3 = (bf16[2,512,256]{2,1,0:T(8,128)(2,1)S(1)}, bf16[2,512,256]{2,1,0:T(8,128)(2,1)S(1)}, u32[]{:S(2)}, u32[]{:S(2)}) collective-permute-start(bf16[2,512,256]{2,1,0:T(8,128)(2,1)S(1)} %pad_maximum_fusion.1), channel_id=1, source_target_pairs={{1,0},{0,1},{3,2},{2,3},{5,4},{4,5},{7,6},{6,7},{9,8},{8,9},{11,10... | collective-permute-start | bytes 1572872 | tf_op jit(solution)/shard_map/ppermute | solution.py:40
  49.8 1.5 %collective-permute-done.3 = bf16[2,512,256]{2,1,0:T(8,128)(2,1)S(1)} collective-permute-done((bf16[2,512,256]{2,1,0:T(8,128)(2,1)S(1)}, bf16[2,512,256]{2,1,0:T(8,128)(2,1)S(1)}, u32[]{:S(2)}, u32[]{:S(2)}) %collective-permute-start.3) | collective-permute-done | bytes 524320 | tf_op jit(solution)/shard_map/ppermute | solution.py:40
  51.3 0.1 pad_maximum_fusion.refs_0_
  51.4 4.0 %collective-permute-start.4 = (bf16[4,512,256]{2,1,0:T(8,128)(2,1)S(1)}, bf16[4,512,256]{2,1,0:T(8,128)(2,1)S(1)}, u32[]{:S(2)}, u32[]{:S(2)}) collective-permute-start(bf16[4,512,256]{2,1,0:T(8,128)(2,1)S(1)} %pad_maximum_fusion.refs_0_), channel_id=1, source_target_pairs={{32,0},{49,1},{34,2},{51,3},{36,4},{53,5},{38,6},{55,7},{40,8},{57... | collective-permute-start | bytes 3145736 | tf_op jit(solution)/shard_map/ppermute | solution.py:35
  55.4 8.7 %collective-permute-start.5 = (bf16[4,512,256]{2,1,0:T(8,128)(2,1)S(1)}, bf16[4,512,256]{2,1,0:T(8,128)(2,1)S(1)}, u32[]{:S(2)}, u32[]{:S(2)}) collective-permute-start(bf16[4,512,256]{2,1,0:T(8,128)(2,1)S(1)} %pad_maximum_fusion.refs_0_), channel_id=1, source_target_pairs={{64,0},{449,1},{66,2},{451,3},{68,4},{453,5},{70,6},{455,7},{72,8}... | collective-permute-start | bytes 3145736 | tf_op jit(solution)/shard_map/ppermute | solution.py:35
  64.1 1.9 %collective-permute-start.6 = (bf16[4,512,256]{2,1,0:T(8,128)(2,1)S(1)}, bf16[4,512,256]{2,1,0:T(8,128)(2,1)S(1)}, u32[]{:S(2)}, u32[]{:S(2)}) collective-permute-start(bf16[4,512,256]{2,1,0:T(8,128)(2,1)S(1)} %pad_maximum_fusion.refs_0_), channel_id=1, source_target_pairs={{2,0},{15,1},{4,2},{1,3},{6,4},{3,5},{8,6},{5,7},{10,8},{7,9},{12,... | collective-permute-start | bytes 3145736 | tf_op jit(solution)/shard_map/ppermute | solution.py:35
  66.0 4.3 %collective-permute-start.2 = (bf16[2,512,256]{2,1,0:T(8,128)(2,1)S(1)}, bf16[2,512,256]{2,1,0:T(8,128)(2,1)S(1)}, u32[]{:S(2)}, u32[]{:S(2)}) collective-permute-start(bf16[2,512,256]{2,1,0:T(8,128)(2,1)S(1)} %pad_maximum_fusion.1), channel_id=1, source_target_pairs={{78,0},{451,1},{64,2},{453,3},{66,4},{455,5},{68,6},{457,7},{70,8}... | collective-permute-start | bytes 1572872 | tf_op jit(solution)/shard_map/ppermute | solution.py:35
  70.3 1.0 %shard_map.86.refs_0_ = bf16[16,2,512,256]{3,2,1,0:T(8,128)(2,1)} custom-call(bf16[4,512,256]{2,1,0:T(8,128)(2,1)S(1)} %pad_maximum_fusion.refs_0_), custom_call_target="tpu_custom_call" | custom-call | bytes 2097152 | tf_op jit(solution)/shard_map/pallas_call | solution.py:199
  71.3 10.5 %collective-permute-done.2 = bf16[2,512,256]{2,1,0:T(8,128)(2,1)S(1)} collective-permute-done((bf16[2,512,256]{2,1,0:T(8,128)(2,1)S(1)}, bf16[2,512,256]{2,1,0:T(8,128)(2,1)S(1)}, u32[]{:S(2)}, u32[]{:S(2)}) %collective-permute-start.2) | collective-permute-done | bytes 524320 | tf_op jit(solution)/shard_map/ppermute | solution.py:35
  81.9 0.0 collective-permute-done.4
  81.9 0.0 collective-permute-done.5
  81.9 4.5 %collective-permute-done.6 = bf16[4,512,256]{2,1,0:T(8,128)(2,1)S(1)} collective-permute-done((bf16[4,512,256]{2,1,0:T(8,128)(2,1)S(1)}, bf16[4,512,256]{2,1,0:T(8,128)(2,1)S(1)}, u32[]{:S(2)}, u32[]{:S(2)}) %collective-permute-start.6) | collective-permute-done | bytes 1048608 | tf_op jit(solution)/shard_map/ppermute | solution.py:35
  86.4 0.1 constant_dynamic-update-slice_fusion.1
  86.5 0.1 constant_dynamic-update-slice_fusion.refs_1_
  86.6 0.0 copy-start.1
  86.6 0.0 copy-start.2
  86.6 2.1 %collective-permute-start.7 = (bf16[8,512,256]{2,1,0:T(8,128)(2,1)S(1)}, bf16[8,512,256]{2,1,0:T(8,128)(2,1)S(1)}, u32[]{:S(2)}, u32[]{:S(2)}) collective-permute-start(bf16[8,512,256]{2,1,0:T(8,128)(2,1)S(1)} %constant_dynamic-update-slice_fusion.refs_1_), channel_id=1, source_target_pairs={{1,0},{0,1},{3,2},{2,3},{5,4},{4,5},{7,6},{6,7},{9,8},{8,9},{11,10... | collective-permute-start | bytes 6291464 | tf_op jit(solution)/shard_map/ppermute | solution.py:40
  88.7 0.1 constant_dynamic-update-slice_fusion.3
  88.8 2.4 %collective-permute-start.8 = (bf16[6,512,256]{2,1,0:T(8,128)(2,1)S(1)}, bf16[6,512,256]{2,1,0:T(8,128)(2,1)S(1)}, u32[]{:S(2)}, u32[]{:S(2)}) collective-permute-start(bf16[6,512,256]{2,1,0:T(8,128)(2,1)S(1)} %constant_dynamic-update-slice_fusion.2.refs_1_), channel_id=1, source_target_pairs={{1,0},{0,1},{3,2},{2,3},{5,4},{4,5},{7,6},{6,7},{9,8},{8,9},{11,10... | collective-permute-start | bytes 4718600 | tf_op jit(solution)/shard_map/ppermute | solution.py:40
  91.2 0.1 fusion
  91.3 0.0 copy-done.1
  91.3 0.0 copy-done.2
  91.3 0.9 add_select_fusion
  92.2 1.4 %shard_map.87.refs_0_ = bf16[16,2,512,256]{3,2,1,0:T(8,128)(2,1)} custom-call(bf16[16,2,512,256]{3,2,1,0:T(8,128)(2,1)} %shard_map.86.refs_0_, bf16[8,512,256]{2,1,0:T(8,128)(2,1)S(1)} %constant_dynamic-update-slice_fusion.refs_1_), custom_call_target="tpu_custom_call", output_to_operand_aliasing={{}: (0, {})} | custom-call | bytes 4194304 | tf_op jit(solution)/shard_map/pallas_call | solution.py:199
  93.6 1.2 %shard_map.88.refs_0_ = bf16[16,2,512,256]{3,2,1,0:T(8,128)(2,1)} custom-call(bf16[16,2,512,256]{3,2,1,0:T(8,128)(2,1)} %shard_map.87.refs_0_, bf16[6,512,256]{2,1,0:T(8,128)(2,1)S(1)} %constant_dynamic-update-slice_fusion.2.refs_1_), custom_call_target="tpu_custom_call", output_to_operand_aliasing={{}: (0, {})} | custom-call | bytes 3145728 | tf_op jit(solution)/shard_map/pallas_call | solution.py:199
  94.9 0.0 collective-permute-done.7.refs_1_
  94.9 1.4 %shard_map.89.refs_0_ = bf16[16,2,512,256]{3,2,1,0:T(8,128)(2,1)} custom-call(bf16[16,2,512,256]{3,2,1,0:T(8,128)(2,1)} %shard_map.88.refs_0_, bf16[8,512,256]{2,1,0:T(8,128)(2,1)S(1)} %collective-permute-done.7.refs_1_), custom_call_target="tpu_custom_call", output_to_operand_aliasing={{}: (0, {})} | custom-call | bytes 4194304 | tf_op jit(solution)/shard_map/pallas_call | solution.py:199
  96.3 0.0 collective-permute-done.8.refs_1_
  96.3 1.2 %shard_map.90 = bf16[16,2,512,256]{3,2,1,0:T(8,128)(2,1)} custom-call(bf16[16,2,512,256]{3,2,1,0:T(8,128)(2,1)} %shard_map.89.refs_0_, bf16[6,512,256]{2,1,0:T(8,128)(2,1)S(1)} %collective-permute-done.8.refs_1_), custom_call_target="tpu_custom_call", output_to_operand_aliasing={{}: (0, {})} | custom-call | bytes 3145728 | tf_op jit(solution)/shard_map/pallas_call | solution.py:199
  (1 shorter events, 0.0 us)
Async XLA Ops:
  0.6 0.7 copy-start
  22.5 14.1 %collective-permute-start = (bf16[512,256]{1,0:T(8,128)(2,1)S(1)}, bf16[512,256]{1,0:T(8,128)(2,1)S(1)}, u32[]{:S(2)}, u32[]{:S(2)}) collective-permute-start(bf16[512,256]{1,0:T(8,128)(2,1)S(1)} %get-tuple-element.20), channel_id=1, source_target_pairs={{2,0},{3,1},{12,2},{13,3},{6,4},{7,5},{0,6},{1,7},{10,8},{11,9},{4... | collective-permute-start | bytes 786440 | tf_op jit(solution)/shard_map/ppermute | solution.py:49
  30.1 13.3 %collective-permute-start.1 = (bf16[512,256]{1,0:T(8,128)(2,1)S(1)}, bf16[512,256]{1,0:T(8,128)(2,1)S(1)}, u32[]{:S(2)}, u32[]{:S(2)}) collective-permute-start(bf16[512,256]{1,0:T(8,128)(2,1)S(1)} %get-tuple-element.20), channel_id=1, source_target_pairs={{54,0},{55,1},{48,2},{49,3},{58,4},{59,5},{52,6},{53,7},{62,8},{63... | collective-permute-start | bytes 786440 | tf_op jit(solution)/shard_map/ppermute | solution.py:49
  43.5 7.7 %collective-permute-start.3 = (bf16[2,512,256]{2,1,0:T(8,128)(2,1)S(1)}, bf16[2,512,256]{2,1,0:T(8,128)(2,1)S(1)}, u32[]{:S(2)}, u32[]{:S(2)}) collective-permute-start(bf16[2,512,256]{2,1,0:T(8,128)(2,1)S(1)} %pad_maximum_fusion.1), channel_id=1, source_target_pairs={{1,0},{0,1},{3,2},{2,3},{5,4},{4,5},{7,6},{6,7},{9,8},{8,9},{11,10... | collective-permute-start | bytes 1572872 | tf_op jit(solution)/shard_map/ppermute | solution.py:40
  51.4 30.5 %collective-permute-start.4 = (bf16[4,512,256]{2,1,0:T(8,128)(2,1)S(1)}, bf16[4,512,256]{2,1,0:T(8,128)(2,1)S(1)}, u32[]{:S(2)}, u32[]{:S(2)}) collective-permute-start(bf16[4,512,256]{2,1,0:T(8,128)(2,1)S(1)} %pad_maximum_fusion.refs_0_), channel_id=1, source_target_pairs={{32,0},{49,1},{34,2},{51,3},{36,4},{53,5},{38,6},{55,7},{40,8},{57... | collective-permute-start | bytes 3145736 | tf_op jit(solution)/shard_map/ppermute | solution.py:35
  55.4 26.5 %collective-permute-start.5 = (bf16[4,512,256]{2,1,0:T(8,128)(2,1)S(1)}, bf16[4,512,256]{2,1,0:T(8,128)(2,1)S(1)}, u32[]{:S(2)}, u32[]{:S(2)}) collective-permute-start(bf16[4,512,256]{2,1,0:T(8,128)(2,1)S(1)} %pad_maximum_fusion.refs_0_), channel_id=1, source_target_pairs={{64,0},{449,1},{66,2},{451,3},{68,4},{453,5},{70,6},{455,7},{72,8}... | collective-permute-start | bytes 3145736 | tf_op jit(solution)/shard_map/ppermute | solution.py:35
  64.1 22.4 %collective-permute-start.6 = (bf16[4,512,256]{2,1,0:T(8,128)(2,1)S(1)}, bf16[4,512,256]{2,1,0:T(8,128)(2,1)S(1)}, u32[]{:S(2)}, u32[]{:S(2)}) collective-permute-start(bf16[4,512,256]{2,1,0:T(8,128)(2,1)S(1)} %pad_maximum_fusion.refs_0_), channel_id=1, source_target_pairs={{2,0},{15,1},{4,2},{1,3},{6,4},{3,5},{8,6},{5,7},{10,8},{7,9},{12,... | collective-permute-start | bytes 3145736 | tf_op jit(solution)/shard_map/ppermute | solution.py:35
  66.0 15.9 %collective-permute-start.2 = (bf16[2,512,256]{2,1,0:T(8,128)(2,1)S(1)}, bf16[2,512,256]{2,1,0:T(8,128)(2,1)S(1)}, u32[]{:S(2)}, u32[]{:S(2)}) collective-permute-start(bf16[2,512,256]{2,1,0:T(8,128)(2,1)S(1)} %pad_maximum_fusion.1), channel_id=1, source_target_pairs={{78,0},{451,1},{64,2},{453,3},{66,4},{455,5},{68,6},{457,7},{70,8}... | collective-permute-start | bytes 1572872 | tf_op jit(solution)/shard_map/ppermute | solution.py:35
  86.6 4.7 %copy-start.1 = (f32[1,512,256]{2,1,0:T(8,128)S(1)}, f32[1,512,256]{2,1,0:T(8,128)}, u32[]{:S(2)}) copy-start(f32[1,512,256]{2,1,0:T(8,128)} %param.6) | copy-start | bytes 1572868
  86.6 4.7 %copy-start.2 = (f32[1,512,256]{2,1,0:T(8,128)S(1)}, f32[1,512,256]{2,1,0:T(8,128)}, u32[]{:S(2)}) copy-start(f32[1,512,256]{2,1,0:T(8,128)} %param.5) | copy-start | bytes 1572868
  86.6 8.2 %collective-permute-start.7 = (bf16[8,512,256]{2,1,0:T(8,128)(2,1)S(1)}, bf16[8,512,256]{2,1,0:T(8,128)(2,1)S(1)}, u32[]{:S(2)}, u32[]{:S(2)}) collective-permute-start(bf16[8,512,256]{2,1,0:T(8,128)(2,1)S(1)} %constant_dynamic-update-slice_fusion.refs_1_), channel_id=1, source_target_pairs={{1,0},{0,1},{3,2},{2,3},{5,4},{4,5},{7,6},{6,7},{9,8},{8,9},{11,10... | collective-permute-start | bytes 6291464 | tf_op jit(solution)/shard_map/ppermute | solution.py:40
  88.8 7.5 %collective-permute-start.8 = (bf16[6,512,256]{2,1,0:T(8,128)(2,1)S(1)}, bf16[6,512,256]{2,1,0:T(8,128)(2,1)S(1)}, u32[]{:S(2)}, u32[]{:S(2)}) collective-permute-start(bf16[6,512,256]{2,1,0:T(8,128)(2,1)S(1)} %constant_dynamic-update-slice_fusion.2.refs_1_), channel_id=1, source_target_pairs={{1,0},{0,1},{3,2},{2,3},{5,4},{4,5},{7,6},{6,7},{9,8},{8,9},{11,10... | collective-permute-start | bytes 4718600 | tf_op jit(solution)/shard_map/ppermute | solution.py:40

commit v8 on v7

--- a/solution.py
+++ b/solution.py
@@ -59,8 +59,20 @@
     return (2 * x + y + 5 * z) % COLOURS
 
 
-def choose_kernel(picks, error, grad, momentum, params, payload, momentum_near, params_near, rows, sems):
+def choose_kernel(
+    picks_hbm, error, grad, momentum, params, payload, momentum_near, params_near, picks_smem, rows, sems
+):
     topk, block = payload.shape[1], error.shape[1]
+    staged = [
+        pltpu.make_async_copy(momentum, momentum_near, sems.at[2 * topk]),
+        pltpu.make_async_copy(params, params_near, sems.at[2 * topk + 1]),
+    ]
+    names_load = pltpu.make_async_copy(picks_hbm, picks_smem, sems.at[2 * topk + 2])
+    names_load.start()
+    for copy in staged:
+        copy.start()
+    names_load.wait()
+    picks = [picks_smem[0, at] for at in range(topk)]
     loads = []
     for at in range(topk):
         first = pl.multiple_of((picks[at] // 8) * 8, 8)
@@ -69,11 +81,7 @@
             loads.append(
                 pltpu.make_async_copy(array.at[pl.ds(first, 8)], rows.at[slot], sems.at[slot])
             )
-    staged = [
-        pltpu.make_async_copy(momentum, momentum_near, sems.at[2 * topk]),
-        pltpu.make_async_copy(params, params_near, sems.at[2 * topk + 1]),
-    ]
-    for copy in loads + staged:
+    for copy in loads:
         copy.start()
     row_of = lax.broadcasted_iota(jnp.int32, (8, block), 0)
     pick_row = lax.broadcasted_iota(jnp.int32, (topk, LANES), 0)
@@ -95,11 +103,12 @@
 
 def choose(picks, error, grad, momentum, params, replicas):
     blocks, block = params.shape
-    topk = picks.shape[0]
+    topk = picks.shape[1]
     vmem = pl.BlockSpec(memory_space=pltpu.VMEM)
     hbm = pl.BlockSpec(memory_space=pltpu.HBM)
-    error, grad, momentum, params = (
-        pltpu.with_memory_space_constraint(array, pltpu.HBM) for array in (error, grad, momentum, params)
+    picks, error, grad, momentum, params = (
+        pltpu.with_memory_space_constraint(array, pltpu.HBM)
+        for array in (picks, error, grad, momentum, params)
     )
     return pl.pallas_call(
         choose_kernel,
@@ -108,11 +117,12 @@
             jax.ShapeDtypeStruct((blocks, block), jnp.float32),
             jax.ShapeDtypeStruct((blocks, block), jnp.float32),
         ),
-        in_specs=[pl.BlockSpec(memory_space=pltpu.SMEM)] + [hbm] * 4,
+        in_specs=[hbm] * 5,
         out_specs=(vmem,) * 3,
         scratch_shapes=[
+            pltpu.SMEM((1, topk), jnp.int32),
             pltpu.VMEM((2 * topk, 8, block), jnp.float32),
-            pltpu.SemaphoreType.DMA((2 * topk + 2,)),
+            pltpu.SemaphoreType.DMA((2 * topk + 3,)),
         ],
         compiler_params=pltpu.CompilerParams(vmem_limit_bytes=VMEM_LIMIT),
         cost_estimate=pl.CostEstimate(flops=10**5, bytes_accessed=2 * 10**6, transcendentals=0),
@@ -174,19 +184,19 @@
         out, sems = refs[-2:]
         x, y, z, core = place_of_self()
         copies = []
-        for (_, first, count, offsets, other), slot in zip(pieces, slots):
+        for (_, first, count, place, offsets, other), slot in zip(pieces, slots):
             by = 1 - core if other else core
             dx, dy, dz = (one + (two - one) * by for one, two in zip(*offsets))
             x_there = (x + dx + NX) % NX
             colour = colour_of(x_there, y + dy + NY, z + dz + NZ)
             own = x_there // 2
             for at in range(count):
-                x_hi = 1 - own if at % 2 else own
+                x_hi = 1 - own if (place + at) % 2 else own
                 shift = SHIFTS[0] + (SHIFTS[1] - SHIFTS[0]) * x_hi
                 copies.append(
                     pltpu.make_async_copy(
                         sources[slot].at[first + at],
-                        out.at[x_hi * NZ + (colour + shift) % NZ, 1 - by if at >= 2 else by],
+                        out.at[x_hi * NZ + (colour + shift) % NZ, 1 - by if place + at >= 2 else by],
                         sems.at[len(copies)],
                     )
                 )
@@ -214,34 +224,38 @@
 HERE = ((0, 0, 0), (0, 0, 0))
 OPPOSITE = ((0, 1, -1), (0, -1, 1))
 NEIGHBOURS = (
-    ((1, 0, 0), (-1, 0, 0)),
     ((0, 1, 0), (0, -1, 0)),
     ((0, 0, 1), (0, 0, -1)),
+    ((1, 0, 0), (-1, 0, 0)),
 )
 
 
-def gather_slab(shard):
+def gather_slab(shard, aside):
     shape = (CLASSES, CORES, *shard.shape)
     half = jnp.stack([collect(shard, partner=False), collect(shard, partner=True)])
     opposite = fetch(half, OPPOSITE)
     portion = jnp.concatenate([half, swap(half)], axis=0)
-    arrived = [fetch(portion, offsets) for offsets in NEIGHBOURS]
-    whole = put(None, [(portion, 0, 4, HERE, False)], shape, shard.dtype)
-    opposite, *arrived, whole = lax.optimization_barrier((opposite, *arrived, whole))
+    near_y, near_z, near_x = (fetch(portion, offsets) for offsets in NEIGHBOURS)
+    whole = put(None, [(portion, 0, 4, 0, HERE, False)], shape, shard.dtype)
+    pieces = [(near_y, 0, 4, 0, NEIGHBOURS[0], False)]
+    pieces += [(swap(near_y[at : at + 2]), 0, 2, at, NEIGHBOURS[0], True) for at in (0, 2)]
+    whole = put(whole, pieces, shape, shard.dtype)
+    near_z, near_x, opposite, whole, aside = lax.optimization_barrier(
+        (near_z, near_x, opposite, whole, aside)
+    )
     batches = (
-        ((arrived[0], 4, NEIGHBOURS[0]), (arrived[1], 4, NEIGHBOURS[1])),
-        ((arrived[2], 4, NEIGHBOURS[2]), (opposite, 2, OPPOSITE)),
+        ((near_x, 4, NEIGHBOURS[2]), (opposite, 2, OPPOSITE)),
+        ((near_z, 4, NEIGHBOURS[1]),),
     )
     here, there = [], []
     for batch in batches:
         joined = jnp.concatenate([array for array, _, _ in batch], axis=0)
-        joined_there = swap(joined)
-        firsts = (0, batch[0][1])
-        here.append([(joined, at, n, off, False) for at, (_, n, off) in zip(firsts, batch)])
-        there.append([(joined_there, at, n, off, True) for at, (_, n, off) in zip(firsts, batch)])
-    for pieces in here + there:
+        for array, other, placed in ((joined, False, here), (swap(joined), True, there)):
+            firsts = (0, batch[0][1])
+            placed.append([(array, at, n, 0, off, other) for at, (_, n, off) in zip(firsts, batch)])
+    for pieces in (here[0] + here[1], *there):
         whole = put(whole, pieces, shape, shard.dtype)
-    return whole
+    return whole, aside
 
 
 def per_device(pseudo_grad, error_buf, momentum, params, picks):
@@ -249,14 +263,14 @@
     replicas = lax.axis_size("rep")
     own_picks = picks[0]
     payload, momentum_near, params_near = choose(
-        own_picks, error_buf[0], pseudo_grad[0], momentum, params, replicas
+        picks, error_buf[0], pseudo_grad[0], momentum, params, replicas
     )
     everyone = lax.all_to_all(payload, "rep", 0, 0).reshape(-1, payload.shape[-1])
     new_params, new_momentum, shard = update(everyone, momentum_near, params_near)
-    gathered = gather_slab(shard)
     accumulated = DECAY_RATE * error_buf[0] + pseudo_grad[0]
     chosen = jnp.any(own_picks[:, None] == lax.iota(jnp.int32, blocks)[None, :], axis=0)
     new_error = jnp.where(chosen[:, None], 0.0, accumulated)[None]
+    gathered, new_error = gather_slab(shard, new_error)
     return (new_params, new_momentum, new_error, gathered.reshape(-1, block))
 
 

time: 98 us -> 101 us (1.031)
  starting transfers between devices: 43.6 us -> 47.6 us
    ppermute x3 -> x5, starting transfers between devices: 10.7 us -> 16.9 us  [swap(): return lax.ppermute(value, AXES, pairs)]
    ppermute x4, starting transfers between devices: 18.9 us -> 16.6 us  [fetch(): return lax.ppermute(value, AXES, pairs)]
  transfers between devices with their start and end apart: 9 -> 11, of which waited for: 4 -> 4; matrix products, arithmetic and copies ran while one was open for 1% -> 1% of each run, Pallas kernels for 5% -> 5%
where the time goes in v8:
time: 101 us; the launch traced here: 100 us
  starting transfers between devices  47.6 us (47%)
  waiting for transfers between devices  23.2 us (23%)
  blocking collectives  17.7 us (18%)
  Pallas kernels  9.54 us (9%)
  other arithmetic  1.17 us (1%)
    all_to_all x1, blocking collectives, per_device(): lax.all_to_all(payload, 'rep', 0, 0).reshape(-1, payload.shape[-1])  17.7 us
    ppermute x5, starting transfers between devices, swap(): return lax.ppermute(value, AXES, pairs)  16.9 us
    ppermute x4, starting transfers between devices, fetch(): return lax.ppermute(value, AXES, pairs)  16.6 us
    ppermute x4, waiting for transfers between devices, fetch(): return lax.ppermute(value, AXES, pairs)  14.8 us
    ppermute x2, starting transfers between devices, collect(): return lax.ppermute(shard, AXES, pairs)  14.1 us
    ppermute x2, waiting for transfers between devices, collect(): return lax.ppermute(shard, AXES, pairs)  6.86 us
    pallas_call x5, Pallas kernels, put(): pl.pallas_call(kernel, out_shape=jax.ShapeDtypeStruct(shape, dtype), in_s...  6.32 us
  transfers between devices with their start and end apart: 11, of which 4 were waited for; matrix products, arithmetic and copies ran while one was open for 1% of the time, Pallas kernels for 5%

profile of v8, /device:TPU:1, one launch (start us, length us, event | category | flops | bytes accessed | tf_op | source)
XLA Modules:
  0.0 100.3 jit_solution(390977130785679534)
XLA Ops:
  0.6 1.8 %shard_map.84 = (f32[16,8,384]{2,1,0:T(8,128)S(1)}, f32[512,256]{1,0:T(8,128)S(1)}, f32[512,256]{1,0:T(8,128)S(1)}) custom-call(s32[1,8]{1,0:T(1,128)} %picks_hbm.1, f32[512,256]{1,0:T(8,128)} %bitcast.9, f32[512,256]{1,0:T(8,128)} %bitcast.10, f32[512,256]{1,0:T(8,128)} %momentum.1, f32[512,256]{1,0:T(8,128)} %params.1), custom_call_target="tpu_custom_call" | custom-call | flops 100000 | bytes 2000000 | tf_op jit(solution)/shard_map/pallas_call | solution.py:113
  2.5 17.7 %all_to_all.5 = f32[16,8,384]{2,1,0:T(8,128)S(1)} all-to-all(f32[16,8,384]{2,1,0:T(8,128)S(1)} %get-tuple-element.15), channel_id=1, replica_groups=mesh['rep'=16,'fsdp'=32] {'rep'}, dimensions={0} | all-to-all | bytes 393216 | tf_op jit(solution)/shard_map/all_to_all | solution.py:268
  20.2 1.4 %shard_map.85 = (f32[512,256]{1,0:T(8,128)}, f32[512,256]{1,0:T(8,128)}, bf16[512,256]{1,0:T(8,128)(2,1)S(1)}) custom-call(f32[128,384]{1,0:T(8,128)S(1)} %bitcast.7, f32[512,256]{1,0:T(8,128)S(1)} %get-tuple-element.16.momentum, f32[512,256]{1,0:T(8,128)S(1)} %get-tuple-element.17.params), custom_call_target="tpu_custom_call" | custom-call | flops 100000000 | bytes 4000000 | tf_op jit(solution)/shard_map/pallas_call | solution.py:160
  21.6 7.6 %collective-permute-start = (bf16[512,256]{1,0:T(8,128)(2,1)S(1)}, bf16[512,256]{1,0:T(8,128)(2,1)S(1)}, u32[]{:S(2)}, u32[]{:S(2)}) collective-permute-start(bf16[512,256]{1,0:T(8,128)(2,1)S(1)} %get-tuple-element.20), channel_id=1, source_target_pairs={{2,0},{3,1},{12,2},{13,3},{6,4},{7,5},{0,6},{1,7},{10,8},{11,9},{4... | collective-permute-start | bytes 786440 | tf_op jit(solution)/shard_map/ppermute | solution.py:49
  29.2 6.5 %collective-permute-start.1 = (bf16[512,256]{1,0:T(8,128)(2,1)S(1)}, bf16[512,256]{1,0:T(8,128)(2,1)S(1)}, u32[]{:S(2)}, u32[]{:S(2)}) collective-permute-start(bf16[512,256]{1,0:T(8,128)(2,1)S(1)} %get-tuple-element.20), channel_id=1, source_target_pairs={{54,0},{55,1},{48,2},{49,3},{58,4},{59,5},{52,6},{53,7},{62,8},{63... | collective-permute-start | bytes 786440 | tf_op jit(solution)/shard_map/ppermute | solution.py:49
  35.7 0.0 collective-permute-done
  35.7 6.9 %collective-permute-done.1 = bf16[512,256]{1,0:T(8,128)(2,1)S(1)} collective-permute-done((bf16[512,256]{1,0:T(8,128)(2,1)S(1)}, bf16[512,256]{1,0:T(8,128)(2,1)S(1)}, u32[]{:S(2)}, u32[]{:S(2)}) %collective-permute-start.1) | collective-permute-done | bytes 262176 | tf_op jit(solution)/shard_map/ppermute | solution.py:49
  42.6 0.1 pad_maximum_fusion.1
  42.6 6.2 %collective-permute-start.2 = (bf16[2,512,256]{2,1,0:T(8,128)(2,1)S(1)}, bf16[2,512,256]{2,1,0:T(8,128)(2,1)S(1)}, u32[]{:S(2)}, u32[]{:S(2)}) collective-permute-start(bf16[2,512,256]{2,1,0:T(8,128)(2,1)S(1)} %pad_maximum_fusion.1), channel_id=1, source_target_pairs={{1,0},{0,1},{3,2},{2,3},{5,4},{4,5},{7,6},{6,7},{9,8},{8,9},{11,10... | collective-permute-start | bytes 1572872 | tf_op jit(solution)/shard_map/ppermute | solution.py:40
  48.8 1.5 %collective-permute-done.2 = bf16[2,512,256]{2,1,0:T(8,128)(2,1)S(1)} collective-permute-done((bf16[2,512,256]{2,1,0:T(8,128)(2,1)S(1)}, bf16[2,512,256]{2,1,0:T(8,128)(2,1)S(1)}, u32[]{:S(2)}, u32[]{:S(2)}) %collective-permute-start.2) | collective-permute-done | bytes 524320 | tf_op jit(solution)/shard_map/ppermute | solution.py:40
  50.3 0.1 pad_maximum_fusion.refs_0_
  50.5 0.0 copy-start.2
  50.5 0.0 copy-start
  50.5 0.0 copy-start.1
  50.5 10.9 %collective-permute-start.6 = (bf16[4,512,256]{2,1,0:T(8,128)(2,1)S(1)}, bf16[4,512,256]{2,1,0:T(8,128)(2,1)S(1)}, u32[]{:S(2)}, u32[]{:S(2)}) collective-permute-start(bf16[4,512,256]{2,1,0:T(8,128)(2,1)S(1)} %pad_maximum_fusion.refs_0_), channel_id=1, source_target_pairs={{64,0},{449,1},{66,2},{451,3},{68,4},{453,5},{70,6},{455,7},{72,8}... | collective-permute-start | bytes 3145736 | tf_op jit(solution)/shard_map/ppermute | solution.py:35
  61.4 1.9 %collective-permute-start.3 = (bf16[4,512,256]{2,1,0:T(8,128)(2,1)S(1)}, bf16[4,512,256]{2,1,0:T(8,128)(2,1)S(1)}, u32[]{:S(2)}, u32[]{:S(2)}) collective-permute-start(bf16[4,512,256]{2,1,0:T(8,128)(2,1)S(1)} %pad_maximum_fusion.refs_0_), channel_id=1, source_target_pairs={{2,0},{15,1},{4,2},{1,3},{6,4},{3,5},{8,6},{5,7},{10,8},{7,9},{12,... | collective-permute-start | bytes 3145736 | tf_op jit(solution)/shard_map/ppermute | solution.py:35
  63.3 1.9 %collective-permute-start.4 = (bf16[4,512,256]{2,1,0:T(8,128)(2,1)S(1)}, bf16[4,512,256]{2,1,0:T(8,128)(2,1)S(1)}, u32[]{:S(2)}, u32[]{:S(2)}) collective-permute-start(bf16[4,512,256]{2,1,0:T(8,128)(2,1)S(1)} %pad_maximum_fusion.refs_0_), channel_id=1, source_target_pairs={{32,0},{49,1},{34,2},{51,3},{36,4},{53,5},{38,6},{55,7},{40,8},{57... | collective-permute-start | bytes 3145736 | tf_op jit(solution)/shard_map/ppermute | solution.py:35
  65.2 7.9 %collective-permute-done.6.refs_1_ = bf16[4,512,256]{2,1,0:T(8,128)(2,1)S(1)} collective-permute-done((bf16[4,512,256]{2,1,0:T(8,128)(2,1)S(1)}, bf16[4,512,256]{2,1,0:T(8,128)(2,1)S(1)}, u32[]{:S(2)}, u32[]{:S(2)}) %collective-permute-start.6) | collective-permute-done | bytes 1048608 | tf_op jit(solution)/shard_map/ppermute | solution.py:35
  73.1 0.1 fusion.1
  73.2 3.6 %collective-permute-start.7 = (bf16[2,512,256]{2,1,0:T(8,128)(2,1)S(1)}, bf16[2,512,256]{2,1,0:T(8,128)(2,1)S(1)}, u32[]{:S(2)}, u32[]{:S(2)}) collective-permute-start(bf16[2,512,256]{2,1,0:T(8,128)(2,1)S(1)} %get-tuple-element.27), channel_id=1, source_target_pairs={{1,0},{0,1},{3,2},{2,3},{5,4},{4,5},{7,6},{6,7},{9,8},{8,9},{11,10... | collective-permute-start | bytes 1572872 | tf_op jit(solution)/shard_map/ppermute | solution.py:40
  76.8 1.9 %collective-permute-start.8 = (bf16[2,512,256]{2,1,0:T(8,128)(2,1)S(1)}, bf16[2,512,256]{2,1,0:T(8,128)(2,1)S(1)}, u32[]{:S(2)}, u32[]{:S(2)}) collective-permute-start(bf16[2,512,256]{2,1,0:T(8,128)(2,1)S(1)} %get-tuple-element.26), channel_id=1, source_target_pairs={{1,0},{0,1},{3,2},{2,3},{5,4},{4,5},{7,6},{6,7},{9,8},{8,9},{11,10... | collective-permute-start | bytes 1572872 | tf_op jit(solution)/shard_map/ppermute | solution.py:40
  78.7 1.9 %collective-permute-start.5 = (bf16[2,512,256]{2,1,0:T(8,128)(2,1)S(1)}, bf16[2,512,256]{2,1,0:T(8,128)(2,1)S(1)}, u32[]{:S(2)}, u32[]{:S(2)}) collective-permute-start(bf16[2,512,256]{2,1,0:T(8,128)(2,1)S(1)} %pad_maximum_fusion.1), channel_id=1, source_target_pairs={{78,0},{451,1},{64,2},{453,3},{66,4},{455,5},{68,6},{457,7},{70,8}... | collective-permute-start | bytes 1572872 | tf_op jit(solution)/shard_map/ppermute | solution.py:35
  80.6 0.0 copy-done.2
  80.7 0.1 fusion
  80.7 0.0 copy-done
  80.7 0.0 copy-done.1
  80.7 0.9 add_select_fusion
  81.7 1.0 shard_map.86.refs_0_
  82.7 0.0 collective-permute-done.7.refs_2_
  82.7 0.0 collective-permute-done.8.refs_3_
  82.7 1.4 %shard_map.87.refs_0_ = bf16[16,2,512,256]{3,2,1,0:T(8,128)(2,1)} custom-call(bf16[16,2,512,256]{3,2,1,0:T(8,128)(2,1)} %shard_map.86.refs_0_, bf16[4,512,256]{2,1,0:T(8,128)(2,1)S(1)} %collective-permute-done.6.refs_1_, bf16[2,512,256]{2,1,0:T(8,128)(2,1)S(1)} %collective-permute-done.7.refs_2_, ...), custom_call_target="tpu_custom_call", output_to_operand_aliasing={{}: (0, {})} | custom-call | bytes 4194304 | tf_op jit(solution)/shard_map/pallas_call | solution.py:209
  84.1 6.9 %collective-permute-done.5 = bf16[2,512,256]{2,1,0:T(8,128)(2,1)S(1)} collective-permute-done((bf16[2,512,256]{2,1,0:T(8,128)(2,1)S(1)}, bf16[2,512,256]{2,1,0:T(8,128)(2,1)S(1)}, u32[]{:S(2)}, u32[]{:S(2)}) %collective-permute-start.5) | collective-permute-done | bytes 524320 | tf_op jit(solution)/shard_map/ppermute | solution.py:35
  91.0 0.0 collective-permute-done.3.refs_2_
  91.0 0.0 collective-permute-done.4
  91.1 0.1 constant_dynamic-update-slice_fusion.1
  91.2 3.3 %collective-permute-start.9 = (bf16[6,512,256]{2,1,0:T(8,128)(2,1)S(1)}, bf16[6,512,256]{2,1,0:T(8,128)(2,1)S(1)}, u32[]{:S(2)}, u32[]{:S(2)}) collective-permute-start(bf16[6,512,256]{2,1,0:T(8,128)(2,1)S(1)} %constant_dynamic-update-slice_fusion.refs_1_), channel_id=1, source_target_pairs={{1,0},{0,1},{3,2},{2,3},{5,4},{4,5},{7,6},{6,7},{9,8},{8,9},{11,10... | collective-permute-start | bytes 4718600 | tf_op jit(solution)/shard_map/ppermute | solution.py:40
  94.4 1.9 %collective-permute-start.10 = (bf16[4,512,256]{2,1,0:T(8,128)(2,1)S(1)}, bf16[4,512,256]{2,1,0:T(8,128)(2,1)S(1)}, u32[]{:S(2)}, u32[]{:S(2)}) collective-permute-start(bf16[4,512,256]{2,1,0:T(8,128)(2,1)S(1)} %collective-permute-done.3.refs_2_), channel_id=1, source_target_pairs={{1,0},{0,1},{3,2},{2,3},{5,4},{4,5},{7,6},{6,7},{9,8},{8,9},{11,10... | collective-permute-start | bytes 3145736 | tf_op jit(solution)/shard_map/ppermute | solution.py:40
  96.4 1.6 %shard_map.88.refs_0_ = bf16[16,2,512,256]{3,2,1,0:T(8,128)(2,1)} custom-call(bf16[16,2,512,256]{3,2,1,0:T(8,128)(2,1)} %shard_map.87.refs_0_, bf16[6,512,256]{2,1,0:T(8,128)(2,1)S(1)} %constant_dynamic-update-slice_fusion.refs_1_, bf16[4,512,256]{2,1,0:T(8,128)(2,1)S(1)} %collective-permute-done.3.refs_2_), custom_call_target="tpu_custom_call", output_to_operand_aliasing={{}: (0, {})} | custom-call | bytes 5242880 | tf_op jit(solution)/shard_map/pallas_call | solution.py:209
  98.0 0.0 collective-permute-done.9.refs_1_
  98.0 1.2 %shard_map.89.refs_0_ = bf16[16,2,512,256]{3,2,1,0:T(8,128)(2,1)} custom-call(bf16[16,2,512,256]{3,2,1,0:T(8,128)(2,1)} %shard_map.88.refs_0_, bf16[6,512,256]{2,1,0:T(8,128)(2,1)S(1)} %collective-permute-done.9.refs_1_), custom_call_target="tpu_custom_call", output_to_operand_aliasing={{}: (0, {})} | custom-call | bytes 3145728 | tf_op jit(solution)/shard_map/pallas_call | solution.py:209
  99.2 0.0 collective-permute-done.10.refs_1_
  99.3 1.0 %shard_map.90 = bf16[16,2,512,256]{3,2,1,0:T(8,128)(2,1)} custom-call(bf16[16,2,512,256]{3,2,1,0:T(8,128)(2,1)} %shard_map.89.refs_0_, bf16[4,512,256]{2,1,0:T(8,128)(2,1)S(1)} %collective-permute-done.10.refs_1_), custom_call_target="tpu_custom_call", output_to_operand_aliasing={{}: (0, {})} | custom-call | bytes 2097152 | tf_op jit(solution)/shard_map/pallas_call | solution.py:209
  (1 shorter events, 0.0 us)
Async XLA Ops:
  21.6 14.1 %collective-permute-start = (bf16[512,256]{1,0:T(8,128)(2,1)S(1)}, bf16[512,256]{1,0:T(8,128)(2,1)S(1)}, u32[]{:S(2)}, u32[]{:S(2)}) collective-permute-start(bf16[512,256]{1,0:T(8,128)(2,1)S(1)} %get-tuple-element.20), channel_id=1, source_target_pairs={{2,0},{3,1},{12,2},{13,3},{6,4},{7,5},{0,6},{1,7},{10,8},{11,9},{4... | collective-permute-start | bytes 786440 | tf_op jit(solution)/shard_map/ppermute | solution.py:49
  29.2 13.3 %collective-permute-start.1 = (bf16[512,256]{1,0:T(8,128)(2,1)S(1)}, bf16[512,256]{1,0:T(8,128)(2,1)S(1)}, u32[]{:S(2)}, u32[]{:S(2)}) collective-permute-start(bf16[512,256]{1,0:T(8,128)(2,1)S(1)} %get-tuple-element.20), channel_id=1, source_target_pairs={{54,0},{55,1},{48,2},{49,3},{58,4},{59,5},{52,6},{53,7},{62,8},{63... | collective-permute-start | bytes 786440 | tf_op jit(solution)/shard_map/ppermute | solution.py:49
  42.6 7.7 %collective-permute-start.2 = (bf16[2,512,256]{2,1,0:T(8,128)(2,1)S(1)}, bf16[2,512,256]{2,1,0:T(8,128)(2,1)S(1)}, u32[]{:S(2)}, u32[]{:S(2)}) collective-permute-start(bf16[2,512,256]{2,1,0:T(8,128)(2,1)S(1)} %pad_maximum_fusion.1), channel_id=1, source_target_pairs={{1,0},{0,1},{3,2},{2,3},{5,4},{4,5},{7,6},{6,7},{9,8},{8,9},{11,10... | collective-permute-start | bytes 1572872 | tf_op jit(solution)/shard_map/ppermute | solution.py:40
  50.5 30.2 %copy-start.2 = (s32[1,8]{1,0:T(1,128)S(1)}, s32[1,8]{1,0:T(1,128)}, u32[]{:S(2)}) copy-start(s32[1,8]{1,0:T(1,128)} %picks_hbm.1) | copy-start | bytes 100
  50.5 30.3 %copy-start = (f32[1,512,256]{2,1,0:T(8,128)S(1)}, f32[1,512,256]{2,1,0:T(8,128)}, u32[]{:S(2)}) copy-start(f32[1,512,256]{2,1,0:T(8,128)} %param.6) | copy-start | bytes 1572868
  50.5 30.3 %copy-start.1 = (f32[1,512,256]{2,1,0:T(8,128)S(1)}, f32[1,512,256]{2,1,0:T(8,128)}, u32[]{:S(2)}) copy-start(f32[1,512,256]{2,1,0:T(8,128)} %param.5) | copy-start | bytes 1572868
  50.5 22.6 %collective-permute-start.6 = (bf16[4,512,256]{2,1,0:T(8,128)(2,1)S(1)}, bf16[4,512,256]{2,1,0:T(8,128)(2,1)S(1)}, u32[]{:S(2)}, u32[]{:S(2)}) collective-permute-start(bf16[4,512,256]{2,1,0:T(8,128)(2,1)S(1)} %pad_maximum_fusion.refs_0_), channel_id=1, source_target_pairs={{64,0},{449,1},{66,2},{451,3},{68,4},{453,5},{70,6},{455,7},{72,8}... | collective-permute-start | bytes 3145736 | tf_op jit(solution)/shard_map/ppermute | solution.py:35
  61.4 29.7 %collective-permute-start.3 = (bf16[4,512,256]{2,1,0:T(8,128)(2,1)S(1)}, bf16[4,512,256]{2,1,0:T(8,128)(2,1)S(1)}, u32[]{:S(2)}, u32[]{:S(2)}) collective-permute-start(bf16[4,512,256]{2,1,0:T(8,128)(2,1)S(1)} %pad_maximum_fusion.refs_0_), channel_id=1, source_target_pairs={{2,0},{15,1},{4,2},{1,3},{6,4},{3,5},{8,6},{5,7},{10,8},{7,9},{12,... | collective-permute-start | bytes 3145736 | tf_op jit(solution)/shard_map/ppermute | solution.py:35
  63.3 27.7 %collective-permute-start.4 = (bf16[4,512,256]{2,1,0:T(8,128)(2,1)S(1)}, bf16[4,512,256]{2,1,0:T(8,128)(2,1)S(1)}, u32[]{:S(2)}, u32[]{:S(2)}) collective-permute-start(bf16[4,512,256]{2,1,0:T(8,128)(2,1)S(1)} %pad_maximum_fusion.refs_0_), channel_id=1, source_target_pairs={{32,0},{49,1},{34,2},{51,3},{36,4},{53,5},{38,6},{55,7},{40,8},{57... | collective-permute-start | bytes 3145736 | tf_op jit(solution)/shard_map/ppermute | solution.py:35
  73.2 9.5 %collective-permute-start.7 = (bf16[2,512,256]{2,1,0:T(8,128)(2,1)S(1)}, bf16[2,512,256]{2,1,0:T(8,128)(2,1)S(1)}, u32[]{:S(2)}, u32[]{:S(2)}) collective-permute-start(bf16[2,512,256]{2,1,0:T(8,128)(2,1)S(1)} %get-tuple-element.27), channel_id=1, source_target_pairs={{1,0},{0,1},{3,2},{2,3},{5,4},{4,5},{7,6},{6,7},{9,8},{8,9},{11,10... | collective-permute-start | bytes 1572872 | tf_op jit(solution)/shard_map/ppermute | solution.py:40
  76.8 5.9 %collective-permute-start.8 = (bf16[2,512,256]{2,1,0:T(8,128)(2,1)S(1)}, bf16[2,512,256]{2,1,0:T(8,128)(2,1)S(1)}, u32[]{:S(2)}, u32[]{:S(2)}) collective-permute-start(bf16[2,512,256]{2,1,0:T(8,128)(2,1)S(1)} %get-tuple-element.26), channel_id=1, source_target_pairs={{1,0},{0,1},{3,2},{2,3},{5,4},{4,5},{7,6},{6,7},{9,8},{8,9},{11,10... | collective-permute-start | bytes 1572872 | tf_op jit(solution)/shard_map/ppermute | solution.py:40
  78.7 12.3 %collective-permute-start.5 = (bf16[2,512,256]{2,1,0:T(8,128)(2,1)S(1)}, bf16[2,512,256]{2,1,0:T(8,128)(2,1)S(1)}, u32[]{:S(2)}, u32[]{:S(2)}) collective-permute-start(bf16[2,512,256]{2,1,0:T(8,128)(2,1)S(1)} %pad_maximum_fusion.1), channel_id=1, source_target_pairs={{78,0},{451,1},{64,2},{453,3},{66,4},{455,5},{68,6},{457,7},{70,8}... | collective-permute-start | bytes 1572872 | tf_op jit(solution)/shard_map/ppermute | solution.py:35
  91.2 6.8 %collective-permute-start.9 = (bf16[6,512,256]{2,1,0:T(8,128)(2,1)S(1)}, bf16[6,512,256]{2,1,0:T(8,128)(2,1)S(1)}, u32[]{:S(2)}, u32[]{:S(2)}) collective-permute-start(bf16[6,512,256]{2,1,0:T(8,128)(2,1)S(1)} %constant_dynamic-update-slice_fusion.refs_1_), channel_id=1, source_target_pairs={{1,0},{0,1},{3,2},{2,3},{5,4},{4,5},{7,6},{6,7},{9,8},{8,9},{11,10... | collective-permute-start | bytes 4718600 | tf_op jit(solution)/shard_map/ppermute | solution.py:40
  94.4 4.8 %collective-permute-start.10 = (bf16[4,512,256]{2,1,0:T(8,128)(2,1)S(1)}, bf16[4,512,256]{2,1,0:T(8,128)(2,1)S(1)}, u32[]{:S(2)}, u32[]{:S(2)}) collective-permute-start(bf16[4,512,256]{2,1,0:T(8,128)(2,1)S(1)} %collective-permute-done.3.refs_2_), channel_id=1, source_target_pairs={{1,0},{0,1},{3,2},{2,3},{5,4},{4,5},{7,6},{6,7},{9,8},{8,9},{11,10... | collective-permute-start | bytes 3145736 | tf_op jit(solution)/shard_map/ppermute | solution.py:40

commit v9 on v8

--- a/solution.py
+++ b/solution.py
@@ -237,23 +237,15 @@
     portion = jnp.concatenate([half, swap(half)], axis=0)
     near_y, near_z, near_x = (fetch(portion, offsets) for offsets in NEIGHBOURS)
     whole = put(None, [(portion, 0, 4, 0, HERE, False)], shape, shard.dtype)
-    pieces = [(near_y, 0, 4, 0, NEIGHBOURS[0], False)]
+    pieces = [(near_y, 0, 4, 0, NEIGHBOURS[0], False), (opposite, 0, 2, 0, OPPOSITE, False)]
     pieces += [(swap(near_y[at : at + 2]), 0, 2, at, NEIGHBOURS[0], True) for at in (0, 2)]
+    pieces += [(swap(opposite), 0, 2, 0, OPPOSITE, True)]
     whole = put(whole, pieces, shape, shard.dtype)
-    near_z, near_x, opposite, whole, aside = lax.optimization_barrier(
-        (near_z, near_x, opposite, whole, aside)
-    )
-    batches = (
-        ((near_x, 4, NEIGHBOURS[2]), (opposite, 2, OPPOSITE)),
-        ((near_z, 4, NEIGHBOURS[1]),),
-    )
-    here, there = [], []
-    for batch in batches:
-        joined = jnp.concatenate([array for array, _, _ in batch], axis=0)
-        for array, other, placed in ((joined, False, here), (swap(joined), True, there)):
-            firsts = (0, batch[0][1])
-            placed.append([(array, at, n, 0, off, other) for at, (_, n, off) in zip(firsts, batch)])
-    for pieces in (here[0] + here[1], *there):
+    near_z, near_x, whole, aside = lax.optimization_barrier((near_z, near_x, whole, aside))
+    batches = ((near_z, NEIGHBOURS[1]), (near_x, NEIGHBOURS[2]))
+    here = [(array, 0, 4, 0, offsets, False) for array, offsets in batches]
+    there = [(swap(array), 0, 4, 0, offsets, True) for array, offsets in batches]
+    for pieces in (here, there[:1], there[1:]):
         whole = put(whole, pieces, shape, shard.dtype)
     return whole, aside
 

time: 101 us -> 98.2 us (0.972)
  waiting for transfers between devices: 23.2 us -> 19 us
    ppermute x4, waiting for transfers between devices: 14.8 us -> 10.4 us  [fetch(): return lax.ppermute(value, AXES, pairs)]
    ppermute x4, starting transfers between devices: 16.6 us -> 17.7 us  [fetch(): return lax.ppermute(value, AXES, pairs)]
    ppermute x5 -> x6, starting transfers between devices: 16.9 us -> 16.8 us  [swap(): return lax.ppermute(value, AXES, pairs)]
  transfers between devices with their start and end apart: 11 -> 12, of which waited for: 4 -> 4; matrix products, arithmetic and copies ran while one was open for 1% -> 1% of each run, Pallas kernels for 5% -> 5%
where the time goes in v9:
time: 98.2 us; the launch traced here: 97 us
  starting transfers between devices  48.5 us (49%)
  waiting for transfers between devices  19 us (19%)
  blocking collectives  17.7 us (18%)
  Pallas kernels  9.61 us (10%)
  other arithmetic  1.17 us (1%)
    all_to_all x1, blocking collectives, per_device(): lax.all_to_all(payload, 'rep', 0, 0).reshape(-1, payload.shape[-1])  17.7 us
    ppermute x4, starting transfers between devices, fetch(): return lax.ppermute(value, AXES, pairs)  17.7 us
    ppermute x6, starting transfers between devices, swap(): return lax.ppermute(value, AXES, pairs)  16.8 us
    ppermute x2, starting transfers between devices, collect(): return lax.ppermute(shard, AXES, pairs)  14.1 us
    ppermute x4, waiting for transfers between devices, fetch(): return lax.ppermute(value, AXES, pairs)  10.4 us
    ppermute x2, waiting for transfers between devices, collect(): return lax.ppermute(shard, AXES, pairs)  6.86 us
    pallas_call x5, Pallas kernels, put(): pl.pallas_call(kernel, out_shape=jax.ShapeDtypeStruct(shape, dtype), in_s...  6.26 us
    pallas_call x1, Pallas kernels, choose(): pl.pallas_call(choose_kernel, out_shape=(jax.ShapeDtypeStruct((replicas,...  1.97 us
  transfers between devices with their start and end apart: 12, of which 4 were waited for; matrix products, arithmetic and copies ran while one was open for 1% of the time, Pallas kernels for 5%

profile of v9, /device:TPU:1, one launch (start us, length us, event | category | flops | bytes accessed | tf_op | source)
XLA Modules:
  0.0 97.0 jit_solution(13064048045376978063)
XLA Ops:
  0.6 0.0 copy-start
  0.6 0.0 copy-start.1
  0.7 0.0 copy-start.2
  0.7 2.0 %shard_map.84 = (f32[16,8,384]{2,1,0:T(8,128)S(1)}, f32[512,256]{1,0:T(8,128)S(1)}, f32[512,256]{1,0:T(8,128)S(1)}) custom-call(s32[1,8]{1,0:T(1,128)} %picks_hbm.1, f32[512,256]{1,0:T(8,128)} %bitcast.9, f32[512,256]{1,0:T(8,128)} %bitcast.10, f32[512,256]{1,0:T(8,128)} %momentum.1, f32[512,256]{1,0:T(8,128)} %params.1), custom_call_target="tpu_custom_call" | custom-call | flops 100000 | bytes 2000000 | tf_op jit(solution)/shard_map/pallas_call | solution.py:113
  2.6 17.7 %all_to_all.5 = f32[16,8,384]{2,1,0:T(8,128)S(1)} all-to-all(f32[16,8,384]{2,1,0:T(8,128)S(1)} %get-tuple-element.14), channel_id=1, replica_groups=mesh['rep'=16,'fsdp'=32] {'rep'}, dimensions={0} | all-to-all | bytes 393216 | tf_op jit(solution)/shard_map/all_to_all | solution.py:260
  20.4 1.4 %shard_map.85 = (f32[512,256]{1,0:T(8,128)}, f32[512,256]{1,0:T(8,128)}, bf16[512,256]{1,0:T(8,128)(2,1)S(1)}) custom-call(f32[128,384]{1,0:T(8,128)S(1)} %bitcast.7, f32[512,256]{1,0:T(8,128)S(1)} %get-tuple-element.15.momentum, f32[512,256]{1,0:T(8,128)S(1)} %get-tuple-element.16.params), custom_call_target="tpu_custom_call" | custom-call | flops 100000000 | bytes 4000000 | tf_op jit(solution)/shard_map/pallas_call | solution.py:160
  21.8 7.6 %collective-permute-start = (bf16[512,256]{1,0:T(8,128)(2,1)S(1)}, bf16[512,256]{1,0:T(8,128)(2,1)S(1)}, u32[]{:S(2)}, u32[]{:S(2)}) collective-permute-start(bf16[512,256]{1,0:T(8,128)(2,1)S(1)} %get-tuple-element.19), channel_id=1, source_target_pairs={{2,0},{3,1},{12,2},{13,3},{6,4},{7,5},{0,6},{1,7},{10,8},{11,9},{4... | collective-permute-start | bytes 786440 | tf_op jit(solution)/shard_map/ppermute | solution.py:49
  29.4 6.5 %collective-permute-start.1 = (bf16[512,256]{1,0:T(8,128)(2,1)S(1)}, bf16[512,256]{1,0:T(8,128)(2,1)S(1)}, u32[]{:S(2)}, u32[]{:S(2)}) collective-permute-start(bf16[512,256]{1,0:T(8,128)(2,1)S(1)} %get-tuple-element.19), channel_id=1, source_target_pairs={{54,0},{55,1},{48,2},{49,3},{58,4},{59,5},{52,6},{53,7},{62,8},{63... | collective-permute-start | bytes 786440 | tf_op jit(solution)/shard_map/ppermute | solution.py:49
  35.9 0.0 collective-permute-done
  35.9 6.9 %collective-permute-done.1 = bf16[512,256]{1,0:T(8,128)(2,1)S(1)} collective-permute-done((bf16[512,256]{1,0:T(8,128)(2,1)S(1)}, bf16[512,256]{1,0:T(8,128)(2,1)S(1)}, u32[]{:S(2)}, u32[]{:S(2)}) %collective-permute-start.1) | collective-permute-done | bytes 262176 | tf_op jit(solution)/shard_map/ppermute | solution.py:49
  42.7 0.1 pad_maximum_fusion.1
  42.8 6.2 %collective-permute-start.2 = (bf16[2,512,256]{2,1,0:T(8,128)(2,1)S(1)}, bf16[2,512,256]{2,1,0:T(8,128)(2,1)S(1)}, u32[]{:S(2)}, u32[]{:S(2)}) collective-permute-start(bf16[2,512,256]{2,1,0:T(8,128)(2,1)S(1)} %pad_maximum_fusion.1), channel_id=1, source_target_pairs={{1,0},{0,1},{3,2},{2,3},{5,4},{4,5},{7,6},{6,7},{9,8},{8,9},{11,10... | collective-permute-start | bytes 1572872 | tf_op jit(solution)/shard_map/ppermute | solution.py:40
  49.0 1.5 %collective-permute-done.2 = bf16[2,512,256]{2,1,0:T(8,128)(2,1)S(1)} collective-permute-done((bf16[2,512,256]{2,1,0:T(8,128)(2,1)S(1)}, bf16[2,512,256]{2,1,0:T(8,128)(2,1)S(1)}, u32[]{:S(2)}, u32[]{:S(2)}) %collective-permute-start.2) | collective-permute-done | bytes 524320 | tf_op jit(solution)/shard_map/ppermute | solution.py:40
  50.5 0.1 pad_maximum_fusion.refs_0_
  50.6 10.7 %collective-permute-start.5 = (bf16[4,512,256]{2,1,0:T(8,128)(2,1)S(1)}, bf16[4,512,256]{2,1,0:T(8,128)(2,1)S(1)}, u32[]{:S(2)}, u32[]{:S(2)}) collective-permute-start(bf16[4,512,256]{2,1,0:T(8,128)(2,1)S(1)} %pad_maximum_fusion.refs_0_), channel_id=1, source_target_pairs={{64,0},{449,1},{66,2},{451,3},{68,4},{453,5},{70,6},{455,7},{72,8}... | collective-permute-start | bytes 3145736 | tf_op jit(solution)/shard_map/ppermute | solution.py:35
  61.4 1.9 %collective-permute-start.6 = (bf16[2,512,256]{2,1,0:T(8,128)(2,1)S(1)}, bf16[2,512,256]{2,1,0:T(8,128)(2,1)S(1)}, u32[]{:S(2)}, u32[]{:S(2)}) collective-permute-start(bf16[2,512,256]{2,1,0:T(8,128)(2,1)S(1)} %pad_maximum_fusion.1), channel_id=1, source_target_pairs={{78,0},{451,1},{64,2},{453,3},{66,4},{455,5},{68,6},{457,7},{70,8}... | collective-permute-start | bytes 1572872 | tf_op jit(solution)/shard_map/ppermute | solution.py:35
  63.3 3.1 %collective-permute-start.3 = (bf16[4,512,256]{2,1,0:T(8,128)(2,1)S(1)}, bf16[4,512,256]{2,1,0:T(8,128)(2,1)S(1)}, u32[]{:S(2)}, u32[]{:S(2)}) collective-permute-start(bf16[4,512,256]{2,1,0:T(8,128)(2,1)S(1)} %pad_maximum_fusion.refs_0_), channel_id=1, source_target_pairs={{2,0},{15,1},{4,2},{1,3},{6,4},{3,5},{8,6},{5,7},{10,8},{7,9},{12,... | collective-permute-start | bytes 3145736 | tf_op jit(solution)/shard_map/ppermute | solution.py:35
  66.4 1.9 %collective-permute-start.4 = (bf16[4,512,256]{2,1,0:T(8,128)(2,1)S(1)}, bf16[4,512,256]{2,1,0:T(8,128)(2,1)S(1)}, u32[]{:S(2)}, u32[]{:S(2)}) collective-permute-start(bf16[4,512,256]{2,1,0:T(8,128)(2,1)S(1)} %pad_maximum_fusion.refs_0_), channel_id=1, source_target_pairs={{32,0},{49,1},{34,2},{51,3},{36,4},{53,5},{38,6},{55,7},{40,8},{57... | collective-permute-start | bytes 3145736 | tf_op jit(solution)/shard_map/ppermute | solution.py:35
  68.3 10.4 %collective-permute-done.6.refs_2_ = bf16[2,512,256]{2,1,0:T(8,128)(2,1)S(1)} collective-permute-done((bf16[2,512,256]{2,1,0:T(8,128)(2,1)S(1)}, bf16[2,512,256]{2,1,0:T(8,128)(2,1)S(1)}, u32[]{:S(2)}, u32[]{:S(2)}) %collective-permute-start.6) | collective-permute-done | bytes 524320 | tf_op jit(solution)/shard_map/ppermute | solution.py:35
  78.8 1.9 %collective-permute-start.9 = (bf16[2,512,256]{2,1,0:T(8,128)(2,1)S(1)}, bf16[2,512,256]{2,1,0:T(8,128)(2,1)S(1)}, u32[]{:S(2)}, u32[]{:S(2)}) collective-permute-start(bf16[2,512,256]{2,1,0:T(8,128)(2,1)S(1)} %collective-permute-done.6.refs_2_), channel_id=1, source_target_pairs={{1,0},{0,1},{3,2},{2,3},{5,4},{4,5},{7,6},{6,7},{9,8},{8,9},{11,10... | collective-permute-start | bytes 1572872 | tf_op jit(solution)/shard_map/ppermute | solution.py:40
  80.7 0.0 collective-permute-done.5.refs_1_
  80.7 0.1 fusion.1
  80.8 2.4 %collective-permute-start.7 = (bf16[2,512,256]{2,1,0:T(8,128)(2,1)S(1)}, bf16[2,512,256]{2,1,0:T(8,128)(2,1)S(1)}, u32[]{:S(2)}, u32[]{:S(2)}) collective-permute-start(bf16[2,512,256]{2,1,0:T(8,128)(2,1)S(1)} %get-tuple-element.25), channel_id=1, source_target_pairs={{1,0},{0,1},{3,2},{2,3},{5,4},{4,5},{7,6},{6,7},{9,8},{8,9},{11,10... | collective-permute-start | bytes 1572872 | tf_op jit(solution)/shard_map/ppermute | solution.py:40
  83.2 1.9 %collective-permute-start.8 = (bf16[2,512,256]{2,1,0:T(8,128)(2,1)S(1)}, bf16[2,512,256]{2,1,0:T(8,128)(2,1)S(1)}, u32[]{:S(2)}, u32[]{:S(2)}) collective-permute-start(bf16[2,512,256]{2,1,0:T(8,128)(2,1)S(1)} %get-tuple-element.24), channel_id=1, source_target_pairs={{1,0},{0,1},{3,2},{2,3},{5,4},{4,5},{7,6},{6,7},{9,8},{8,9},{11,10... | collective-permute-start | bytes 1572872 | tf_op jit(solution)/shard_map/ppermute | solution.py:40
  85.1 0.0 copy-done.2
  85.1 0.1 fusion
  85.2 0.0 copy-done
  85.2 0.0 copy-done.1
  85.2 0.9 add_select_fusion
  86.1 1.0 %shard_map.86.refs_0_ = bf16[16,2,512,256]{3,2,1,0:T(8,128)(2,1)} custom-call(bf16[4,512,256]{2,1,0:T(8,128)(2,1)S(1)} %pad_maximum_fusion.refs_0_), custom_call_target="tpu_custom_call" | custom-call | bytes 2097152 | tf_op jit(solution)/shard_map/pallas_call | solution.py:209
  87.1 0.0 collective-permute-done.9.refs_5_
  87.1 0.0 collective-permute-done.7.refs_3_
  87.2 0.0 collective-permute-done.8.refs_4_
  87.2 1.8 %shard_map.87.refs_0_ = bf16[16,2,512,256]{3,2,1,0:T(8,128)(2,1)} custom-call(bf16[16,2,512,256]{3,2,1,0:T(8,128)(2,1)} %shard_map.86.refs_0_, bf16[4,512,256]{2,1,0:T(8,128)(2,1)S(1)} %collective-permute-done.5.refs_1_, bf16[2,512,256]{2,1,0:T(8,128)(2,1)S(1)} %collective-permute-done.6.refs_2_, ...), custom_call_target="tpu_custom_call", output_to_operand_aliasing={{}: (0, {})} | custom-call | bytes 6291456 | tf_op jit(solution)/shard_map/pallas_call | solution.py:209
  89.0 0.0 collective-permute-done.3.refs_1_
  89.0 0.0 collective-permute-done.4.refs_2_
  89.0 2.4 %collective-permute-start.10 = (bf16[4,512,256]{2,1,0:T(8,128)(2,1)S(1)}, bf16[4,512,256]{2,1,0:T(8,128)(2,1)S(1)}, u32[]{:S(2)}, u32[]{:S(2)}) collective-permute-start(bf16[4,512,256]{2,1,0:T(8,128)(2,1)S(1)} %collective-permute-done.3.refs_1_), channel_id=1, source_target_pairs={{1,0},{0,1},{3,2},{2,3},{5,4},{4,5},{7,6},{6,7},{9,8},{8,9},{11,10... | collective-permute-start | bytes 3145736 | tf_op jit(solution)/shard_map/ppermute | solution.py:40
  91.4 1.9 %collective-permute-start.11 = (bf16[4,512,256]{2,1,0:T(8,128)(2,1)S(1)}, bf16[4,512,256]{2,1,0:T(8,128)(2,1)S(1)}, u32[]{:S(2)}, u32[]{:S(2)}) collective-permute-start(bf16[4,512,256]{2,1,0:T(8,128)(2,1)S(1)} %collective-permute-done.4.refs_2_), channel_id=1, source_target_pairs={{1,0},{0,1},{3,2},{2,3},{5,4},{4,5},{7,6},{6,7},{9,8},{8,9},{11,10... | collective-permute-start | bytes 3145736 | tf_op jit(solution)/shard_map/ppermute | solution.py:40
  93.3 1.4 %shard_map.88.refs_0_ = bf16[16,2,512,256]{3,2,1,0:T(8,128)(2,1)} custom-call(bf16[16,2,512,256]{3,2,1,0:T(8,128)(2,1)} %shard_map.87.refs_0_, bf16[4,512,256]{2,1,0:T(8,128)(2,1)S(1)} %collective-permute-done.3.refs_1_, bf16[4,512,256]{2,1,0:T(8,128)(2,1)S(1)} %collective-permute-done.4.refs_2_), custom_call_target="tpu_custom_call", output_to_operand_aliasing={{}: (0, {})} | custom-call | bytes 4194304 | tf_op jit(solution)/shard_map/pallas_call | solution.py:209
  94.8 0.0 collective-permute-done.10.refs_1_
  94.8 1.0 %shard_map.89.refs_0_ = bf16[16,2,512,256]{3,2,1,0:T(8,128)(2,1)} custom-call(bf16[16,2,512,256]{3,2,1,0:T(8,128)(2,1)} %shard_map.88.refs_0_, bf16[4,512,256]{2,1,0:T(8,128)(2,1)S(1)} %collective-permute-done.10.refs_1_), custom_call_target="tpu_custom_call", output_to_operand_aliasing={{}: (0, {})} | custom-call | bytes 2097152 | tf_op jit(solution)/shard_map/pallas_call | solution.py:209
  95.8 0.1 collective-permute-done.11.refs_1_
  96.0 1.0 %shard_map.90 = bf16[16,2,512,256]{3,2,1,0:T(8,128)(2,1)} custom-call(bf16[16,2,512,256]{3,2,1,0:T(8,128)(2,1)} %shard_map.89.refs_0_, bf16[4,512,256]{2,1,0:T(8,128)(2,1)S(1)} %collective-permute-done.11.refs_1_), custom_call_target="tpu_custom_call", output_to_operand_aliasing={{}: (0, {})} | custom-call | bytes 2097152 | tf_op jit(solution)/shard_map/pallas_call | solution.py:209
Async XLA Ops:
  0.6 84.6 %copy-start = (f32[1,512,256]{2,1,0:T(8,128)S(1)}, f32[1,512,256]{2,1,0:T(8,128)}, u32[]{:S(2)}) copy-start(f32[1,512,256]{2,1,0:T(8,128)} %param.6) | copy-start | bytes 1572868
  0.6 84.6 %copy-start.1 = (f32[1,512,256]{2,1,0:T(8,128)S(1)}, f32[1,512,256]{2,1,0:T(8,128)}, u32[]{:S(2)}) copy-start(f32[1,512,256]{2,1,0:T(8,128)} %param.5) | copy-start | bytes 1572868
  0.7 84.5 %copy-start.2 = (s32[1,8]{1,0:T(1,128)S(1)}, s32[1,8]{1,0:T(1,128)}, u32[]{:S(2)}) copy-start(s32[1,8]{1,0:T(1,128)} %picks_hbm.1) | copy-start | bytes 100
  21.8 14.1 %collective-permute-start = (bf16[512,256]{1,0:T(8,128)(2,1)S(1)}, bf16[512,256]{1,0:T(8,128)(2,1)S(1)}, u32[]{:S(2)}, u32[]{:S(2)}) collective-permute-start(bf16[512,256]{1,0:T(8,128)(2,1)S(1)} %get-tuple-element.19), channel_id=1, source_target_pairs={{2,0},{3,1},{12,2},{13,3},{6,4},{7,5},{0,6},{1,7},{10,8},{11,9},{4... | collective-permute-start | bytes 786440 | tf_op jit(solution)/shard_map/ppermute | solution.py:49
  29.4 13.3 %collective-permute-start.1 = (bf16[512,256]{1,0:T(8,128)(2,1)S(1)}, bf16[512,256]{1,0:T(8,128)(2,1)S(1)}, u32[]{:S(2)}, u32[]{:S(2)}) collective-permute-start(bf16[512,256]{1,0:T(8,128)(2,1)S(1)} %get-tuple-element.19), channel_id=1, source_target_pairs={{54,0},{55,1},{48,2},{49,3},{58,4},{59,5},{52,6},{53,7},{62,8},{63... | collective-permute-start | bytes 786440 | tf_op jit(solution)/shard_map/ppermute | solution.py:49
  42.8 7.7 %collective-permute-start.2 = (bf16[2,512,256]{2,1,0:T(8,128)(2,1)S(1)}, bf16[2,512,256]{2,1,0:T(8,128)(2,1)S(1)}, u32[]{:S(2)}, u32[]{:S(2)}) collective-permute-start(bf16[2,512,256]{2,1,0:T(8,128)(2,1)S(1)} %pad_maximum_fusion.1), channel_id=1, source_target_pairs={{1,0},{0,1},{3,2},{2,3},{5,4},{4,5},{7,6},{6,7},{9,8},{8,9},{11,10... | collective-permute-start | bytes 1572872 | tf_op jit(solution)/shard_map/ppermute | solution.py:40
  50.6 30.1 %collective-permute-start.5 = (bf16[4,512,256]{2,1,0:T(8,128)(2,1)S(1)}, bf16[4,512,256]{2,1,0:T(8,128)(2,1)S(1)}, u32[]{:S(2)}, u32[]{:S(2)}) collective-permute-start(bf16[4,512,256]{2,1,0:T(8,128)(2,1)S(1)} %pad_maximum_fusion.refs_0_), channel_id=1, source_target_pairs={{64,0},{449,1},{66,2},{451,3},{68,4},{453,5},{70,6},{455,7},{72,8}... | collective-permute-start | bytes 3145736 | tf_op jit(solution)/shard_map/ppermute | solution.py:35
  61.4 17.4 %collective-permute-start.6 = (bf16[2,512,256]{2,1,0:T(8,128)(2,1)S(1)}, bf16[2,512,256]{2,1,0:T(8,128)(2,1)S(1)}, u32[]{:S(2)}, u32[]{:S(2)}) collective-permute-start(bf16[2,512,256]{2,1,0:T(8,128)(2,1)S(1)} %pad_maximum_fusion.1), channel_id=1, source_target_pairs={{78,0},{451,1},{64,2},{453,3},{66,4},{455,5},{68,6},{457,7},{70,8}... | collective-permute-start | bytes 1572872 | tf_op jit(solution)/shard_map/ppermute | solution.py:35
  63.3 25.7 %collective-permute-start.3 = (bf16[4,512,256]{2,1,0:T(8,128)(2,1)S(1)}, bf16[4,512,256]{2,1,0:T(8,128)(2,1)S(1)}, u32[]{:S(2)}, u32[]{:S(2)}) collective-permute-start(bf16[4,512,256]{2,1,0:T(8,128)(2,1)S(1)} %pad_maximum_fusion.refs_0_), channel_id=1, source_target_pairs={{2,0},{15,1},{4,2},{1,3},{6,4},{3,5},{8,6},{5,7},{10,8},{7,9},{12,... | collective-permute-start | bytes 3145736 | tf_op jit(solution)/shard_map/ppermute | solution.py:35
  66.4 22.6 %collective-permute-start.4 = (bf16[4,512,256]{2,1,0:T(8,128)(2,1)S(1)}, bf16[4,512,256]{2,1,0:T(8,128)(2,1)S(1)}, u32[]{:S(2)}, u32[]{:S(2)}) collective-permute-start(bf16[4,512,256]{2,1,0:T(8,128)(2,1)S(1)} %pad_maximum_fusion.refs_0_), channel_id=1, source_target_pairs={{32,0},{49,1},{34,2},{51,3},{36,4},{53,5},{38,6},{55,7},{40,8},{57... | collective-permute-start | bytes 3145736 | tf_op jit(solution)/shard_map/ppermute | solution.py:35
  78.8 8.4 %collective-permute-start.9 = (bf16[2,512,256]{2,1,0:T(8,128)(2,1)S(1)}, bf16[2,512,256]{2,1,0:T(8,128)(2,1)S(1)}, u32[]{:S(2)}, u32[]{:S(2)}) collective-permute-start(bf16[2,512,256]{2,1,0:T(8,128)(2,1)S(1)} %collective-permute-done.6.refs_2_), channel_id=1, source_target_pairs={{1,0},{0,1},{3,2},{2,3},{5,4},{4,5},{7,6},{6,7},{9,8},{8,9},{11,10... | collective-permute-start | bytes 1572872 | tf_op jit(solution)/shard_map/ppermute | solution.py:40
  80.8 6.4 %collective-permute-start.7 = (bf16[2,512,256]{2,1,0:T(8,128)(2,1)S(1)}, bf16[2,512,256]{2,1,0:T(8,128)(2,1)S(1)}, u32[]{:S(2)}, u32[]{:S(2)}) collective-permute-start(bf16[2,512,256]{2,1,0:T(8,128)(2,1)S(1)} %get-tuple-element.25), channel_id=1, source_target_pairs={{1,0},{0,1},{3,2},{2,3},{5,4},{4,5},{7,6},{6,7},{9,8},{8,9},{11,10... | collective-permute-start | bytes 1572872 | tf_op jit(solution)/shard_map/ppermute | solution.py:40
  83.2 4.0 %collective-permute-start.8 = (bf16[2,512,256]{2,1,0:T(8,128)(2,1)S(1)}, bf16[2,512,256]{2,1,0:T(8,128)(2,1)S(1)}, u32[]{:S(2)}, u32[]{:S(2)}) collective-permute-start(bf16[2,512,256]{2,1,0:T(8,128)(2,1)S(1)} %get-tuple-element.24), channel_id=1, source_target_pairs={{1,0},{0,1},{3,2},{2,3},{5,4},{4,5},{7,6},{6,7},{9,8},{8,9},{11,10... | collective-permute-start | bytes 1572872 | tf_op jit(solution)/shard_map/ppermute | solution.py:40
  89.0 5.8 %collective-permute-start.10 = (bf16[4,512,256]{2,1,0:T(8,128)(2,1)S(1)}, bf16[4,512,256]{2,1,0:T(8,128)(2,1)S(1)}, u32[]{:S(2)}, u32[]{:S(2)}) collective-permute-start(bf16[4,512,256]{2,1,0:T(8,128)(2,1)S(1)} %collective-permute-done.3.refs_1_), channel_id=1, source_target_pairs={{1,0},{0,1},{3,2},{2,3},{5,4},{4,5},{7,6},{6,7},{9,8},{8,9},{11,10... | collective-permute-start | bytes 3145736 | tf_op jit(solution)/shard_map/ppermute | solution.py:40
  91.4 4.6 %collective-permute-start.11 = (bf16[4,512,256]{2,1,0:T(8,128)(2,1)S(1)}, bf16[4,512,256]{2,1,0:T(8,128)(2,1)S(1)}, u32[]{:S(2)}, u32[]{:S(2)}) collective-permute-start(bf16[4,512,256]{2,1,0:T(8,128)(2,1)S(1)} %collective-permute-done.4.refs_2_), channel_id=1, source_target_pairs={{1,0},{0,1},{3,2},{2,3},{5,4},{4,5},{7,6},{6,7},{9,8},{8,9},{11,10... | collective-permute-start | bytes 3145736 | tf_op jit(solution)/shard_map/ppermute | solution.py:40

commit v10 on v9

--- a/solution.py
+++ b/solution.py
@@ -222,30 +222,36 @@
 
 
 HERE = ((0, 0, 0), (0, 0, 0))
-OPPOSITE = ((0, 1, -1), (0, -1, 1))
-NEIGHBOURS = (
-    ((0, 1, 0), (0, -1, 0)),
-    ((0, 0, 1), (0, 0, -1)),
-    ((1, 0, 0), (-1, 0, 0)),
-)
+X = ((1, 0, 0), (-1, 0, 0))
+XX = ((2, 0, 0), (-2, 0, 0))
+Y = ((0, 1, 0), (0, -1, 0))
+Z = ((0, 0, 1), (0, 0, -1))
 
 
 def gather_slab(shard, aside):
     shape = (CLASSES, CORES, *shard.shape)
-    half = jnp.stack([collect(shard, partner=False), collect(shard, partner=True)])
-    opposite = fetch(half, OPPOSITE)
+    own, partners = collect(shard, partner=False), collect(shard, partner=True)
+    own, partners, aside = lax.optimization_barrier((own, partners, aside))
+    half = jnp.stack([own, partners])
+    near_x = fetch(half, X)
     portion = jnp.concatenate([half, swap(half)], axis=0)
-    near_y, near_z, near_x = (fetch(portion, offsets) for offsets in NEIGHBOURS)
+    near_y, near_z = fetch(portion, Y), fetch(portion, Z)
+    far_x = fetch(jnp.concatenate(lax.optimization_barrier((portion[2:], near_x)), axis=0), X)
     whole = put(None, [(portion, 0, 4, 0, HERE, False)], shape, shard.dtype)
-    pieces = [(near_y, 0, 4, 0, NEIGHBOURS[0], False), (opposite, 0, 2, 0, OPPOSITE, False)]
-    pieces += [(swap(near_y[at : at + 2]), 0, 2, at, NEIGHBOURS[0], True) for at in (0, 2)]
-    pieces += [(swap(opposite), 0, 2, 0, OPPOSITE, True)]
+    pieces = [(near_x, 0, 2, 0, X, False)]
+    for array, offsets in ((near_y, Y), (near_z, Z)):
+        pieces += [(array, 0, 4, 0, offsets, False), (swap(array[:2]), 0, 2, 0, offsets, True)]
     whole = put(whole, pieces, shape, shard.dtype)
-    near_z, near_x, whole, aside = lax.optimization_barrier((near_z, near_x, whole, aside))
-    batches = ((near_z, NEIGHBOURS[1]), (near_x, NEIGHBOURS[2]))
-    here = [(array, 0, 4, 0, offsets, False) for array, offsets in batches]
-    there = [(swap(array), 0, 4, 0, offsets, True) for array, offsets in batches]
-    for pieces in (here, there[:1], there[1:]):
+    near_x, near_y, near_z, far_x, whole = lax.optimization_barrier(
+        (near_x, near_y, near_z, far_x, whole)
+    )
+    rest = swap(jnp.concatenate([near_x, near_y[2:], near_z[2:]], axis=0))
+    far_there = swap(far_x)
+    for pieces in (
+        [(far_x, 0, 2, 2, X, False), (far_x, 2, 2, 0, XX, False)],
+        [(rest, 0, 2, 0, X, True), (rest, 2, 2, 2, Y, True), (rest, 4, 2, 2, Z, True)],
+        [(far_there, 0, 2, 2, X, True), (far_there, 2, 2, 0, XX, True)],
+    ):
         whole = put(whole, pieces, shape, shard.dtype)
     return whole, aside
 

time: 98.2 us -> 93.9 us (0.956)
  blocking collectives: 17.7 us -> 0 us
  starting transfers between devices: 48.5 us -> 56.3 us
  waiting for transfers between devices: 19 us -> 24.3 us
    all_to_all x1 -> x0, blocking collectives: 17.7 us -> none  [per_device(): lax.all_to_all(payload, 'rep', 0, 0).reshape(-1, payload.shape[-1])]
    all_to_all x0 -> x1, waiting for transfers between devices: none -> 9.05 us  [per_device(): lax.all_to_all(payload, 'rep', 0, 0).reshape(-1, payload.shape[-1])]
    all_to_all x0 -> x1, starting transfers between devices: none -> 8.69 us  [per_device(): lax.all_to_all(payload, 'rep', 0, 0).reshape(-1, payload.shape[-1])]
    ppermute x4, waiting for transfers between devices: 10.4 us -> 8.31 us  [fetch(): return lax.ppermute(value, AXES, pairs)]
    ppermute x6 -> x5, starting transfers between devices: 16.8 us -> 15.7 us  [swap(): return lax.ppermute(value, AXES, pairs)]
  transfers between devices with their start and end apart: 12 -> 12, of which waited for: 4 -> 6; matrix products, arithmetic and copies ran while one was open for 1% -> 1% of each run, Pallas kernels for 5% -> 6%
where the time goes in v10:
time: 93.9 us; the launch traced here: 93.3 us
  starting transfers between devices  56.3 us (60%)
  waiting for transfers between devices  24.3 us (26%)
  Pallas kernels  10.3 us (11%)
  other arithmetic  1.44 us (2%)
    ppermute x4, starting transfers between devices, fetch(): return lax.ppermute(value, AXES, pairs)  17.7 us
    ppermute x5, starting transfers between devices, swap(): return lax.ppermute(value, AXES, pairs)  15.7 us
    ppermute x2, starting transfers between devices, collect(): return lax.ppermute(shard, AXES, pairs)  14.2 us
    all_to_all x1, waiting for transfers between devices, per_device(): lax.all_to_all(payload, 'rep', 0, 0).reshape(-1, payload.shape[-1])  9.05 us
    all_to_all x1, starting transfers between devices, per_device(): lax.all_to_all(payload, 'rep', 0, 0).reshape(-1, payload.shape[-1])  8.69 us
    ppermute x4, waiting for transfers between devices, fetch(): return lax.ppermute(value, AXES, pairs)  8.31 us
    pallas_call x5, Pallas kernels, put(): pl.pallas_call(kernel, out_shape=jax.ShapeDtypeStruct(shape, dtype), in_s...  6.26 us
    ppermute x2, waiting for transfers between devices, collect(): return lax.ppermute(shard, AXES, pairs)  5.93 us
  transfers between devices with their start and end apart: 12, of which 6 were waited for; matrix products, arithmetic and copies ran while one was open for 1% of the time, Pallas kernels for 6%

profile of v10, /device:TPU:1, one launch (start us, length us, event | category | flops | bytes accessed | tf_op | source)
XLA Modules:
  0.0 93.3 jit_solution(18129346449649166434)
XLA Ops:
  0.6 0.0 copy-start.2
  0.6 0.0 copy-start
  0.7 0.0 copy-start.1
  0.7 2.6 %shard_map.84 = (f32[16,8,384]{2,1,0:T(8,128)}, f32[512,256]{1,0:T(8,128)S(1)}, f32[512,256]{1,0:T(8,128)S(1)}) custom-call(s32[1,8]{1,0:T(1,128)} %picks_hbm.1, f32[512,256]{1,0:T(8,128)} %bitcast.9, f32[512,256]{1,0:T(8,128)} %bitcast.10, f32[512,256]{1,0:T(8,128)} %momentum.1, f32[512,256]{1,0:T(8,128)} %params.1), custom_call_target="tpu_custom_call" | custom-call | flops 100000 | bytes 2000000 | tf_op jit(solution)/shard_map/pallas_call | solution.py:113
  3.3 8.7 %all-to-all-start = ((f32[16,8,384]{2,1,0:T(8,128)}), f32[16,8,384]{2,1,0:T(8,128)S(1)}, u32[]{:S(2)}, u32[]{:S(2)}) async-start(f32[16,8,384]{2,1,0:T(8,128)} %get-tuple-element.20), calls=%async_computation | async-start | bytes 393216 | tf_op jit(solution)/shard_map/all_to_all | solution.py:266
  12.0 0.0 copy-done.2
  12.0 0.1 fusion
  12.1 9.1 %all-to-all-done = f32[16,8,384]{2,1,0:T(8,128)S(1)} async-done(((f32[16,8,384]{2,1,0:T(8,128)}), f32[16,8,384]{2,1,0:T(8,128)S(1)}, u32[]{:S(2)}, u32[]{:S(2)}) %all-to-all-start) | async-done | bytes 196640 | tf_op jit(solution)/shard_map/all_to_all | solution.py:266
  21.2 1.4 %shard_map.85 = (f32[512,256]{1,0:T(8,128)}, f32[512,256]{1,0:T(8,128)}, bf16[512,256]{1,0:T(8,128)(2,1)S(1)}) custom-call(f32[128,384]{1,0:T(8,128)S(1)} %bitcast.7, f32[512,256]{1,0:T(8,128)S(1)} %get-tuple-element.21.momentum, f32[512,256]{1,0:T(8,128)S(1)} %get-tuple-element.22.params), custom_call_target="tpu_custom_call" | custom-call | flops 100000000 | bytes 4000000 | tf_op jit(solution)/shard_map/pallas_call | solution.py:160
  22.6 7.7 %collective-permute-start = (bf16[512,256]{1,0:T(8,128)(2,1)S(1)}, bf16[512,256]{1,0:T(8,128)(2,1)S(1)}, u32[]{:S(2)}, u32[]{:S(2)}) collective-permute-start(bf16[512,256]{1,0:T(8,128)(2,1)S(1)} %get-tuple-element.25), channel_id=1, source_target_pairs={{2,0},{3,1},{12,2},{13,3},{6,4},{7,5},{0,6},{1,7},{10,8},{11,9},{4... | collective-permute-start | bytes 786440 | tf_op jit(solution)/shard_map/ppermute | solution.py:49
  30.3 6.5 %collective-permute-start.1 = (bf16[512,256]{1,0:T(8,128)(2,1)S(1)}, bf16[512,256]{1,0:T(8,128)(2,1)S(1)}, u32[]{:S(2)}, u32[]{:S(2)}) collective-permute-start(bf16[512,256]{1,0:T(8,128)(2,1)S(1)} %get-tuple-element.25), channel_id=1, source_target_pairs={{54,0},{55,1},{48,2},{49,3},{58,4},{59,5},{52,6},{53,7},{62,8},{63... | collective-permute-start | bytes 786440 | tf_op jit(solution)/shard_map/ppermute | solution.py:49
  36.8 0.0 copy-done
  36.8 0.0 copy-done.1
  36.8 0.9 add_select_fusion
  37.7 0.0 collective-permute-done
  37.7 5.9 %collective-permute-done.1 = bf16[512,256]{1,0:T(8,128)(2,1)S(1)} collective-permute-done((bf16[512,256]{1,0:T(8,128)(2,1)S(1)}, bf16[512,256]{1,0:T(8,128)(2,1)S(1)}, u32[]{:S(2)}, u32[]{:S(2)}) %collective-permute-start.1) | collective-permute-done | bytes 262176 | tf_op jit(solution)/shard_map/ppermute | solution.py:49
  43.6 0.1 pad_maximum_fusion.3
  43.7 6.2 %collective-permute-start.3 = (bf16[2,512,256]{2,1,0:T(8,128)(2,1)S(1)}, bf16[2,512,256]{2,1,0:T(8,128)(2,1)S(1)}, u32[]{:S(2)}, u32[]{:S(2)}) collective-permute-start(bf16[2,512,256]{2,1,0:T(8,128)(2,1)S(1)} %pad_maximum_fusion.3), channel_id=1, source_target_pairs={{1,0},{0,1},{3,2},{2,3},{5,4},{4,5},{7,6},{6,7},{9,8},{8,9},{11,10... | collective-permute-start | bytes 1572872 | tf_op jit(solution)/shard_map/ppermute | solution.py:40
  49.9 4.0 %collective-permute-start.2 = (bf16[2,512,256]{2,1,0:T(8,128)(2,1)S(1)}, bf16[2,512,256]{2,1,0:T(8,128)(2,1)S(1)}, u32[]{:S(2)}, u32[]{:S(2)}) collective-permute-start(bf16[2,512,256]{2,1,0:T(8,128)(2,1)S(1)} %pad_maximum_fusion.3), channel_id=1, source_target_pairs={{32,0},{49,1},{34,2},{51,3},{36,4},{53,5},{38,6},{55,7},{40,8},{57... | collective-permute-start | bytes 1572872 | tf_op jit(solution)/shard_map/ppermute | solution.py:35
  53.9 0.0 collective-permute-done.3
  53.9 0.1 pad_maximum_fusion.1.refs_0_
  54.0 8.7 %collective-permute-start.4 = (bf16[4,512,256]{2,1,0:T(8,128)(2,1)S(1)}, bf16[4,512,256]{2,1,0:T(8,128)(2,1)S(1)}, u32[]{:S(2)}, u32[]{:S(2)}) collective-permute-start(bf16[4,512,256]{2,1,0:T(8,128)(2,1)S(1)} %pad_maximum_fusion.1.refs_0_), channel_id=1, source_target_pairs={{64,0},{449,1},{66,2},{451,3},{68,4},{453,5},{70,6},{455,7},{72,8}... | collective-permute-start | bytes 3145736 | tf_op jit(solution)/shard_map/ppermute | solution.py:35
  62.7 1.9 %collective-permute-start.5 = (bf16[4,512,256]{2,1,0:T(8,128)(2,1)S(1)}, bf16[4,512,256]{2,1,0:T(8,128)(2,1)S(1)}, u32[]{:S(2)}, u32[]{:S(2)}) collective-permute-start(bf16[4,512,256]{2,1,0:T(8,128)(2,1)S(1)} %pad_maximum_fusion.1.refs_0_), channel_id=1, source_target_pairs={{2,0},{15,1},{4,2},{1,3},{6,4},{3,5},{8,6},{5,7},{10,8},{7,9},{12,... | collective-permute-start | bytes 3145736 | tf_op jit(solution)/shard_map/ppermute | solution.py:35
  64.6 0.0 collective-permute-done.2.refs_1_
  64.6 0.1 pad_maximum_fusion.2
  64.7 3.1 %collective-permute-start.6 = (bf16[4,512,256]{2,1,0:T(8,128)(2,1)S(1)}, bf16[4,512,256]{2,1,0:T(8,128)(2,1)S(1)}, u32[]{:S(2)}, u32[]{:S(2)}) collective-permute-start(bf16[4,512,256]{2,1,0:T(8,128)(2,1)S(1)} %pad_maximum_fusion.2), channel_id=1, source_target_pairs={{32,0},{49,1},{34,2},{51,3},{36,4},{53,5},{38,6},{55,7},{40,8},{57... | collective-permute-start | bytes 3145736 | tf_op jit(solution)/shard_map/ppermute | solution.py:35
  67.9 6.6 %collective-permute-done.4.refs_2_ = bf16[4,512,256]{2,1,0:T(8,128)(2,1)S(1)} collective-permute-done((bf16[4,512,256]{2,1,0:T(8,128)(2,1)S(1)}, bf16[4,512,256]{2,1,0:T(8,128)(2,1)S(1)}, u32[]{:S(2)}, u32[]{:S(2)}) %collective-permute-start.4) | collective-permute-done | bytes 1048608 | tf_op jit(solution)/shard_map/ppermute | solution.py:35
  74.5 3.2 %collective-permute-start.7 = (bf16[2,512,256]{2,1,0:T(8,128)(2,1)S(1)}, bf16[2,512,256]{2,1,0:T(8,128)(2,1)S(1)}, u32[]{:S(2)}, u32[]{:S(2)}) collective-permute-start(bf16[2,512,256]{2,1,0:T(8,128)(2,1)S(1)} %slice.16), channel_id=1, source_target_pairs={{1,0},{0,1},{3,2},{2,3},{5,4},{4,5},{7,6},{6,7},{9,8},{8,9},{11,10... | collective-permute-start | bytes 1572872 | tf_op jit(solution)/shard_map/ppermute | solution.py:40
  77.7 1.7 %collective-permute-done.5.refs_4_ = bf16[4,512,256]{2,1,0:T(8,128)(2,1)S(1)} collective-permute-done((bf16[4,512,256]{2,1,0:T(8,128)(2,1)S(1)}, bf16[4,512,256]{2,1,0:T(8,128)(2,1)S(1)}, u32[]{:S(2)}, u32[]{:S(2)}) %collective-permute-start.5) | collective-permute-done | bytes 1048608 | tf_op jit(solution)/shard_map/ppermute | solution.py:35
  79.5 1.9 %collective-permute-start.8 = (bf16[2,512,256]{2,1,0:T(8,128)(2,1)S(1)}, bf16[2,512,256]{2,1,0:T(8,128)(2,1)S(1)}, u32[]{:S(2)}, u32[]{:S(2)}) collective-permute-start(bf16[2,512,256]{2,1,0:T(8,128)(2,1)S(1)} %slice.17), channel_id=1, source_target_pairs={{1,0},{0,1},{3,2},{2,3},{5,4},{4,5},{7,6},{6,7},{9,8},{8,9},{11,10... | collective-permute-start | bytes 1572872 | tf_op jit(solution)/shard_map/ppermute | solution.py:40
  81.4 1.0 %shard_map.86.refs_0_ = bf16[16,2,512,256]{3,2,1,0:T(8,128)(2,1)} custom-call(bf16[4,512,256]{2,1,0:T(8,128)(2,1)S(1)} %pad_maximum_fusion.1.refs_0_), custom_call_target="tpu_custom_call" | custom-call | bytes 2097152 | tf_op jit(solution)/shard_map/pallas_call | solution.py:209
  82.5 0.0 collective-permute-done.7.refs_3_
  82.5 0.8 collective-permute-done.8.refs_5_
  83.3 1.9 %shard_map.87.refs_0_ = bf16[16,2,512,256]{3,2,1,0:T(8,128)(2,1)} custom-call(bf16[16,2,512,256]{3,2,1,0:T(8,128)(2,1)} %shard_map.86.refs_0_, bf16[2,512,256]{2,1,0:T(8,128)(2,1)S(1)} %collective-permute-done.2.refs_1_, bf16[4,512,256]{2,1,0:T(8,128)(2,1)S(1)} %collective-permute-done.4.refs_2_, ...), custom_call_target="tpu_custom_call", output_to_operand_aliasing={{}: (0, {})} | custom-call | bytes 7340032 | tf_op jit(solution)/shard_map/pallas_call | solution.py:209
  85.2 0.0 collective-permute-done.6.refs_1_
  85.3 0.2 pad_maximum_fusion
  85.5 2.0 %collective-permute-start.9 = (bf16[6,512,256]{2,1,0:T(8,128)(2,1)S(1)}, bf16[6,512,256]{2,1,0:T(8,128)(2,1)S(1)}, u32[]{:S(2)}, u32[]{:S(2)}) collective-permute-start(bf16[6,512,256]{2,1,0:T(8,128)(2,1)S(1)} %pad_maximum_fusion), channel_id=1, source_target_pairs={{1,0},{0,1},{3,2},{2,3},{5,4},{4,5},{7,6},{6,7},{9,8},{8,9},{11,10... | collective-permute-start | bytes 4718600 | tf_op jit(solution)/shard_map/ppermute | solution.py:40
  87.6 2.3 %collective-permute-start.10 = (bf16[4,512,256]{2,1,0:T(8,128)(2,1)S(1)}, bf16[4,512,256]{2,1,0:T(8,128)(2,1)S(1)}, u32[]{:S(2)}, u32[]{:S(2)}) collective-permute-start(bf16[4,512,256]{2,1,0:T(8,128)(2,1)S(1)} %collective-permute-done.6.refs_1_), channel_id=1, source_target_pairs={{1,0},{0,1},{3,2},{2,3},{5,4},{4,5},{7,6},{6,7},{9,8},{8,9},{11,10... | collective-permute-start | bytes 3145736 | tf_op jit(solution)/shard_map/ppermute | solution.py:40
  89.9 1.0 %shard_map.88.refs_0_ = bf16[16,2,512,256]{3,2,1,0:T(8,128)(2,1)} custom-call(bf16[16,2,512,256]{3,2,1,0:T(8,128)(2,1)} %shard_map.87.refs_0_, bf16[4,512,256]{2,1,0:T(8,128)(2,1)S(1)} %collective-permute-done.6.refs_1_), custom_call_target="tpu_custom_call", output_to_operand_aliasing={{}: (0, {})} | custom-call | bytes 2097152 | tf_op jit(solution)/shard_map/pallas_call | solution.py:209
  90.9 0.0 collective-permute-done.9.refs_1_
  90.9 1.2 %shard_map.89.refs_0_ = bf16[16,2,512,256]{3,2,1,0:T(8,128)(2,1)} custom-call(bf16[16,2,512,256]{3,2,1,0:T(8,128)(2,1)} %shard_map.88.refs_0_, bf16[6,512,256]{2,1,0:T(8,128)(2,1)S(1)} %collective-permute-done.9.refs_1_), custom_call_target="tpu_custom_call", output_to_operand_aliasing={{}: (0, {})} | custom-call | bytes 3145728 | tf_op jit(solution)/shard_map/pallas_call | solution.py:209
  92.2 0.2 collective-permute-done.10.refs_1_
  92.3 1.0 %shard_map.90 = bf16[16,2,512,256]{3,2,1,0:T(8,128)(2,1)} custom-call(bf16[16,2,512,256]{3,2,1,0:T(8,128)(2,1)} %shard_map.89.refs_0_, bf16[4,512,256]{2,1,0:T(8,128)(2,1)S(1)} %collective-permute-done.10.refs_1_), custom_call_target="tpu_custom_call", output_to_operand_aliasing={{}: (0, {})} | custom-call | bytes 2097152 | tf_op jit(solution)/shard_map/pallas_call | solution.py:209
  (4 shorter events, 0.1 us)
Async XLA Ops:
  0.6 11.4 %copy-start.2 = (s32[1,8]{1,0:T(1,128)S(1)}, s32[1,8]{1,0:T(1,128)}, u32[]{:S(2)}) copy-start(s32[1,8]{1,0:T(1,128)} %picks_hbm.1) | copy-start | bytes 100
  0.6 36.1 %copy-start = (f32[1,512,256]{2,1,0:T(8,128)S(1)}, f32[1,512,256]{2,1,0:T(8,128)}, u32[]{:S(2)}) copy-start(f32[1,512,256]{2,1,0:T(8,128)} %param.6) | copy-start | bytes 1572868
  0.7 36.1 %copy-start.1 = (f32[1,512,256]{2,1,0:T(8,128)S(1)}, f32[1,512,256]{2,1,0:T(8,128)}, u32[]{:S(2)}) copy-start(f32[1,512,256]{2,1,0:T(8,128)} %param.5) | copy-start | bytes 1572868
  3.3 17.9 %all-to-all-start = ((f32[16,8,384]{2,1,0:T(8,128)}), f32[16,8,384]{2,1,0:T(8,128)S(1)}, u32[]{:S(2)}, u32[]{:S(2)}) async-start(f32[16,8,384]{2,1,0:T(8,128)} %get-tuple-element.20), calls=%async_computation | async-start | bytes 393216 | tf_op jit(solution)/shard_map/all_to_all | solution.py:266
  22.6 15.2 %collective-permute-start = (bf16[512,256]{1,0:T(8,128)(2,1)S(1)}, bf16[512,256]{1,0:T(8,128)(2,1)S(1)}, u32[]{:S(2)}, u32[]{:S(2)}) collective-permute-start(bf16[512,256]{1,0:T(8,128)(2,1)S(1)} %get-tuple-element.25), channel_id=1, source_target_pairs={{2,0},{3,1},{12,2},{13,3},{6,4},{7,5},{0,6},{1,7},{10,8},{11,9},{4... | collective-permute-start | bytes 786440 | tf_op jit(solution)/shard_map/ppermute | solution.py:49
  30.3 13.4 %collective-permute-start.1 = (bf16[512,256]{1,0:T(8,128)(2,1)S(1)}, bf16[512,256]{1,0:T(8,128)(2,1)S(1)}, u32[]{:S(2)}, u32[]{:S(2)}) collective-permute-start(bf16[512,256]{1,0:T(8,128)(2,1)S(1)} %get-tuple-element.25), channel_id=1, source_target_pairs={{54,0},{55,1},{48,2},{49,3},{58,4},{59,5},{52,6},{53,7},{62,8},{63... | collective-permute-start | bytes 786440 | tf_op jit(solution)/shard_map/ppermute | solution.py:49
  43.7 10.2 %collective-permute-start.3 = (bf16[2,512,256]{2,1,0:T(8,128)(2,1)S(1)}, bf16[2,512,256]{2,1,0:T(8,128)(2,1)S(1)}, u32[]{:S(2)}, u32[]{:S(2)}) collective-permute-start(bf16[2,512,256]{2,1,0:T(8,128)(2,1)S(1)} %pad_maximum_fusion.3), channel_id=1, source_target_pairs={{1,0},{0,1},{3,2},{2,3},{5,4},{4,5},{7,6},{6,7},{9,8},{8,9},{11,10... | collective-permute-start | bytes 1572872 | tf_op jit(solution)/shard_map/ppermute | solution.py:40
  49.9 14.7 %collective-permute-start.2 = (bf16[2,512,256]{2,1,0:T(8,128)(2,1)S(1)}, bf16[2,512,256]{2,1,0:T(8,128)(2,1)S(1)}, u32[]{:S(2)}, u32[]{:S(2)}) collective-permute-start(bf16[2,512,256]{2,1,0:T(8,128)(2,1)S(1)} %pad_maximum_fusion.3), channel_id=1, source_target_pairs={{32,0},{49,1},{34,2},{51,3},{36,4},{53,5},{38,6},{55,7},{40,8},{57... | collective-permute-start | bytes 1572872 | tf_op jit(solution)/shard_map/ppermute | solution.py:35
  54.0 20.4 %collective-permute-start.4 = (bf16[4,512,256]{2,1,0:T(8,128)(2,1)S(1)}, bf16[4,512,256]{2,1,0:T(8,128)(2,1)S(1)}, u32[]{:S(2)}, u32[]{:S(2)}) collective-permute-start(bf16[4,512,256]{2,1,0:T(8,128)(2,1)S(1)} %pad_maximum_fusion.1.refs_0_), channel_id=1, source_target_pairs={{64,0},{449,1},{66,2},{451,3},{68,4},{453,5},{70,6},{455,7},{72,8}... | collective-permute-start | bytes 3145736 | tf_op jit(solution)/shard_map/ppermute | solution.py:35
  62.7 16.8 %collective-permute-start.5 = (bf16[4,512,256]{2,1,0:T(8,128)(2,1)S(1)}, bf16[4,512,256]{2,1,0:T(8,128)(2,1)S(1)}, u32[]{:S(2)}, u32[]{:S(2)}) collective-permute-start(bf16[4,512,256]{2,1,0:T(8,128)(2,1)S(1)} %pad_maximum_fusion.1.refs_0_), channel_id=1, source_target_pairs={{2,0},{15,1},{4,2},{1,3},{6,4},{3,5},{8,6},{5,7},{10,8},{7,9},{12,... | collective-permute-start | bytes 3145736 | tf_op jit(solution)/shard_map/ppermute | solution.py:35
  64.7 20.5 %collective-permute-start.6 = (bf16[4,512,256]{2,1,0:T(8,128)(2,1)S(1)}, bf16[4,512,256]{2,1,0:T(8,128)(2,1)S(1)}, u32[]{:S(2)}, u32[]{:S(2)}) collective-permute-start(bf16[4,512,256]{2,1,0:T(8,128)(2,1)S(1)} %pad_maximum_fusion.2), channel_id=1, source_target_pairs={{32,0},{49,1},{34,2},{51,3},{36,4},{53,5},{38,6},{55,7},{40,8},{57... | collective-permute-start | bytes 3145736 | tf_op jit(solution)/shard_map/ppermute | solution.py:35
  74.5 8.0 %collective-permute-start.7 = (bf16[2,512,256]{2,1,0:T(8,128)(2,1)S(1)}, bf16[2,512,256]{2,1,0:T(8,128)(2,1)S(1)}, u32[]{:S(2)}, u32[]{:S(2)}) collective-permute-start(bf16[2,512,256]{2,1,0:T(8,128)(2,1)S(1)} %slice.16), channel_id=1, source_target_pairs={{1,0},{0,1},{3,2},{2,3},{5,4},{4,5},{7,6},{6,7},{9,8},{8,9},{11,10... | collective-permute-start | bytes 1572872 | tf_op jit(solution)/shard_map/ppermute | solution.py:40
  79.5 3.8 %collective-permute-start.8 = (bf16[2,512,256]{2,1,0:T(8,128)(2,1)S(1)}, bf16[2,512,256]{2,1,0:T(8,128)(2,1)S(1)}, u32[]{:S(2)}, u32[]{:S(2)}) collective-permute-start(bf16[2,512,256]{2,1,0:T(8,128)(2,1)S(1)} %slice.17), channel_id=1, source_target_pairs={{1,0},{0,1},{3,2},{2,3},{5,4},{4,5},{7,6},{6,7},{9,8},{8,9},{11,10... | collective-permute-start | bytes 1572872 | tf_op jit(solution)/shard_map/ppermute | solution.py:40
  85.5 5.4 %collective-permute-start.9 = (bf16[6,512,256]{2,1,0:T(8,128)(2,1)S(1)}, bf16[6,512,256]{2,1,0:T(8,128)(2,1)S(1)}, u32[]{:S(2)}, u32[]{:S(2)}) collective-permute-start(bf16[6,512,256]{2,1,0:T(8,128)(2,1)S(1)} %pad_maximum_fusion), channel_id=1, source_target_pairs={{1,0},{0,1},{3,2},{2,3},{5,4},{4,5},{7,6},{6,7},{9,8},{8,9},{11,10... | collective-permute-start | bytes 4718600 | tf_op jit(solution)/shard_map/ppermute | solution.py:40
  87.6 4.8 %collective-permute-start.10 = (bf16[4,512,256]{2,1,0:T(8,128)(2,1)S(1)}, bf16[4,512,256]{2,1,0:T(8,128)(2,1)S(1)}, u32[]{:S(2)}, u32[]{:S(2)}) collective-permute-start(bf16[4,512,256]{2,1,0:T(8,128)(2,1)S(1)} %collective-permute-done.6.refs_1_), channel_id=1, source_target_pairs={{1,0},{0,1},{3,2},{2,3},{5,4},{4,5},{7,6},{6,7},{9,8},{8,9},{11,10... | collective-permute-start | bytes 3145736 | tf_op jit(solution)/shard_map/ppermute | solution.py:40

commit v11 on v10

--- a/solution.py
+++ b/solution.py
@@ -13,8 +13,11 @@
 NX, NY, NZ, CORES = 4, 8, 8, 2
 CLASSES = 2 * NZ
 COLOURS = 8
-SHIFTS = (1, 3)
 VMEM_LIMIT = 40 * 1024 * 1024
+
+
+def z_of(colour, x_hi, core):
+    return (colour + 1 + 4 * core - x_hi + NZ) % NZ
 
 
 def device_at(x, y, z, core):
@@ -44,7 +47,7 @@
     pairs = []
     for x, y, z, core in PLACES:
         x_there = NX - 1 - x if partner else x
-        z_there = colour_of(x, y, z) + SHIFTS[x_there // 2]
+        z_there = z_of(colour_of(x, y, z), x_there // 2, core)
         pairs.append((device_at(x_there, y, z_there, core), device_at(x, y, z, core)))
     return lax.ppermute(shard, AXES, pairs)
 
@@ -56,7 +59,7 @@
 
 
 def colour_of(x, y, z):
-    return (2 * x + y + 5 * z) % COLOURS
+    return (2 * x + y + 3 * z) % COLOURS
 
 
 def choose_kernel(
@@ -129,6 +132,44 @@
     )(picks, error, grad, momentum, params)
 
 
+def keep_kernel(picks_hbm, error_hbm, grad_hbm, new_error, picks_smem, error, grad, sems):
+    copies = [
+        pltpu.make_async_copy(picks_hbm, picks_smem, sems.at[0]),
+        pltpu.make_async_copy(error_hbm, error, sems.at[1]),
+        pltpu.make_async_copy(grad_hbm, grad, sems.at[2]),
+    ]
+    for copy in copies:
+        copy.start()
+    for copy in copies:
+        copy.wait()
+    row = lax.broadcasted_iota(jnp.int32, error.shape, 0)
+    chosen = row == picks_smem[0, 0]
+    for at in range(1, picks_smem.shape[1]):
+        chosen = chosen | (row == picks_smem[0, at])
+    new_error[...] = jnp.where(chosen, 0.0, DECAY_RATE * error[...] + grad[...])
+
+
+def keep(picks, error, grad):
+    hbm = pl.BlockSpec(memory_space=pltpu.HBM)
+    picks, error, grad = (
+        pltpu.with_memory_space_constraint(array, pltpu.HBM) for array in (picks, error, grad)
+    )
+    return pl.pallas_call(
+        keep_kernel,
+        out_shape=jax.ShapeDtypeStruct(error.shape, jnp.float32),
+        in_specs=[hbm] * 3,
+        out_specs=pl.BlockSpec(memory_space=pltpu.VMEM),
+        scratch_shapes=[
+            pltpu.SMEM(picks.shape, jnp.int32),
+            pltpu.VMEM(error.shape, jnp.float32),
+            pltpu.VMEM(error.shape, jnp.float32),
+            pltpu.SemaphoreType.DMA((3,)),
+        ],
+        compiler_params=pltpu.CompilerParams(vmem_limit_bytes=VMEM_LIMIT),
+        cost_estimate=pl.CostEstimate(flops=10**6, bytes_accessed=2 * 10**6, transcendentals=0),
+    )(picks, error, grad)
+
+
 def update_kernel(everyone, momentum, params, new_params, new_momentum, shard):
     blocks, block = params.shape
     entries = everyone.shape[0]
@@ -192,11 +233,11 @@
             own = x_there // 2
             for at in range(count):
                 x_hi = 1 - own if (place + at) % 2 else own
-                shift = SHIFTS[0] + (SHIFTS[1] - SHIFTS[0]) * x_hi
+                from_core = 1 - by if place + at >= 2 else by
                 copies.append(
                     pltpu.make_async_copy(
                         sources[slot].at[first + at],
-                        out.at[x_hi * NZ + (colour + shift) % NZ, 1 - by if place + at >= 2 else by],
+                        out.at[x_hi * NZ + z_of(colour, x_hi, from_core), from_core],
                         sems.at[len(copies)],
                     )
                 )
@@ -259,15 +300,13 @@
 def per_device(pseudo_grad, error_buf, momentum, params, picks):
     blocks, block = params.shape
     replicas = lax.axis_size("rep")
-    own_picks = picks[0]
     payload, momentum_near, params_near = choose(
         picks, error_buf[0], pseudo_grad[0], momentum, params, replicas
     )
     everyone = lax.all_to_all(payload, "rep", 0, 0).reshape(-1, payload.shape[-1])
     new_params, new_momentum, shard = update(everyone, momentum_near, params_near)
-    accumulated = DECAY_RATE * error_buf[0] + pseudo_grad[0]
-    chosen = jnp.any(own_picks[:, None] == lax.iota(jnp.int32, blocks)[None, :], axis=0)
-    new_error = jnp.where(chosen[:, None], 0.0, accumulated)[None]
+    error_buf, pseudo_grad, shard = lax.optimization_barrier((error_buf, pseudo_grad, shard))
+    new_error = keep(picks, error_buf[0], pseudo_grad[0])[None]
     gathered, new_error = gather_slab(shard, new_error)
     return (new_params, new_momentum, new_error, gathered.reshape(-1, block))
 

time: 93.9 us -> 89.7 us (0.955)
  blocking collectives: 0 us -> 17.7 us
  starting transfers between devices: 56.3 us -> 44.5 us
  waiting for transfers between devices: 24.3 us -> 13.7 us
  Pallas kernels: 10.3 us -> 11.8 us
  other arithmetic: 1.44 us -> 0.42 us
    all_to_all x0 -> x1, blocking collectives: none -> 17.7 us  [per_device(): lax.all_to_all(payload, 'rep', 0, 0).reshape(-1, payload.shape[-1])]
    all_to_all x1 -> x0, waiting for transfers between devices: 9.05 us -> none  [per_device(): lax.all_to_all(payload, 'rep', 0, 0).reshape(-1, payload.shape[-1])]
    all_to_all x1 -> x0, starting transfers between devices: 8.69 us -> none  [per_device(): lax.all_to_all(payload, 'rep', 0, 0).reshape(-1, payload.shape[-1])]
    ppermute x4, starting transfers between devices: 17.7 us -> 14.1 us  [fetch(): return lax.ppermute(value, AXES, pairs)]
    pallas_call x0 -> x1, Pallas kernels: none -> 2.3 us  [keep(): pl.pallas_call(keep_kernel, out_shape=jax.ShapeDtypeStruct(error.shape, j...]
    ppermute x5, starting transfers between devices: 15.7 us -> 17.8 us  [swap(): return lax.ppermute(value, AXES, pairs)]
    ppermute x4, waiting for transfers between devices: 8.31 us -> 6.58 us  [fetch(): return lax.ppermute(value, AXES, pairs)]
    ppermute x2, starting transfers between devices: 14.2 us -> 12.6 us  [collect(): return lax.ppermute(shard, AXES, pairs)]
  transfers between devices with their start and end apart: 12 -> 11, of which waited for: 6 -> 6; matrix products, arithmetic and copies ran while one was open for 1% -> 0% of each run, Pallas kernels for 6% -> 8%
where the time goes in v11:
time: 89.7 us; the launch traced here: 89.2 us
  starting transfers between devices  44.5 us (50%)
  blocking collectives  17.7 us (20%)
  waiting for transfers between devices  13.7 us (15%)
  Pallas kernels  11.8 us (13%)
    ppermute x5, starting transfers between devices, swap(): return lax.ppermute(value, AXES, pairs)  17.8 us
    all_to_all x1, blocking collectives, per_device(): lax.all_to_all(payload, 'rep', 0, 0).reshape(-1, payload.shape[-1])  17.7 us
    ppermute x4, starting transfers between devices, fetch(): return lax.ppermute(value, AXES, pairs)  14.1 us
    ppermute x2, starting transfers between devices, collect(): return lax.ppermute(shard, AXES, pairs)  12.6 us
    ppermute x4, waiting for transfers between devices, fetch(): return lax.ppermute(value, AXES, pairs)  6.58 us
    ppermute x2, waiting for transfers between devices, collect(): return lax.ppermute(shard, AXES, pairs)  6.49 us
    pallas_call x5, Pallas kernels, put(): pl.pallas_call(kernel, out_shape=jax.ShapeDtypeStruct(shape, dtype), in_s...  6.26 us
    pallas_call x1, Pallas kernels, keep(): pl.pallas_call(keep_kernel, out_shape=jax.ShapeDtypeStruct(error.shape, j...  2.3 us
  transfers between devices with their start and end apart: 11, of which 6 were waited for; matrix products, arithmetic and copies ran while one was open for 0% of the time, Pallas kernels for 8%

profile of v11, /device:TPU:1, one launch (start us, length us, event | category | flops | bytes accessed | tf_op | source)
XLA Modules:
  0.0 89.2 jit_solution(2996694578906393907)
XLA Ops:
  0.6 1.8 %shard_map.84 = (f32[16,8,384]{2,1,0:T(8,128)S(1)}, f32[512,256]{1,0:T(8,128)S(1)}, f32[512,256]{1,0:T(8,128)S(1)}) custom-call(s32[1,8]{1,0:T(1,128)} %picks_hbm.3, f32[512,256]{1,0:T(8,128)} %bitcast.11, f32[512,256]{1,0:T(8,128)} %bitcast.13, f32[512,256]{1,0:T(8,128)} %momentum.1, f32[512,256]{1,0:T(8,128)} %params.1), custom_call_target="tpu_custom_call" | custom-call | flops 100000 | bytes 2000000 | tf_op jit(solution)/shard_map/pallas_call | solution.py:116
  2.5 17.7 %all_to_all.5 = f32[16,8,384]{2,1,0:T(8,128)S(1)} all-to-all(f32[16,8,384]{2,1,0:T(8,128)S(1)} %get-tuple-element.23), channel_id=1, replica_groups=mesh['rep'=16,'fsdp'=32] {'rep'}, dimensions={0} | all-to-all | bytes 393216 | tf_op jit(solution)/shard_map/all_to_all | solution.py:306
  20.2 1.4 %shard_map.85 = (f32[512,256]{1,0:T(8,128)}, f32[512,256]{1,0:T(8,128)}, bf16[512,256]{1,0:T(8,128)(2,1)S(1)}) custom-call(f32[128,384]{1,0:T(8,128)S(1)} %bitcast.9, f32[512,256]{1,0:T(8,128)S(1)} %get-tuple-element.24.momentum, f32[512,256]{1,0:T(8,128)S(1)} %get-tuple-element.25.params), custom_call_target="tpu_custom_call" | custom-call | flops 100000000 | bytes 4000000 | tf_op jit(solution)/shard_map/pallas_call | solution.py:201
  21.6 4.0 %collective-permute-start = (bf16[512,256]{1,0:T(8,128)(2,1)S(1)}, bf16[512,256]{1,0:T(8,128)(2,1)S(1)}, u32[]{:S(2)}, u32[]{:S(2)}) collective-permute-start(bf16[512,256]{1,0:T(8,128)(2,1)S(1)} %get-tuple-element.29), channel_id=1, source_target_pairs={{2,0},{11,1},{8,2},{1,3},{14,4},{7,5},{4,6},{13,7},{10,8},{3,9},{0... | collective-permute-start | bytes 786440 | tf_op jit(solution)/shard_map/ppermute | solution.py:52
  25.6 8.6 %collective-permute-start.1 = (bf16[512,256]{1,0:T(8,128)(2,1)S(1)}, bf16[512,256]{1,0:T(8,128)(2,1)S(1)}, u32[]{:S(2)}, u32[]{:S(2)}) collective-permute-start(bf16[512,256]{1,0:T(8,128)(2,1)S(1)} %get-tuple-element.29), channel_id=1, source_target_pairs={{48,0},{57,1},{54,2},{63,3},{60,4},{53,5},{50,6},{59,7},{56,8},{49... | collective-permute-start | bytes 786440 | tf_op jit(solution)/shard_map/ppermute | solution.py:52
  34.2 2.3 %shard_map.86 = f32[512,256]{1,0:T(8,128)} custom-call(s32[1,8]{1,0:T(1,128)} %picks_hbm.3, f32[512,256]{1,0:T(8,128)} %bitcast.12, f32[512,256]{1,0:T(8,128)} %bitcast.14), custom_call_target="tpu_custom_call" | custom-call | flops 1000000 | bytes 2000000 | tf_op jit(solution)/shard_map/pallas_call | solution.py:157
  36.5 0.0 collective-permute-done
  36.5 6.5 %collective-permute-done.1 = bf16[512,256]{1,0:T(8,128)(2,1)S(1)} collective-permute-done((bf16[512,256]{1,0:T(8,128)(2,1)S(1)}, bf16[512,256]{1,0:T(8,128)(2,1)S(1)}, u32[]{:S(2)}, u32[]{:S(2)}) %collective-permute-start.1) | collective-permute-done | bytes 262176 | tf_op jit(solution)/shard_map/ppermute | solution.py:52
  43.0 0.1 pad_maximum_fusion.3
  43.1 5.3 %collective-permute-start.3 = (bf16[2,512,256]{2,1,0:T(8,128)(2,1)S(1)}, bf16[2,512,256]{2,1,0:T(8,128)(2,1)S(1)}, u32[]{:S(2)}, u32[]{:S(2)}) collective-permute-start(bf16[2,512,256]{2,1,0:T(8,128)(2,1)S(1)} %pad_maximum_fusion.3), channel_id=1, source_target_pairs={{1,0},{0,1},{3,2},{2,3},{5,4},{4,5},{7,6},{6,7},{9,8},{8,9},{11,10... | collective-permute-start | bytes 1572872 | tf_op jit(solution)/shard_map/ppermute | solution.py:43
  48.3 4.0 %collective-permute-start.2 = (bf16[2,512,256]{2,1,0:T(8,128)(2,1)S(1)}, bf16[2,512,256]{2,1,0:T(8,128)(2,1)S(1)}, u32[]{:S(2)}, u32[]{:S(2)}) collective-permute-start(bf16[2,512,256]{2,1,0:T(8,128)(2,1)S(1)} %pad_maximum_fusion.3), channel_id=1, source_target_pairs={{32,0},{49,1},{34,2},{51,3},{36,4},{53,5},{38,6},{55,7},{40,8},{57... | collective-permute-start | bytes 1572872 | tf_op jit(solution)/shard_map/ppermute | solution.py:38
  52.3 0.0 collective-permute-done.3
  52.3 0.1 pad_maximum_fusion.1.refs_0_
  52.4 3.6 %collective-permute-start.4 = (bf16[4,512,256]{2,1,0:T(8,128)(2,1)S(1)}, bf16[4,512,256]{2,1,0:T(8,128)(2,1)S(1)}, u32[]{:S(2)}, u32[]{:S(2)}) collective-permute-start(bf16[4,512,256]{2,1,0:T(8,128)(2,1)S(1)} %pad_maximum_fusion.1.refs_0_), channel_id=1, source_target_pairs={{64,0},{449,1},{66,2},{451,3},{68,4},{453,5},{70,6},{455,7},{72,8}... | collective-permute-start | bytes 3145736 | tf_op jit(solution)/shard_map/ppermute | solution.py:38
  56.0 3.5 %collective-permute-start.5 = (bf16[4,512,256]{2,1,0:T(8,128)(2,1)S(1)}, bf16[4,512,256]{2,1,0:T(8,128)(2,1)S(1)}, u32[]{:S(2)}, u32[]{:S(2)}) collective-permute-start(bf16[4,512,256]{2,1,0:T(8,128)(2,1)S(1)} %pad_maximum_fusion.1.refs_0_), channel_id=1, source_target_pairs={{2,0},{15,1},{4,2},{1,3},{6,4},{3,5},{8,6},{5,7},{10,8},{7,9},{12,... | collective-permute-start | bytes 3145736 | tf_op jit(solution)/shard_map/ppermute | solution.py:38
  59.5 0.5 collective-permute-done.2.refs_1_
  60.0 0.1 pad_maximum_fusion.2
  60.1 3.1 %collective-permute-start.6 = (bf16[4,512,256]{2,1,0:T(8,128)(2,1)S(1)}, bf16[4,512,256]{2,1,0:T(8,128)(2,1)S(1)}, u32[]{:S(2)}, u32[]{:S(2)}) collective-permute-start(bf16[4,512,256]{2,1,0:T(8,128)(2,1)S(1)} %pad_maximum_fusion.2), channel_id=1, source_target_pairs={{32,0},{49,1},{34,2},{51,3},{36,4},{53,5},{38,6},{55,7},{40,8},{57... | collective-permute-start | bytes 3145736 | tf_op jit(solution)/shard_map/ppermute | solution.py:38
  63.2 6.0 %collective-permute-done.4.refs_2_ = bf16[4,512,256]{2,1,0:T(8,128)(2,1)S(1)} collective-permute-done((bf16[4,512,256]{2,1,0:T(8,128)(2,1)S(1)}, bf16[4,512,256]{2,1,0:T(8,128)(2,1)S(1)}, u32[]{:S(2)}, u32[]{:S(2)}) %collective-permute-start.4) | collective-permute-done | bytes 1048608 | tf_op jit(solution)/shard_map/ppermute | solution.py:38
  69.2 3.4 %collective-permute-start.7 = (bf16[2,512,256]{2,1,0:T(8,128)(2,1)S(1)}, bf16[2,512,256]{2,1,0:T(8,128)(2,1)S(1)}, u32[]{:S(2)}, u32[]{:S(2)}) collective-permute-start(bf16[2,512,256]{2,1,0:T(8,128)(2,1)S(1)} %slice.16), channel_id=1, source_target_pairs={{1,0},{0,1},{3,2},{2,3},{5,4},{4,5},{7,6},{6,7},{9,8},{8,9},{11,10... | collective-permute-start | bytes 1572872 | tf_op jit(solution)/shard_map/ppermute | solution.py:43
  72.6 0.1 collective-permute-done.5.refs_4_
  72.8 4.8 %collective-permute-start.8 = (bf16[2,512,256]{2,1,0:T(8,128)(2,1)S(1)}, bf16[2,512,256]{2,1,0:T(8,128)(2,1)S(1)}, u32[]{:S(2)}, u32[]{:S(2)}) collective-permute-start(bf16[2,512,256]{2,1,0:T(8,128)(2,1)S(1)} %slice.17), channel_id=1, source_target_pairs={{1,0},{0,1},{3,2},{2,3},{5,4},{4,5},{7,6},{6,7},{9,8},{8,9},{11,10... | collective-permute-start | bytes 1572872 | tf_op jit(solution)/shard_map/ppermute | solution.py:43
  77.6 1.0 %shard_map.87.refs_0_ = bf16[16,2,512,256]{3,2,1,0:T(8,128)(2,1)} custom-call(bf16[4,512,256]{2,1,0:T(8,128)(2,1)S(1)} %pad_maximum_fusion.1.refs_0_), custom_call_target="tpu_custom_call" | custom-call | bytes 2097152 | tf_op jit(solution)/shard_map/pallas_call | solution.py:250
  78.6 0.0 collective-permute-done.7.refs_3_
  78.6 0.5 collective-permute-done.8.refs_5_
  79.1 1.9 %shard_map.88.refs_0_ = bf16[16,2,512,256]{3,2,1,0:T(8,128)(2,1)} custom-call(bf16[16,2,512,256]{3,2,1,0:T(8,128)(2,1)} %shard_map.87.refs_0_, bf16[2,512,256]{2,1,0:T(8,128)(2,1)S(1)} %collective-permute-done.2.refs_1_, bf16[4,512,256]{2,1,0:T(8,128)(2,1)S(1)} %collective-permute-done.4.refs_2_, ...), custom_call_target="tpu_custom_call", output_to_operand_aliasing={{}: (0, {})} | custom-call | bytes 7340032 | tf_op jit(solution)/shard_map/pallas_call | solution.py:250
  81.1 0.0 collective-permute-done.6.refs_1_
  81.2 0.2 pad_maximum_fusion
  81.3 2.3 %collective-permute-start.9 = (bf16[6,512,256]{2,1,0:T(8,128)(2,1)S(1)}, bf16[6,512,256]{2,1,0:T(8,128)(2,1)S(1)}, u32[]{:S(2)}, u32[]{:S(2)}) collective-permute-start(bf16[6,512,256]{2,1,0:T(8,128)(2,1)S(1)} %pad_maximum_fusion), channel_id=1, source_target_pairs={{1,0},{0,1},{3,2},{2,3},{5,4},{4,5},{7,6},{6,7},{9,8},{8,9},{11,10... | collective-permute-start | bytes 4718600 | tf_op jit(solution)/shard_map/ppermute | solution.py:43
  83.6 2.0 %collective-permute-start.10 = (bf16[4,512,256]{2,1,0:T(8,128)(2,1)S(1)}, bf16[4,512,256]{2,1,0:T(8,128)(2,1)S(1)}, u32[]{:S(2)}, u32[]{:S(2)}) collective-permute-start(bf16[4,512,256]{2,1,0:T(8,128)(2,1)S(1)} %collective-permute-done.6.refs_1_), channel_id=1, source_target_pairs={{1,0},{0,1},{3,2},{2,3},{5,4},{4,5},{7,6},{6,7},{9,8},{8,9},{11,10... | collective-permute-start | bytes 3145736 | tf_op jit(solution)/shard_map/ppermute | solution.py:43
  85.7 1.0 %shard_map.89.refs_0_ = bf16[16,2,512,256]{3,2,1,0:T(8,128)(2,1)} custom-call(bf16[16,2,512,256]{3,2,1,0:T(8,128)(2,1)} %shard_map.88.refs_0_, bf16[4,512,256]{2,1,0:T(8,128)(2,1)S(1)} %collective-permute-done.6.refs_1_), custom_call_target="tpu_custom_call", output_to_operand_aliasing={{}: (0, {})} | custom-call | bytes 2097152 | tf_op jit(solution)/shard_map/pallas_call | solution.py:250
  86.7 0.0 collective-permute-done.9.refs_1_
  86.7 1.2 %shard_map.90.refs_0_ = bf16[16,2,512,256]{3,2,1,0:T(8,128)(2,1)} custom-call(bf16[16,2,512,256]{3,2,1,0:T(8,128)(2,1)} %shard_map.89.refs_0_, bf16[6,512,256]{2,1,0:T(8,128)(2,1)S(1)} %collective-permute-done.9.refs_1_), custom_call_target="tpu_custom_call", output_to_operand_aliasing={{}: (0, {})} | custom-call | bytes 3145728 | tf_op jit(solution)/shard_map/pallas_call | solution.py:250
  88.0 0.2 collective-permute-done.10.refs_1_
  88.2 1.0 %shard_map.91 = bf16[16,2,512,256]{3,2,1,0:T(8,128)(2,1)} custom-call(bf16[16,2,512,256]{3,2,1,0:T(8,128)(2,1)} %shard_map.90.refs_0_, bf16[4,512,256]{2,1,0:T(8,128)(2,1)S(1)} %collective-permute-done.10.refs_1_), custom_call_target="tpu_custom_call", output_to_operand_aliasing={{}: (0, {})} | custom-call | bytes 2097152 | tf_op jit(solution)/shard_map/pallas_call | solution.py:250
  (4 shorter events, 0.1 us)
Async XLA Ops:
  21.6 14.9 %collective-permute-start = (bf16[512,256]{1,0:T(8,128)(2,1)S(1)}, bf16[512,256]{1,0:T(8,128)(2,1)S(1)}, u32[]{:S(2)}, u32[]{:S(2)}) collective-permute-start(bf16[512,256]{1,0:T(8,128)(2,1)S(1)} %get-tuple-element.29), channel_id=1, source_target_pairs={{2,0},{11,1},{8,2},{1,3},{14,4},{7,5},{4,6},{13,7},{10,8},{3,9},{0... | collective-permute-start | bytes 786440 | tf_op jit(solution)/shard_map/ppermute | solution.py:52
  25.6 17.4 %collective-permute-start.1 = (bf16[512,256]{1,0:T(8,128)(2,1)S(1)}, bf16[512,256]{1,0:T(8,128)(2,1)S(1)}, u32[]{:S(2)}, u32[]{:S(2)}) collective-permute-start(bf16[512,256]{1,0:T(8,128)(2,1)S(1)} %get-tuple-element.29), channel_id=1, source_target_pairs={{48,0},{57,1},{54,2},{63,3},{60,4},{53,5},{50,6},{59,7},{56,8},{49... | collective-permute-start | bytes 786440 | tf_op jit(solution)/shard_map/ppermute | solution.py:52
  43.1 9.2 %collective-permute-start.3 = (bf16[2,512,256]{2,1,0:T(8,128)(2,1)S(1)}, bf16[2,512,256]{2,1,0:T(8,128)(2,1)S(1)}, u32[]{:S(2)}, u32[]{:S(2)}) collective-permute-start(bf16[2,512,256]{2,1,0:T(8,128)(2,1)S(1)} %pad_maximum_fusion.3), channel_id=1, source_target_pairs={{1,0},{0,1},{3,2},{2,3},{5,4},{4,5},{7,6},{6,7},{9,8},{8,9},{11,10... | collective-permute-start | bytes 1572872 | tf_op jit(solution)/shard_map/ppermute | solution.py:43
  48.3 11.6 %collective-permute-start.2 = (bf16[2,512,256]{2,1,0:T(8,128)(2,1)S(1)}, bf16[2,512,256]{2,1,0:T(8,128)(2,1)S(1)}, u32[]{:S(2)}, u32[]{:S(2)}) collective-permute-start(bf16[2,512,256]{2,1,0:T(8,128)(2,1)S(1)} %pad_maximum_fusion.3), channel_id=1, source_target_pairs={{32,0},{49,1},{34,2},{51,3},{36,4},{53,5},{38,6},{55,7},{40,8},{57... | collective-permute-start | bytes 1572872 | tf_op jit(solution)/shard_map/ppermute | solution.py:38
  52.4 16.8 %collective-permute-start.4 = (bf16[4,512,256]{2,1,0:T(8,128)(2,1)S(1)}, bf16[4,512,256]{2,1,0:T(8,128)(2,1)S(1)}, u32[]{:S(2)}, u32[]{:S(2)}) collective-permute-start(bf16[4,512,256]{2,1,0:T(8,128)(2,1)S(1)} %pad_maximum_fusion.1.refs_0_), channel_id=1, source_target_pairs={{64,0},{449,1},{66,2},{451,3},{68,4},{453,5},{70,6},{455,7},{72,8}... | collective-permute-start | bytes 3145736 | tf_op jit(solution)/shard_map/ppermute | solution.py:38
  56.0 16.8 %collective-permute-start.5 = (bf16[4,512,256]{2,1,0:T(8,128)(2,1)S(1)}, bf16[4,512,256]{2,1,0:T(8,128)(2,1)S(1)}, u32[]{:S(2)}, u32[]{:S(2)}) collective-permute-start(bf16[4,512,256]{2,1,0:T(8,128)(2,1)S(1)} %pad_maximum_fusion.1.refs_0_), channel_id=1, source_target_pairs={{2,0},{15,1},{4,2},{1,3},{6,4},{3,5},{8,6},{5,7},{10,8},{7,9},{12,... | collective-permute-start | bytes 3145736 | tf_op jit(solution)/shard_map/ppermute | solution.py:38
  60.1 21.0 %collective-permute-start.6 = (bf16[4,512,256]{2,1,0:T(8,128)(2,1)S(1)}, bf16[4,512,256]{2,1,0:T(8,128)(2,1)S(1)}, u32[]{:S(2)}, u32[]{:S(2)}) collective-permute-start(bf16[4,512,256]{2,1,0:T(8,128)(2,1)S(1)} %pad_maximum_fusion.2), channel_id=1, source_target_pairs={{32,0},{49,1},{34,2},{51,3},{36,4},{53,5},{38,6},{55,7},{40,8},{57... | collective-permute-start | bytes 3145736 | tf_op jit(solution)/shard_map/ppermute | solution.py:38
  69.2 9.4 %collective-permute-start.7 = (bf16[2,512,256]{2,1,0:T(8,128)(2,1)S(1)}, bf16[2,512,256]{2,1,0:T(8,128)(2,1)S(1)}, u32[]{:S(2)}, u32[]{:S(2)}) collective-permute-start(bf16[2,512,256]{2,1,0:T(8,128)(2,1)S(1)} %slice.16), channel_id=1, source_target_pairs={{1,0},{0,1},{3,2},{2,3},{5,4},{4,5},{7,6},{6,7},{9,8},{8,9},{11,10... | collective-permute-start | bytes 1572872 | tf_op jit(solution)/shard_map/ppermute | solution.py:43
  72.8 6.3 %collective-permute-start.8 = (bf16[2,512,256]{2,1,0:T(8,128)(2,1)S(1)}, bf16[2,512,256]{2,1,0:T(8,128)(2,1)S(1)}, u32[]{:S(2)}, u32[]{:S(2)}) collective-permute-start(bf16[2,512,256]{2,1,0:T(8,128)(2,1)S(1)} %slice.17), channel_id=1, source_target_pairs={{1,0},{0,1},{3,2},{2,3},{5,4},{4,5},{7,6},{6,7},{9,8},{8,9},{11,10... | collective-permute-start | bytes 1572872 | tf_op jit(solution)/shard_map/ppermute | solution.py:43
  81.3 5.4 %collective-permute-start.9 = (bf16[6,512,256]{2,1,0:T(8,128)(2,1)S(1)}, bf16[6,512,256]{2,1,0:T(8,128)(2,1)S(1)}, u32[]{:S(2)}, u32[]{:S(2)}) collective-permute-start(bf16[6,512,256]{2,1,0:T(8,128)(2,1)S(1)} %pad_maximum_fusion), channel_id=1, source_target_pairs={{1,0},{0,1},{3,2},{2,3},{5,4},{4,5},{7,6},{6,7},{9,8},{8,9},{11,10... | collective-permute-start | bytes 4718600 | tf_op jit(solution)/shard_map/ppermute | solution.py:43
  83.6 4.6 %collective-permute-start.10 = (bf16[4,512,256]{2,1,0:T(8,128)(2,1)S(1)}, bf16[4,512,256]{2,1,0:T(8,128)(2,1)S(1)}, u32[]{:S(2)}, u32[]{:S(2)}) collective-permute-start(bf16[4,512,256]{2,1,0:T(8,128)(2,1)S(1)} %collective-permute-done.6.refs_1_), channel_id=1, source_target_pairs={{1,0},{0,1},{3,2},{2,3},{5,4},{4,5},{7,6},{6,7},{9,8},{8,9},{11,10... | collective-permute-start | bytes 3145736 | tf_op jit(solution)/shard_map/ppermute | solution.py:43

commit v12 on v11

--- a/solution.py
+++ b/solution.py
@@ -170,7 +170,7 @@
     )(picks, error, grad)
 
 
-def update_kernel(everyone, momentum, params, new_params, new_momentum, shard):
+def step(everyone, momentum, params):
     blocks, block = params.shape
     entries = everyone.shape[0]
     values = everyone[:, :block]
@@ -189,26 +189,26 @@
         )
     delta = delta / 16.0
     momentum_now = MOMENTUM_COEF * momentum[...] + delta
-    params_now = params[...] - STEP_SCALE * (delta + MOMENTUM_COEF * momentum_now)
-    new_momentum[...] = momentum_now
-    new_params[...] = params_now
-    shard[...] = params_now.astype(jnp.bfloat16)
-
-
-def update(everyone, momentum, params):
-    blocks, block = params.shape
+    return params[...] - STEP_SCALE * (delta + MOMENTUM_COEF * momentum_now), momentum_now
+
+
+def shard_kernel(everyone, momentum, params, shard):
+    shard[...] = step(everyone, momentum, params)[0].astype(jnp.bfloat16)
+
+
+def state_kernel(everyone, momentum, params, new_params, new_momentum):
+    new_params[...], new_momentum[...] = step(everyone, momentum, params)
+
+
+def update(kernel, everyone, momentum, params, dtypes):
     vmem = pl.BlockSpec(memory_space=pltpu.VMEM)
     return pl.pallas_call(
-        update_kernel,
-        out_shape=(
-            jax.ShapeDtypeStruct((blocks, block), jnp.float32),
-            jax.ShapeDtypeStruct((blocks, block), jnp.float32),
-            jax.ShapeDtypeStruct((blocks, block), jnp.bfloat16),
-        ),
+        kernel,
+        out_shape=[jax.ShapeDtypeStruct(params.shape, dtype) for dtype in dtypes],
         in_specs=[vmem] * 3,
-        out_specs=(vmem,) * 3,
+        out_specs=[vmem] * len(dtypes),
         compiler_params=pltpu.CompilerParams(vmem_limit_bytes=VMEM_LIMIT),
-        cost_estimate=pl.CostEstimate(flops=10**8, bytes_accessed=4 * 10**6, transcendentals=0),
+        cost_estimate=pl.CostEstimate(flops=10**8, bytes_accessed=3 * 10**6, transcendentals=0),
     )(everyone, momentum, params)
 
 
@@ -304,10 +304,13 @@
         picks, error_buf[0], pseudo_grad[0], momentum, params, replicas
     )
     everyone = lax.all_to_all(payload, "rep", 0, 0).reshape(-1, payload.shape[-1])
-    new_params, new_momentum, shard = update(everyone, momentum_near, params_near)
-    error_buf, pseudo_grad, shard = lax.optimization_barrier((error_buf, pseudo_grad, shard))
+    (shard,) = update(shard_kernel, everyone, momentum_near, params_near, [jnp.bfloat16])
+    error_buf, pseudo_grad, everyone, shard = lax.optimization_barrier(
+        (error_buf, pseudo_grad, everyone, shard)
+    )
     new_error = keep(picks, error_buf[0], pseudo_grad[0])[None]
-    gathered, new_error = gather_slab(shard, new_error)
+    state = update(state_kernel, everyone, momentum_near, params_near, [jnp.float32] * 2)
+    gathered, (new_error, new_params, new_momentum) = gather_slab(shard, (new_error, *state))
     return (new_params, new_momentum, new_error, gathered.reshape(-1, block))
 
 

time: 89.7 us -> 88.7 us (0.989)
  waiting for transfers between devices: 13.7 us -> 12.4 us
    ppermute x2, waiting for transfers between devices: 6.49 us -> 5.12 us  [collect(): return lax.ppermute(shard, AXES, pairs)]
  transfers between devices with their start and end apart: 11 -> 11, of which waited for: 6 -> 6; matrix products, arithmetic and copies ran while one was open for 0% -> 0% of each run, Pallas kernels for 8% -> 10%
where the time goes in v12:
time: 88.7 us; the launch traced here: 88.2 us
  starting transfers between devices  44.5 us (50%)
  blocking collectives  17.7 us (20%)
  waiting for transfers between devices  12.4 us (14%)
  Pallas kernels  12.2 us (14%)
    ppermute x5, starting transfers between devices, swap(): return lax.ppermute(value, AXES, pairs)  17.8 us
    all_to_all x1, blocking collectives, per_device(): lax.all_to_all(payload, 'rep', 0, 0).reshape(-1, payload.shape[-1])  17.7 us
    ppermute x4, starting transfers between devices, fetch(): return lax.ppermute(value, AXES, pairs)  14.1 us
    ppermute x2, starting transfers between devices, collect(): return lax.ppermute(shard, AXES, pairs)  12.6 us
    ppermute x4, waiting for transfers between devices, fetch(): return lax.ppermute(value, AXES, pairs)  6.64 us
    pallas_call x5, Pallas kernels, put(): pl.pallas_call(kernel, out_shape=jax.ShapeDtypeStruct(shape, dtype), in_s...  6.26 us
    ppermute x2, waiting for transfers between devices, collect(): return lax.ppermute(shard, AXES, pairs)  5.12 us
    pallas_call x1, Pallas kernels, keep(): pl.pallas_call(keep_kernel, out_shape=jax.ShapeDtypeStruct(error.shape, j...  2.3 us
  transfers between devices with their start and end apart: 11, of which 6 were waited for; matrix products, arithmetic and copies ran while one was open for 0% of the time, Pallas kernels for 10%

profile of v12, /device:TPU:1, one launch (start us, length us, event | category | flops | bytes accessed | tf_op | source)
XLA Modules:
  0.0 88.2 jit_solution(5252432360512227790)
XLA Ops:
  0.6 1.8 %shard_map.84 = (f32[16,8,384]{2,1,0:T(8,128)S(1)}, f32[512,256]{1,0:T(8,128)S(1)}, f32[512,256]{1,0:T(8,128)S(1)}) custom-call(s32[1,8]{1,0:T(1,128)} %picks_hbm.3, f32[512,256]{1,0:T(8,128)} %bitcast.12, f32[512,256]{1,0:T(8,128)} %bitcast.14, f32[512,256]{1,0:T(8,128)} %momentum.1, f32[512,256]{1,0:T(8,128)} %params.1), custom_call_target="tpu_custom_call" | custom-call | flops 100000 | bytes 2000000 | tf_op jit(solution)/shard_map/pallas_call | solution.py:116
  2.5 17.7 %all_to_all.5 = f32[16,8,384]{2,1,0:T(8,128)S(1)} all-to-all(f32[16,8,384]{2,1,0:T(8,128)S(1)} %get-tuple-element.25), channel_id=1, replica_groups=mesh['rep'=16,'fsdp'=32] {'rep'}, dimensions={0} | all-to-all | bytes 393216 | tf_op jit(solution)/shard_map/all_to_all | solution.py:306
  20.2 0.4 shard_map.85
  20.6 4.0 %collective-permute-start = (bf16[512,256]{1,0:T(8,128)(2,1)S(1)}, bf16[512,256]{1,0:T(8,128)(2,1)S(1)}, u32[]{:S(2)}, u32[]{:S(2)}) collective-permute-start(bf16[512,256]{1,0:T(8,128)(2,1)S(1)} %shard_map.85), channel_id=1, source_target_pairs={{2,0},{11,1},{8,2},{1,3},{14,4},{7,5},{4,6},{13,7},{10,8},{3,9},{0... | collective-permute-start | bytes 786440 | tf_op jit(solution)/shard_map/ppermute | solution.py:52
  24.7 8.6 %collective-permute-start.1 = (bf16[512,256]{1,0:T(8,128)(2,1)S(1)}, bf16[512,256]{1,0:T(8,128)(2,1)S(1)}, u32[]{:S(2)}, u32[]{:S(2)}) collective-permute-start(bf16[512,256]{1,0:T(8,128)(2,1)S(1)} %shard_map.85), channel_id=1, source_target_pairs={{48,0},{57,1},{54,2},{63,3},{60,4},{53,5},{50,6},{59,7},{56,8},{49... | collective-permute-start | bytes 786440 | tf_op jit(solution)/shard_map/ppermute | solution.py:52
  33.3 2.3 %shard_map.86 = f32[512,256]{1,0:T(8,128)} custom-call(s32[1,8]{1,0:T(1,128)} %picks_hbm.3, f32[512,256]{1,0:T(8,128)} %bitcast.13, f32[512,256]{1,0:T(8,128)} %bitcast.15), custom_call_target="tpu_custom_call" | custom-call | flops 1000000 | bytes 2000000 | tf_op jit(solution)/shard_map/pallas_call | solution.py:157
  35.6 1.4 %shard_map.87 = (f32[512,256]{1,0:T(8,128)}, f32[512,256]{1,0:T(8,128)}) custom-call(f32[128,384]{1,0:T(8,128)S(1)} %bitcast.10, f32[512,256]{1,0:T(8,128)S(1)} %get-tuple-element.26.momentum, f32[512,256]{1,0:T(8,128)S(1)} %get-tuple-element.27.params), custom_call_target="tpu_custom_call" | custom-call | flops 100000000 | bytes 3000000 | tf_op jit(solution)/shard_map/pallas_call | solution.py:205
  36.9 0.0 collective-permute-done
  36.9 5.1 %collective-permute-done.1 = bf16[512,256]{1,0:T(8,128)(2,1)S(1)} collective-permute-done((bf16[512,256]{1,0:T(8,128)(2,1)S(1)}, bf16[512,256]{1,0:T(8,128)(2,1)S(1)}, u32[]{:S(2)}, u32[]{:S(2)}) %collective-permute-start.1) | collective-permute-done | bytes 262176 | tf_op jit(solution)/shard_map/ppermute | solution.py:52
  42.1 0.1 pad_maximum_fusion.3
  42.1 5.3 %collective-permute-start.3 = (bf16[2,512,256]{2,1,0:T(8,128)(2,1)S(1)}, bf16[2,512,256]{2,1,0:T(8,128)(2,1)S(1)}, u32[]{:S(2)}, u32[]{:S(2)}) collective-permute-start(bf16[2,512,256]{2,1,0:T(8,128)(2,1)S(1)} %pad_maximum_fusion.3), channel_id=1, source_target_pairs={{1,0},{0,1},{3,2},{2,3},{5,4},{4,5},{7,6},{6,7},{9,8},{8,9},{11,10... | collective-permute-start | bytes 1572872 | tf_op jit(solution)/shard_map/ppermute | solution.py:43
  47.4 4.0 %collective-permute-start.2 = (bf16[2,512,256]{2,1,0:T(8,128)(2,1)S(1)}, bf16[2,512,256]{2,1,0:T(8,128)(2,1)S(1)}, u32[]{:S(2)}, u32[]{:S(2)}) collective-permute-start(bf16[2,512,256]{2,1,0:T(8,128)(2,1)S(1)} %pad_maximum_fusion.3), channel_id=1, source_target_pairs={{32,0},{49,1},{34,2},{51,3},{36,4},{53,5},{38,6},{55,7},{40,8},{57... | collective-permute-start | bytes 1572872 | tf_op jit(solution)/shard_map/ppermute | solution.py:38
  51.4 0.0 collective-permute-done.3
  51.4 0.1 pad_maximum_fusion.1.refs_0_
  51.5 3.6 %collective-permute-start.4 = (bf16[4,512,256]{2,1,0:T(8,128)(2,1)S(1)}, bf16[4,512,256]{2,1,0:T(8,128)(2,1)S(1)}, u32[]{:S(2)}, u32[]{:S(2)}) collective-permute-start(bf16[4,512,256]{2,1,0:T(8,128)(2,1)S(1)} %pad_maximum_fusion.1.refs_0_), channel_id=1, source_target_pairs={{64,0},{449,1},{66,2},{451,3},{68,4},{453,5},{70,6},{455,7},{72,8}... | collective-permute-start | bytes 3145736 | tf_op jit(solution)/shard_map/ppermute | solution.py:38
  55.1 3.5 %collective-permute-start.5 = (bf16[4,512,256]{2,1,0:T(8,128)(2,1)S(1)}, bf16[4,512,256]{2,1,0:T(8,128)(2,1)S(1)}, u32[]{:S(2)}, u32[]{:S(2)}) collective-permute-start(bf16[4,512,256]{2,1,0:T(8,128)(2,1)S(1)} %pad_maximum_fusion.1.refs_0_), channel_id=1, source_target_pairs={{2,0},{15,1},{4,2},{1,3},{6,4},{3,5},{8,6},{5,7},{10,8},{7,9},{12,... | collective-permute-start | bytes 3145736 | tf_op jit(solution)/shard_map/ppermute | solution.py:38
  58.5 0.5 collective-permute-done.2.refs_1_
  59.0 0.1 pad_maximum_fusion.2
  59.1 3.1 %collective-permute-start.6 = (bf16[4,512,256]{2,1,0:T(8,128)(2,1)S(1)}, bf16[4,512,256]{2,1,0:T(8,128)(2,1)S(1)}, u32[]{:S(2)}, u32[]{:S(2)}) collective-permute-start(bf16[4,512,256]{2,1,0:T(8,128)(2,1)S(1)} %pad_maximum_fusion.2), channel_id=1, source_target_pairs={{32,0},{49,1},{34,2},{51,3},{36,4},{53,5},{38,6},{55,7},{40,8},{57... | collective-permute-start | bytes 3145736 | tf_op jit(solution)/shard_map/ppermute | solution.py:38
  62.2 6.0 %collective-permute-done.4.refs_2_ = bf16[4,512,256]{2,1,0:T(8,128)(2,1)S(1)} collective-permute-done((bf16[4,512,256]{2,1,0:T(8,128)(2,1)S(1)}, bf16[4,512,256]{2,1,0:T(8,128)(2,1)S(1)}, u32[]{:S(2)}, u32[]{:S(2)}) %collective-permute-start.4) | collective-permute-done | bytes 1048608 | tf_op jit(solution)/shard_map/ppermute | solution.py:38
  68.3 3.4 %collective-permute-start.7 = (bf16[2,512,256]{2,1,0:T(8,128)(2,1)S(1)}, bf16[2,512,256]{2,1,0:T(8,128)(2,1)S(1)}, u32[]{:S(2)}, u32[]{:S(2)}) collective-permute-start(bf16[2,512,256]{2,1,0:T(8,128)(2,1)S(1)} %slice.16), channel_id=1, source_target_pairs={{1,0},{0,1},{3,2},{2,3},{5,4},{4,5},{7,6},{6,7},{9,8},{8,9},{11,10... | collective-permute-start | bytes 1572872 | tf_op jit(solution)/shard_map/ppermute | solution.py:43
  71.7 0.1 collective-permute-done.5.refs_4_
  71.8 4.8 %collective-permute-start.8 = (bf16[2,512,256]{2,1,0:T(8,128)(2,1)S(1)}, bf16[2,512,256]{2,1,0:T(8,128)(2,1)S(1)}, u32[]{:S(2)}, u32[]{:S(2)}) collective-permute-start(bf16[2,512,256]{2,1,0:T(8,128)(2,1)S(1)} %slice.17), channel_id=1, source_target_pairs={{1,0},{0,1},{3,2},{2,3},{5,4},{4,5},{7,6},{6,7},{9,8},{8,9},{11,10... | collective-permute-start | bytes 1572872 | tf_op jit(solution)/shard_map/ppermute | solution.py:43
  76.6 1.0 %shard_map.88.refs_0_ = bf16[16,2,512,256]{3,2,1,0:T(8,128)(2,1)} custom-call(bf16[4,512,256]{2,1,0:T(8,128)(2,1)S(1)} %pad_maximum_fusion.1.refs_0_), custom_call_target="tpu_custom_call" | custom-call | bytes 2097152 | tf_op jit(solution)/shard_map/pallas_call | solution.py:250
  77.7 0.0 collective-permute-done.7.refs_3_
  77.7 0.5 collective-permute-done.8.refs_5_
  78.1 1.9 %shard_map.89.refs_0_ = bf16[16,2,512,256]{3,2,1,0:T(8,128)(2,1)} custom-call(bf16[16,2,512,256]{3,2,1,0:T(8,128)(2,1)} %shard_map.88.refs_0_, bf16[2,512,256]{2,1,0:T(8,128)(2,1)S(1)} %collective-permute-done.2.refs_1_, bf16[4,512,256]{2,1,0:T(8,128)(2,1)S(1)} %collective-permute-done.4.refs_2_, ...), custom_call_target="tpu_custom_call", output_to_operand_aliasing={{}: (0, {})} | custom-call | bytes 7340032 | tf_op jit(solution)/shard_map/pallas_call | solution.py:250
  80.1 0.0 collective-permute-done.6.refs_1_
  80.2 0.2 pad_maximum_fusion
  80.4 2.3 %collective-permute-start.9 = (bf16[6,512,256]{2,1,0:T(8,128)(2,1)S(1)}, bf16[6,512,256]{2,1,0:T(8,128)(2,1)S(1)}, u32[]{:S(2)}, u32[]{:S(2)}) collective-permute-start(bf16[6,512,256]{2,1,0:T(8,128)(2,1)S(1)} %pad_maximum_fusion), channel_id=1, source_target_pairs={{1,0},{0,1},{3,2},{2,3},{5,4},{4,5},{7,6},{6,7},{9,8},{8,9},{11,10... | collective-permute-start | bytes 4718600 | tf_op jit(solution)/shard_map/ppermute | solution.py:43
  82.7 2.0 %collective-permute-start.10 = (bf16[4,512,256]{2,1,0:T(8,128)(2,1)S(1)}, bf16[4,512,256]{2,1,0:T(8,128)(2,1)S(1)}, u32[]{:S(2)}, u32[]{:S(2)}) collective-permute-start(bf16[4,512,256]{2,1,0:T(8,128)(2,1)S(1)} %collective-permute-done.6.refs_1_), channel_id=1, source_target_pairs={{1,0},{0,1},{3,2},{2,3},{5,4},{4,5},{7,6},{6,7},{9,8},{8,9},{11,10... | collective-permute-start | bytes 3145736 | tf_op jit(solution)/shard_map/ppermute | solution.py:43
  84.7 1.0 %shard_map.90.refs_0_ = bf16[16,2,512,256]{3,2,1,0:T(8,128)(2,1)} custom-call(bf16[16,2,512,256]{3,2,1,0:T(8,128)(2,1)} %shard_map.89.refs_0_, bf16[4,512,256]{2,1,0:T(8,128)(2,1)S(1)} %collective-permute-done.6.refs_1_), custom_call_target="tpu_custom_call", output_to_operand_aliasing={{}: (0, {})} | custom-call | bytes 2097152 | tf_op jit(solution)/shard_map/pallas_call | solution.py:250
  85.8 0.0 collective-permute-done.9.refs_1_
  85.8 1.2 %shard_map.91.refs_0_ = bf16[16,2,512,256]{3,2,1,0:T(8,128)(2,1)} custom-call(bf16[16,2,512,256]{3,2,1,0:T(8,128)(2,1)} %shard_map.90.refs_0_, bf16[6,512,256]{2,1,0:T(8,128)(2,1)S(1)} %collective-permute-done.9.refs_1_), custom_call_target="tpu_custom_call", output_to_operand_aliasing={{}: (0, {})} | custom-call | bytes 3145728 | tf_op jit(solution)/shard_map/pallas_call | solution.py:250
  87.0 0.2 collective-permute-done.10.refs_1_
  87.2 1.0 %shard_map.92 = bf16[16,2,512,256]{3,2,1,0:T(8,128)(2,1)} custom-call(bf16[16,2,512,256]{3,2,1,0:T(8,128)(2,1)} %shard_map.91.refs_0_, bf16[4,512,256]{2,1,0:T(8,128)(2,1)S(1)} %collective-permute-done.10.refs_1_), custom_call_target="tpu_custom_call", output_to_operand_aliasing={{}: (0, {})} | custom-call | bytes 2097152 | tf_op jit(solution)/shard_map/pallas_call | solution.py:250
  (4 shorter events, 0.1 us)
Async XLA Ops:
  20.6 16.3 %collective-permute-start = (bf16[512,256]{1,0:T(8,128)(2,1)S(1)}, bf16[512,256]{1,0:T(8,128)(2,1)S(1)}, u32[]{:S(2)}, u32[]{:S(2)}) collective-permute-start(bf16[512,256]{1,0:T(8,128)(2,1)S(1)} %shard_map.85), channel_id=1, source_target_pairs={{2,0},{11,1},{8,2},{1,3},{14,4},{7,5},{4,6},{13,7},{10,8},{3,9},{0... | collective-permute-start | bytes 786440 | tf_op jit(solution)/shard_map/ppermute | solution.py:52
  24.7 17.4 %collective-permute-start.1 = (bf16[512,256]{1,0:T(8,128)(2,1)S(1)}, bf16[512,256]{1,0:T(8,128)(2,1)S(1)}, u32[]{:S(2)}, u32[]{:S(2)}) collective-permute-start(bf16[512,256]{1,0:T(8,128)(2,1)S(1)} %shard_map.85), channel_id=1, source_target_pairs={{48,0},{57,1},{54,2},{63,3},{60,4},{53,5},{50,6},{59,7},{56,8},{49... | collective-permute-start | bytes 786440 | tf_op jit(solution)/shard_map/ppermute | solution.py:52
  42.1 9.2 %collective-permute-start.3 = (bf16[2,512,256]{2,1,0:T(8,128)(2,1)S(1)}, bf16[2,512,256]{2,1,0:T(8,128)(2,1)S(1)}, u32[]{:S(2)}, u32[]{:S(2)}) collective-permute-start(bf16[2,512,256]{2,1,0:T(8,128)(2,1)S(1)} %pad_maximum_fusion.3), channel_id=1, source_target_pairs={{1,0},{0,1},{3,2},{2,3},{5,4},{4,5},{7,6},{6,7},{9,8},{8,9},{11,10... | collective-permute-start | bytes 1572872 | tf_op jit(solution)/shard_map/ppermute | solution.py:43
  47.4 11.6 %collective-permute-start.2 = (bf16[2,512,256]{2,1,0:T(8,128)(2,1)S(1)}, bf16[2,512,256]{2,1,0:T(8,128)(2,1)S(1)}, u32[]{:S(2)}, u32[]{:S(2)}) collective-permute-start(bf16[2,512,256]{2,1,0:T(8,128)(2,1)S(1)} %pad_maximum_fusion.3), channel_id=1, source_target_pairs={{32,0},{49,1},{34,2},{51,3},{36,4},{53,5},{38,6},{55,7},{40,8},{57... | collective-permute-start | bytes 1572872 | tf_op jit(solution)/shard_map/ppermute | solution.py:38
  51.5 16.8 %collective-permute-start.4 = (bf16[4,512,256]{2,1,0:T(8,128)(2,1)S(1)}, bf16[4,512,256]{2,1,0:T(8,128)(2,1)S(1)}, u32[]{:S(2)}, u32[]{:S(2)}) collective-permute-start(bf16[4,512,256]{2,1,0:T(8,128)(2,1)S(1)} %pad_maximum_fusion.1.refs_0_), channel_id=1, source_target_pairs={{64,0},{449,1},{66,2},{451,3},{68,4},{453,5},{70,6},{455,7},{72,8}... | collective-permute-start | bytes 3145736 | tf_op jit(solution)/shard_map/ppermute | solution.py:38
  55.1 16.8 %collective-permute-start.5 = (bf16[4,512,256]{2,1,0:T(8,128)(2,1)S(1)}, bf16[4,512,256]{2,1,0:T(8,128)(2,1)S(1)}, u32[]{:S(2)}, u32[]{:S(2)}) collective-permute-start(bf16[4,512,256]{2,1,0:T(8,128)(2,1)S(1)} %pad_maximum_fusion.1.refs_0_), channel_id=1, source_target_pairs={{2,0},{15,1},{4,2},{1,3},{6,4},{3,5},{8,6},{5,7},{10,8},{7,9},{12,... | collective-permute-start | bytes 3145736 | tf_op jit(solution)/shard_map/ppermute | solution.py:38
  59.1 21.0 %collective-permute-start.6 = (bf16[4,512,256]{2,1,0:T(8,128)(2,1)S(1)}, bf16[4,512,256]{2,1,0:T(8,128)(2,1)S(1)}, u32[]{:S(2)}, u32[]{:S(2)}) collective-permute-start(bf16[4,512,256]{2,1,0:T(8,128)(2,1)S(1)} %pad_maximum_fusion.2), channel_id=1, source_target_pairs={{32,0},{49,1},{34,2},{51,3},{36,4},{53,5},{38,6},{55,7},{40,8},{57... | collective-permute-start | bytes 3145736 | tf_op jit(solution)/shard_map/ppermute | solution.py:38
  68.3 9.4 %collective-permute-start.7 = (bf16[2,512,256]{2,1,0:T(8,128)(2,1)S(1)}, bf16[2,512,256]{2,1,0:T(8,128)(2,1)S(1)}, u32[]{:S(2)}, u32[]{:S(2)}) collective-permute-start(bf16[2,512,256]{2,1,0:T(8,128)(2,1)S(1)} %slice.16), channel_id=1, source_target_pairs={{1,0},{0,1},{3,2},{2,3},{5,4},{4,5},{7,6},{6,7},{9,8},{8,9},{11,10... | collective-permute-start | bytes 1572872 | tf_op jit(solution)/shard_map/ppermute | solution.py:43
  71.8 6.3 %collective-permute-start.8 = (bf16[2,512,256]{2,1,0:T(8,128)(2,1)S(1)}, bf16[2,512,256]{2,1,0:T(8,128)(2,1)S(1)}, u32[]{:S(2)}, u32[]{:S(2)}) collective-permute-start(bf16[2,512,256]{2,1,0:T(8,128)(2,1)S(1)} %slice.17), channel_id=1, source_target_pairs={{1,0},{0,1},{3,2},{2,3},{5,4},{4,5},{7,6},{6,7},{9,8},{8,9},{11,10... | collective-permute-start | bytes 1572872 | tf_op jit(solution)/shard_map/ppermute | solution.py:43
  80.4 5.4 %collective-permute-start.9 = (bf16[6,512,256]{2,1,0:T(8,128)(2,1)S(1)}, bf16[6,512,256]{2,1,0:T(8,128)(2,1)S(1)}, u32[]{:S(2)}, u32[]{:S(2)}) collective-permute-start(bf16[6,512,256]{2,1,0:T(8,128)(2,1)S(1)} %pad_maximum_fusion), channel_id=1, source_target_pairs={{1,0},{0,1},{3,2},{2,3},{5,4},{4,5},{7,6},{6,7},{9,8},{8,9},{11,10... | collective-permute-start | bytes 4718600 | tf_op jit(solution)/shard_map/ppermute | solution.py:43
  82.7 4.6 %collective-permute-start.10 = (bf16[4,512,256]{2,1,0:T(8,128)(2,1)S(1)}, bf16[4,512,256]{2,1,0:T(8,128)(2,1)S(1)}, u32[]{:S(2)}, u32[]{:S(2)}) collective-permute-start(bf16[4,512,256]{2,1,0:T(8,128)(2,1)S(1)} %collective-permute-done.6.refs_1_), channel_id=1, source_target_pairs={{1,0},{0,1},{3,2},{2,3},{5,4},{4,5},{7,6},{6,7},{9,8},{8,9},{11,10... | collective-permute-start | bytes 3145736 | tf_op jit(solution)/shard_map/ppermute | solution.py:43

commit v13 on v12

--- a/solution.py
+++ b/solution.py
@@ -278,8 +278,10 @@
     portion = jnp.concatenate([half, swap(half)], axis=0)
     near_y, near_z = fetch(portion, Y), fetch(portion, Z)
     far_x = fetch(jnp.concatenate(lax.optimization_barrier((portion[2:], near_x)), axis=0), X)
-    whole = put(None, [(portion, 0, 4, 0, HERE, False)], shape, shard.dtype)
-    pieces = [(near_x, 0, 2, 0, X, False)]
+    pieces = [(portion, 0, 4, 0, HERE, False), (near_x, 0, 2, 0, X, False)]
+    whole = put(None, pieces, shape, shard.dtype)
+    near_y, whole = lax.optimization_barrier((near_y, whole))
+    pieces = []
     for array, offsets in ((near_y, Y), (near_z, Z)):
         pieces += [(array, 0, 4, 0, offsets, False), (swap(array[:2]), 0, 2, 0, offsets, True)]
     whole = put(whole, pieces, shape, shard.dtype)

time: 88.7 us -> 88.5 us (level)
    ppermute x4, waiting for transfers between devices: 6.64 us -> 5.35 us  [fetch(): return lax.ppermute(value, AXES, pairs)]
    ppermute x5, waiting for transfers between devices: 0.65 us -> 1.7 us  [swap(): return lax.ppermute(value, AXES, pairs)]
where the time goes in v13:
time: 88.5 us; the launch traced here: 88 us
  starting transfers between devices  44.5 us (50%)
  blocking collectives  17.7 us (20%)
  Pallas kernels  12.2 us (14%)
  waiting for transfers between devices  12.2 us (14%)
    ppermute x5, starting transfers between devices, swap(): return lax.ppermute(value, AXES, pairs)  17.8 us
    all_to_all x1, blocking collectives, per_device(): lax.all_to_all(payload, 'rep', 0, 0).reshape(-1, payload.shape[-1])  17.7 us
    ppermute x4, starting transfers between devices, fetch(): return lax.ppermute(value, AXES, pairs)  14.1 us
    ppermute x2, starting transfers between devices, collect(): return lax.ppermute(shard, AXES, pairs)  12.6 us
    pallas_call x5, Pallas kernels, put(): pl.pallas_call(kernel, out_shape=jax.ShapeDtypeStruct(shape, dtype), in_s...  6.26 us
    ppermute x4, waiting for transfers between devices, fetch(): return lax.ppermute(value, AXES, pairs)  5.35 us
    ppermute x2, waiting for transfers between devices, collect(): return lax.ppermute(shard, AXES, pairs)  5.12 us
    pallas_call x1, Pallas kernels, keep(): pl.pallas_call(keep_kernel, out_shape=jax.ShapeDtypeStruct(error.shape, j...  2.3 us
  transfers between devices with their start and end apart: 11, of which 6 were waited for; matrix products, arithmetic and copies ran while one was open for 0% of the time, Pallas kernels for 10%

profile of v13, /device:TPU:1, one launch (start us, length us, event | category | flops | bytes accessed | tf_op | source)
XLA Modules:
  0.0 88.0 jit_solution(9501929709457253533)
XLA Ops:
  0.6 1.8 %shard_map.84 = (f32[16,8,384]{2,1,0:T(8,128)S(1)}, f32[512,256]{1,0:T(8,128)S(1)}, f32[512,256]{1,0:T(8,128)S(1)}) custom-call(s32[1,8]{1,0:T(1,128)} %picks_hbm.3, f32[512,256]{1,0:T(8,128)} %bitcast.12, f32[512,256]{1,0:T(8,128)} %bitcast.14, f32[512,256]{1,0:T(8,128)} %momentum.1, f32[512,256]{1,0:T(8,128)} %params.1), custom_call_target="tpu_custom_call" | custom-call | flops 100000 | bytes 2000000 | tf_op jit(solution)/shard_map/pallas_call | solution.py:116
  2.5 17.7 %all_to_all.5 = f32[16,8,384]{2,1,0:T(8,128)S(1)} all-to-all(f32[16,8,384]{2,1,0:T(8,128)S(1)} %get-tuple-element.27), channel_id=1, replica_groups=mesh['rep'=16,'fsdp'=32] {'rep'}, dimensions={0} | all-to-all | bytes 393216 | tf_op jit(solution)/shard_map/all_to_all | solution.py:308
  20.2 0.4 shard_map.85
  20.6 4.0 %collective-permute-start = (bf16[512,256]{1,0:T(8,128)(2,1)S(1)}, bf16[512,256]{1,0:T(8,128)(2,1)S(1)}, u32[]{:S(2)}, u32[]{:S(2)}) collective-permute-start(bf16[512,256]{1,0:T(8,128)(2,1)S(1)} %shard_map.85), channel_id=1, source_target_pairs={{2,0},{11,1},{8,2},{1,3},{14,4},{7,5},{4,6},{13,7},{10,8},{3,9},{0... | collective-permute-start | bytes 786440 | tf_op jit(solution)/shard_map/ppermute | solution.py:52
  24.7 8.6 %collective-permute-start.1 = (bf16[512,256]{1,0:T(8,128)(2,1)S(1)}, bf16[512,256]{1,0:T(8,128)(2,1)S(1)}, u32[]{:S(2)}, u32[]{:S(2)}) collective-permute-start(bf16[512,256]{1,0:T(8,128)(2,1)S(1)} %shard_map.85), channel_id=1, source_target_pairs={{48,0},{57,1},{54,2},{63,3},{60,4},{53,5},{50,6},{59,7},{56,8},{49... | collective-permute-start | bytes 786440 | tf_op jit(solution)/shard_map/ppermute | solution.py:52
  33.3 2.3 %shard_map.86 = f32[512,256]{1,0:T(8,128)} custom-call(s32[1,8]{1,0:T(1,128)} %picks_hbm.3, f32[512,256]{1,0:T(8,128)} %bitcast.13, f32[512,256]{1,0:T(8,128)} %bitcast.15), custom_call_target="tpu_custom_call" | custom-call | flops 1000000 | bytes 2000000 | tf_op jit(solution)/shard_map/pallas_call | solution.py:157
  35.6 1.4 %shard_map.87 = (f32[512,256]{1,0:T(8,128)}, f32[512,256]{1,0:T(8,128)}) custom-call(f32[128,384]{1,0:T(8,128)S(1)} %bitcast.10, f32[512,256]{1,0:T(8,128)S(1)} %get-tuple-element.28.momentum, f32[512,256]{1,0:T(8,128)S(1)} %get-tuple-element.29.params), custom_call_target="tpu_custom_call" | custom-call | flops 100000000 | bytes 3000000 | tf_op jit(solution)/shard_map/pallas_call | solution.py:205
  36.9 0.0 collective-permute-done
  36.9 5.1 %collective-permute-done.1 = bf16[512,256]{1,0:T(8,128)(2,1)S(1)} collective-permute-done((bf16[512,256]{1,0:T(8,128)(2,1)S(1)}, bf16[512,256]{1,0:T(8,128)(2,1)S(1)}, u32[]{:S(2)}, u32[]{:S(2)}) %collective-permute-start.1) | collective-permute-done | bytes 262176 | tf_op jit(solution)/shard_map/ppermute | solution.py:52
  42.1 0.1 pad_maximum_fusion.3
  42.1 5.3 %collective-permute-start.3 = (bf16[2,512,256]{2,1,0:T(8,128)(2,1)S(1)}, bf16[2,512,256]{2,1,0:T(8,128)(2,1)S(1)}, u32[]{:S(2)}, u32[]{:S(2)}) collective-permute-start(bf16[2,512,256]{2,1,0:T(8,128)(2,1)S(1)} %pad_maximum_fusion.3), channel_id=1, source_target_pairs={{1,0},{0,1},{3,2},{2,3},{5,4},{4,5},{7,6},{6,7},{9,8},{8,9},{11,10... | collective-permute-start | bytes 1572872 | tf_op jit(solution)/shard_map/ppermute | solution.py:43
  47.4 4.0 %collective-permute-start.2 = (bf16[2,512,256]{2,1,0:T(8,128)(2,1)S(1)}, bf16[2,512,256]{2,1,0:T(8,128)(2,1)S(1)}, u32[]{:S(2)}, u32[]{:S(2)}) collective-permute-start(bf16[2,512,256]{2,1,0:T(8,128)(2,1)S(1)} %pad_maximum_fusion.3), channel_id=1, source_target_pairs={{32,0},{49,1},{34,2},{51,3},{36,4},{53,5},{38,6},{55,7},{40,8},{57... | collective-permute-start | bytes 1572872 | tf_op jit(solution)/shard_map/ppermute | solution.py:38
  51.4 0.0 collective-permute-done.3
  51.4 0.1 pad_maximum_fusion.1.refs_0_
  51.5 3.6 %collective-permute-start.4 = (bf16[4,512,256]{2,1,0:T(8,128)(2,1)S(1)}, bf16[4,512,256]{2,1,0:T(8,128)(2,1)S(1)}, u32[]{:S(2)}, u32[]{:S(2)}) collective-permute-start(bf16[4,512,256]{2,1,0:T(8,128)(2,1)S(1)} %pad_maximum_fusion.1.refs_0_), channel_id=1, source_target_pairs={{64,0},{449,1},{66,2},{451,3},{68,4},{453,5},{70,6},{455,7},{72,8}... | collective-permute-start | bytes 3145736 | tf_op jit(solution)/shard_map/ppermute | solution.py:38
  55.1 3.5 %collective-permute-start.5 = (bf16[4,512,256]{2,1,0:T(8,128)(2,1)S(1)}, bf16[4,512,256]{2,1,0:T(8,128)(2,1)S(1)}, u32[]{:S(2)}, u32[]{:S(2)}) collective-permute-start(bf16[4,512,256]{2,1,0:T(8,128)(2,1)S(1)} %pad_maximum_fusion.1.refs_0_), channel_id=1, source_target_pairs={{2,0},{15,1},{4,2},{1,3},{6,4},{3,5},{8,6},{5,7},{10,8},{7,9},{12,... | collective-permute-start | bytes 3145736 | tf_op jit(solution)/shard_map/ppermute | solution.py:38
  58.5 0.5 collective-permute-done.2.refs_1_
  59.0 0.1 pad_maximum_fusion.2
  59.1 3.1 %collective-permute-start.6 = (bf16[4,512,256]{2,1,0:T(8,128)(2,1)S(1)}, bf16[4,512,256]{2,1,0:T(8,128)(2,1)S(1)}, u32[]{:S(2)}, u32[]{:S(2)}) collective-permute-start(bf16[4,512,256]{2,1,0:T(8,128)(2,1)S(1)} %pad_maximum_fusion.2), channel_id=1, source_target_pairs={{32,0},{49,1},{34,2},{51,3},{36,4},{53,5},{38,6},{55,7},{40,8},{57... | collective-permute-start | bytes 3145736 | tf_op jit(solution)/shard_map/ppermute | solution.py:38
  62.2 1.2 %shard_map.88.refs_0_ = bf16[16,2,512,256]{3,2,1,0:T(8,128)(2,1)} custom-call(bf16[4,512,256]{2,1,0:T(8,128)(2,1)S(1)} %pad_maximum_fusion.1.refs_0_, bf16[2,512,256]{2,1,0:T(8,128)(2,1)S(1)} %collective-permute-done.2.refs_1_), custom_call_target="tpu_custom_call" | custom-call | bytes 3145728 | tf_op jit(solution)/shard_map/pallas_call | solution.py:250
  63.5 4.7 %collective-permute-done.4.refs_1_ = bf16[4,512,256]{2,1,0:T(8,128)(2,1)S(1)} collective-permute-done((bf16[4,512,256]{2,1,0:T(8,128)(2,1)S(1)}, bf16[4,512,256]{2,1,0:T(8,128)(2,1)S(1)}, u32[]{:S(2)}, u32[]{:S(2)}) %collective-permute-start.4) | collective-permute-done | bytes 1048608 | tf_op jit(solution)/shard_map/ppermute | solution.py:38
  68.3 3.4 %collective-permute-start.7 = (bf16[2,512,256]{2,1,0:T(8,128)(2,1)S(1)}, bf16[2,512,256]{2,1,0:T(8,128)(2,1)S(1)}, u32[]{:S(2)}, u32[]{:S(2)}) collective-permute-start(bf16[2,512,256]{2,1,0:T(8,128)(2,1)S(1)} %slice.12), channel_id=1, source_target_pairs={{1,0},{0,1},{3,2},{2,3},{5,4},{4,5},{7,6},{6,7},{9,8},{8,9},{11,10... | collective-permute-start | bytes 1572872 | tf_op jit(solution)/shard_map/ppermute | solution.py:43
  71.7 0.1 collective-permute-done.5.refs_3_
  71.8 4.8 %collective-permute-start.8 = (bf16[2,512,256]{2,1,0:T(8,128)(2,1)S(1)}, bf16[2,512,256]{2,1,0:T(8,128)(2,1)S(1)}, u32[]{:S(2)}, u32[]{:S(2)}) collective-permute-start(bf16[2,512,256]{2,1,0:T(8,128)(2,1)S(1)} %slice.16), channel_id=1, source_target_pairs={{1,0},{0,1},{3,2},{2,3},{5,4},{4,5},{7,6},{6,7},{9,8},{8,9},{11,10... | collective-permute-start | bytes 1572872 | tf_op jit(solution)/shard_map/ppermute | solution.py:43
  76.6 0.0 collective-permute-done.7.refs_2_
  76.6 1.5 %collective-permute-done.8.refs_4_ = bf16[2,512,256]{2,1,0:T(8,128)(2,1)S(1)} collective-permute-done((bf16[2,512,256]{2,1,0:T(8,128)(2,1)S(1)}, bf16[2,512,256]{2,1,0:T(8,128)(2,1)S(1)}, u32[]{:S(2)}, u32[]{:S(2)}) %collective-permute-start.8) | collective-permute-done | bytes 524320 | tf_op jit(solution)/shard_map/ppermute | solution.py:43
  78.1 1.8 %shard_map.89.refs_0_ = bf16[16,2,512,256]{3,2,1,0:T(8,128)(2,1)} custom-call(bf16[16,2,512,256]{3,2,1,0:T(8,128)(2,1)} %shard_map.88.refs_0_, bf16[4,512,256]{2,1,0:T(8,128)(2,1)S(1)} %collective-permute-done.4.refs_1_, bf16[2,512,256]{2,1,0:T(8,128)(2,1)S(1)} %collective-permute-done.7.refs_2_, ...), custom_call_target="tpu_custom_call", output_to_operand_aliasing={{}: (0, {})} | custom-call | bytes 6291456 | tf_op jit(solution)/shard_map/pallas_call | solution.py:250
  79.9 0.0 collective-permute-done.6.refs_1_
  80.0 0.2 pad_maximum_fusion
  80.2 2.3 %collective-permute-start.9 = (bf16[6,512,256]{2,1,0:T(8,128)(2,1)S(1)}, bf16[6,512,256]{2,1,0:T(8,128)(2,1)S(1)}, u32[]{:S(2)}, u32[]{:S(2)}) collective-permute-start(bf16[6,512,256]{2,1,0:T(8,128)(2,1)S(1)} %pad_maximum_fusion), channel_id=1, source_target_pairs={{1,0},{0,1},{3,2},{2,3},{5,4},{4,5},{7,6},{6,7},{9,8},{8,9},{11,10... | collective-permute-start | bytes 4718600 | tf_op jit(solution)/shard_map/ppermute | solution.py:43
  82.5 2.0 %collective-permute-start.10 = (bf16[4,512,256]{2,1,0:T(8,128)(2,1)S(1)}, bf16[4,512,256]{2,1,0:T(8,128)(2,1)S(1)}, u32[]{:S(2)}, u32[]{:S(2)}) collective-permute-start(bf16[4,512,256]{2,1,0:T(8,128)(2,1)S(1)} %collective-permute-done.6.refs_1_), channel_id=1, source_target_pairs={{1,0},{0,1},{3,2},{2,3},{5,4},{4,5},{7,6},{6,7},{9,8},{8,9},{11,10... | collective-permute-start | bytes 3145736 | tf_op jit(solution)/shard_map/ppermute | solution.py:43
  84.5 1.0 %shard_map.90.refs_0_ = bf16[16,2,512,256]{3,2,1,0:T(8,128)(2,1)} custom-call(bf16[16,2,512,256]{3,2,1,0:T(8,128)(2,1)} %shard_map.89.refs_0_, bf16[4,512,256]{2,1,0:T(8,128)(2,1)S(1)} %collective-permute-done.6.refs_1_), custom_call_target="tpu_custom_call", output_to_operand_aliasing={{}: (0, {})} | custom-call | bytes 2097152 | tf_op jit(solution)/shard_map/pallas_call | solution.py:250
  85.6 0.0 collective-permute-done.9.refs_1_
  85.6 1.2 %shard_map.91.refs_0_ = bf16[16,2,512,256]{3,2,1,0:T(8,128)(2,1)} custom-call(bf16[16,2,512,256]{3,2,1,0:T(8,128)(2,1)} %shard_map.90.refs_0_, bf16[6,512,256]{2,1,0:T(8,128)(2,1)S(1)} %collective-permute-done.9.refs_1_), custom_call_target="tpu_custom_call", output_to_operand_aliasing={{}: (0, {})} | custom-call | bytes 3145728 | tf_op jit(solution)/shard_map/pallas_call | solution.py:250
  86.8 0.2 collective-permute-done.10.refs_1_
  87.0 1.0 %shard_map.92 = bf16[16,2,512,256]{3,2,1,0:T(8,128)(2,1)} custom-call(bf16[16,2,512,256]{3,2,1,0:T(8,128)(2,1)} %shard_map.91.refs_0_, bf16[4,512,256]{2,1,0:T(8,128)(2,1)S(1)} %collective-permute-done.10.refs_1_), custom_call_target="tpu_custom_call", output_to_operand_aliasing={{}: (0, {})} | custom-call | bytes 2097152 | tf_op jit(solution)/shard_map/pallas_call | solution.py:250
  (4 shorter events, 0.1 us)
Async XLA Ops:
  20.6 16.3 %collective-permute-start = (bf16[512,256]{1,0:T(8,128)(2,1)S(1)}, bf16[512,256]{1,0:T(8,128)(2,1)S(1)}, u32[]{:S(2)}, u32[]{:S(2)}) collective-permute-start(bf16[512,256]{1,0:T(8,128)(2,1)S(1)} %shard_map.85), channel_id=1, source_target_pairs={{2,0},{11,1},{8,2},{1,3},{14,4},{7,5},{4,6},{13,7},{10,8},{3,9},{0... | collective-permute-start | bytes 786440 | tf_op jit(solution)/shard_map/ppermute | solution.py:52
  24.7 17.4 %collective-permute-start.1 = (bf16[512,256]{1,0:T(8,128)(2,1)S(1)}, bf16[512,256]{1,0:T(8,128)(2,1)S(1)}, u32[]{:S(2)}, u32[]{:S(2)}) collective-permute-start(bf16[512,256]{1,0:T(8,128)(2,1)S(1)} %shard_map.85), channel_id=1, source_target_pairs={{48,0},{57,1},{54,2},{63,3},{60,4},{53,5},{50,6},{59,7},{56,8},{49... | collective-permute-start | bytes 786440 | tf_op jit(solution)/shard_map/ppermute | solution.py:52
  42.1 9.2 %collective-permute-start.3 = (bf16[2,512,256]{2,1,0:T(8,128)(2,1)S(1)}, bf16[2,512,256]{2,1,0:T(8,128)(2,1)S(1)}, u32[]{:S(2)}, u32[]{:S(2)}) collective-permute-start(bf16[2,512,256]{2,1,0:T(8,128)(2,1)S(1)} %pad_maximum_fusion.3), channel_id=1, source_target_pairs={{1,0},{0,1},{3,2},{2,3},{5,4},{4,5},{7,6},{6,7},{9,8},{8,9},{11,10... | collective-permute-start | bytes 1572872 | tf_op jit(solution)/shard_map/ppermute | solution.py:43
  47.4 11.6 %collective-permute-start.2 = (bf16[2,512,256]{2,1,0:T(8,128)(2,1)S(1)}, bf16[2,512,256]{2,1,0:T(8,128)(2,1)S(1)}, u32[]{:S(2)}, u32[]{:S(2)}) collective-permute-start(bf16[2,512,256]{2,1,0:T(8,128)(2,1)S(1)} %pad_maximum_fusion.3), channel_id=1, source_target_pairs={{32,0},{49,1},{34,2},{51,3},{36,4},{53,5},{38,6},{55,7},{40,8},{57... | collective-permute-start | bytes 1572872 | tf_op jit(solution)/shard_map/ppermute | solution.py:38
  51.5 16.8 %collective-permute-start.4 = (bf16[4,512,256]{2,1,0:T(8,128)(2,1)S(1)}, bf16[4,512,256]{2,1,0:T(8,128)(2,1)S(1)}, u32[]{:S(2)}, u32[]{:S(2)}) collective-permute-start(bf16[4,512,256]{2,1,0:T(8,128)(2,1)S(1)} %pad_maximum_fusion.1.refs_0_), channel_id=1, source_target_pairs={{64,0},{449,1},{66,2},{451,3},{68,4},{453,5},{70,6},{455,7},{72,8}... | collective-permute-start | bytes 3145736 | tf_op jit(solution)/shard_map/ppermute | solution.py:38
  55.1 16.8 %collective-permute-start.5 = (bf16[4,512,256]{2,1,0:T(8,128)(2,1)S(1)}, bf16[4,512,256]{2,1,0:T(8,128)(2,1)S(1)}, u32[]{:S(2)}, u32[]{:S(2)}) collective-permute-start(bf16[4,512,256]{2,1,0:T(8,128)(2,1)S(1)} %pad_maximum_fusion.1.refs_0_), channel_id=1, source_target_pairs={{2,0},{15,1},{4,2},{1,3},{6,4},{3,5},{8,6},{5,7},{10,8},{7,9},{12,... | collective-permute-start | bytes 3145736 | tf_op jit(solution)/shard_map/ppermute | solution.py:38
  59.1 20.8 %collective-permute-start.6 = (bf16[4,512,256]{2,1,0:T(8,128)(2,1)S(1)}, bf16[4,512,256]{2,1,0:T(8,128)(2,1)S(1)}, u32[]{:S(2)}, u32[]{:S(2)}) collective-permute-start(bf16[4,512,256]{2,1,0:T(8,128)(2,1)S(1)} %pad_maximum_fusion.2), channel_id=1, source_target_pairs={{32,0},{49,1},{34,2},{51,3},{36,4},{53,5},{38,6},{55,7},{40,8},{57... | collective-permute-start | bytes 3145736 | tf_op jit(solution)/shard_map/ppermute | solution.py:38
  68.3 8.4 %collective-permute-start.7 = (bf16[2,512,256]{2,1,0:T(8,128)(2,1)S(1)}, bf16[2,512,256]{2,1,0:T(8,128)(2,1)S(1)}, u32[]{:S(2)}, u32[]{:S(2)}) collective-permute-start(bf16[2,512,256]{2,1,0:T(8,128)(2,1)S(1)} %slice.12), channel_id=1, source_target_pairs={{1,0},{0,1},{3,2},{2,3},{5,4},{4,5},{7,6},{6,7},{9,8},{8,9},{11,10... | collective-permute-start | bytes 1572872 | tf_op jit(solution)/shard_map/ppermute | solution.py:43
  71.8 6.3 %collective-permute-start.8 = (bf16[2,512,256]{2,1,0:T(8,128)(2,1)S(1)}, bf16[2,512,256]{2,1,0:T(8,128)(2,1)S(1)}, u32[]{:S(2)}, u32[]{:S(2)}) collective-permute-start(bf16[2,512,256]{2,1,0:T(8,128)(2,1)S(1)} %slice.16), channel_id=1, source_target_pairs={{1,0},{0,1},{3,2},{2,3},{5,4},{4,5},{7,6},{6,7},{9,8},{8,9},{11,10... | collective-permute-start | bytes 1572872 | tf_op jit(solution)/shard_map/ppermute | solution.py:43
  80.2 5.4 %collective-permute-start.9 = (bf16[6,512,256]{2,1,0:T(8,128)(2,1)S(1)}, bf16[6,512,256]{2,1,0:T(8,128)(2,1)S(1)}, u32[]{:S(2)}, u32[]{:S(2)}) collective-permute-start(bf16[6,512,256]{2,1,0:T(8,128)(2,1)S(1)} %pad_maximum_fusion), channel_id=1, source_target_pairs={{1,0},{0,1},{3,2},{2,3},{5,4},{4,5},{7,6},{6,7},{9,8},{8,9},{11,10... | collective-permute-start | bytes 4718600 | tf_op jit(solution)/shard_map/ppermute | solution.py:43
  82.5 4.6 %collective-permute-start.10 = (bf16[4,512,256]{2,1,0:T(8,128)(2,1)S(1)}, bf16[4,512,256]{2,1,0:T(8,128)(2,1)S(1)}, u32[]{:S(2)}, u32[]{:S(2)}) collective-permute-start(bf16[4,512,256]{2,1,0:T(8,128)(2,1)S(1)} %collective-permute-done.6.refs_1_), channel_id=1, source_target_pairs={{1,0},{0,1},{3,2},{2,3},{5,4},{4,5},{7,6},{6,7},{9,8},{8,9},{11,10... | collective-permute-start | bytes 3145736 | tf_op jit(solution)/shard_map/ppermute | solution.py:43

commit v14 on v13

--- a/solution.py
+++ b/solution.py
@@ -281,17 +281,16 @@
     pieces = [(portion, 0, 4, 0, HERE, False), (near_x, 0, 2, 0, X, False)]
     whole = put(None, pieces, shape, shard.dtype)
     near_y, whole = lax.optimization_barrier((near_y, whole))
-    pieces = []
-    for array, offsets in ((near_y, Y), (near_z, Z)):
-        pieces += [(array, 0, 4, 0, offsets, False), (swap(array[:2]), 0, 2, 0, offsets, True)]
-    whole = put(whole, pieces, shape, shard.dtype)
-    near_x, near_y, near_z, far_x, whole = lax.optimization_barrier(
-        (near_x, near_y, near_z, far_x, whole)
+    pieces = [(near_y, 0, 4, 0, Y, False), (swap(near_y[:2]), 0, 2, 0, Y, True)]
+    whole = put(whole, [*pieces, (near_z, 0, 4, 0, Z, False)], shape, shard.dtype)
+    near_z_there = swap(near_z[:2])
+    near_x, near_y, near_z, near_z_there, far_x, whole = lax.optimization_barrier(
+        (near_x, near_y, near_z, near_z_there, far_x, whole)
     )
     rest = swap(jnp.concatenate([near_x, near_y[2:], near_z[2:]], axis=0))
     far_there = swap(far_x)
     for pieces in (
-        [(far_x, 0, 2, 2, X, False), (far_x, 2, 2, 0, XX, False)],
+        [(far_x, 0, 2, 2, X, False), (far_x, 2, 2, 0, XX, False), (near_z_there, 0, 2, 0, Z, True)],
         [(rest, 0, 2, 0, X, True), (rest, 2, 2, 2, Y, True), (rest, 4, 2, 2, Z, True)],
         [(far_there, 0, 2, 2, X, True), (far_there, 2, 2, 0, XX, True)],
     ):

time: 88.5 us -> 87.4 us (0.988)
  waiting for transfers between devices: 12.2 us -> 10.6 us
    ppermute x5, waiting for transfers between devices: 1.7 us -> 0.13 us  [swap(): return lax.ppermute(value, AXES, pairs)]
  transfers between devices with their start and end apart: 11 -> 11, of which waited for: 6 -> 5; matrix products, arithmetic and copies ran while one was open for 0% -> 0% of each run, Pallas kernels for 10% -> 10%
where the time goes in v14:
time: 87.4 us; the launch traced here: 86.9 us
  starting transfers between devices  44.9 us (51%)
  blocking collectives  17.7 us (20%)
  Pallas kernels  12.2 us (14%)
  waiting for transfers between devices  10.6 us (12%)
    ppermute x5, starting transfers between devices, swap(): return lax.ppermute(value, AXES, pairs)  18.2 us
    all_to_all x1, blocking collectives, per_device(): lax.all_to_all(payload, 'rep', 0, 0).reshape(-1, payload.shape[-1])  17.7 us
    ppermute x4, starting transfers between devices, fetch(): return lax.ppermute(value, AXES, pairs)  14.1 us
    ppermute x2, starting transfers between devices, collect(): return lax.ppermute(shard, AXES, pairs)  12.6 us
    pallas_call x5, Pallas kernels, put(): pl.pallas_call(kernel, out_shape=jax.ShapeDtypeStruct(shape, dtype), in_s...  6.32 us
    ppermute x4, waiting for transfers between devices, fetch(): return lax.ppermute(value, AXES, pairs)  5.35 us
    ppermute x2, waiting for transfers between devices, collect(): return lax.ppermute(shard, AXES, pairs)  5.12 us
    pallas_call x1, Pallas kernels, keep(): pl.pallas_call(keep_kernel, out_shape=jax.ShapeDtypeStruct(error.shape, j...  2.3 us
  transfers between devices with their start and end apart: 11, of which 5 were waited for; matrix products, arithmetic and copies ran while one was open for 0% of the time, Pallas kernels for 10%

profile of v14, /device:TPU:1, one launch (start us, length us, event | category | flops | bytes accessed | tf_op | source)
XLA Modules:
  0.0 86.9 jit_solution(24136926814023536)
XLA Ops:
  0.6 1.8 %shard_map.84 = (f32[16,8,384]{2,1,0:T(8,128)S(1)}, f32[512,256]{1,0:T(8,128)S(1)}, f32[512,256]{1,0:T(8,128)S(1)}) custom-call(s32[1,8]{1,0:T(1,128)} %picks_hbm.3, f32[512,256]{1,0:T(8,128)} %bitcast.12, f32[512,256]{1,0:T(8,128)} %bitcast.14, f32[512,256]{1,0:T(8,128)} %momentum.1, f32[512,256]{1,0:T(8,128)} %params.1), custom_call_target="tpu_custom_call" | custom-call | flops 100000 | bytes 2000000 | tf_op jit(solution)/shard_map/pallas_call | solution.py:116
  2.5 17.7 %all_to_all.5 = f32[16,8,384]{2,1,0:T(8,128)S(1)} all-to-all(f32[16,8,384]{2,1,0:T(8,128)S(1)} %get-tuple-element.28), channel_id=1, replica_groups=mesh['rep'=16,'fsdp'=32] {'rep'}, dimensions={0} | all-to-all | bytes 393216 | tf_op jit(solution)/shard_map/all_to_all | solution.py:307
  20.2 0.4 shard_map.85
  20.6 4.0 %collective-permute-start = (bf16[512,256]{1,0:T(8,128)(2,1)S(1)}, bf16[512,256]{1,0:T(8,128)(2,1)S(1)}, u32[]{:S(2)}, u32[]{:S(2)}) collective-permute-start(bf16[512,256]{1,0:T(8,128)(2,1)S(1)} %shard_map.85), channel_id=1, source_target_pairs={{2,0},{11,1},{8,2},{1,3},{14,4},{7,5},{4,6},{13,7},{10,8},{3,9},{0... | collective-permute-start | bytes 786440 | tf_op jit(solution)/shard_map/ppermute | solution.py:52
  24.7 8.6 %collective-permute-start.1 = (bf16[512,256]{1,0:T(8,128)(2,1)S(1)}, bf16[512,256]{1,0:T(8,128)(2,1)S(1)}, u32[]{:S(2)}, u32[]{:S(2)}) collective-permute-start(bf16[512,256]{1,0:T(8,128)(2,1)S(1)} %shard_map.85), channel_id=1, source_target_pairs={{48,0},{57,1},{54,2},{63,3},{60,4},{53,5},{50,6},{59,7},{56,8},{49... | collective-permute-start | bytes 786440 | tf_op jit(solution)/shard_map/ppermute | solution.py:52
  33.3 2.3 %shard_map.86 = f32[512,256]{1,0:T(8,128)} custom-call(s32[1,8]{1,0:T(1,128)} %picks_hbm.3, f32[512,256]{1,0:T(8,128)} %bitcast.13, f32[512,256]{1,0:T(8,128)} %bitcast.15), custom_call_target="tpu_custom_call" | custom-call | flops 1000000 | bytes 2000000 | tf_op jit(solution)/shard_map/pallas_call | solution.py:157
  35.6 1.4 %shard_map.87 = (f32[512,256]{1,0:T(8,128)}, f32[512,256]{1,0:T(8,128)}) custom-call(f32[128,384]{1,0:T(8,128)S(1)} %bitcast.10, f32[512,256]{1,0:T(8,128)S(1)} %get-tuple-element.29.momentum, f32[512,256]{1,0:T(8,128)S(1)} %get-tuple-element.30.params), custom_call_target="tpu_custom_call" | custom-call | flops 100000000 | bytes 3000000 | tf_op jit(solution)/shard_map/pallas_call | solution.py:205
  36.9 0.0 collective-permute-done
  36.9 5.1 %collective-permute-done.1 = bf16[512,256]{1,0:T(8,128)(2,1)S(1)} collective-permute-done((bf16[512,256]{1,0:T(8,128)(2,1)S(1)}, bf16[512,256]{1,0:T(8,128)(2,1)S(1)}, u32[]{:S(2)}, u32[]{:S(2)}) %collective-permute-start.1) | collective-permute-done | bytes 262176 | tf_op jit(solution)/shard_map/ppermute | solution.py:52
  42.1 0.1 pad_maximum_fusion.3
  42.1 5.3 %collective-permute-start.3 = (bf16[2,512,256]{2,1,0:T(8,128)(2,1)S(1)}, bf16[2,512,256]{2,1,0:T(8,128)(2,1)S(1)}, u32[]{:S(2)}, u32[]{:S(2)}) collective-permute-start(bf16[2,512,256]{2,1,0:T(8,128)(2,1)S(1)} %pad_maximum_fusion.3), channel_id=1, source_target_pairs={{1,0},{0,1},{3,2},{2,3},{5,4},{4,5},{7,6},{6,7},{9,8},{8,9},{11,10... | collective-permute-start | bytes 1572872 | tf_op jit(solution)/shard_map/ppermute | solution.py:43
  47.4 4.0 %collective-permute-start.2 = (bf16[2,512,256]{2,1,0:T(8,128)(2,1)S(1)}, bf16[2,512,256]{2,1,0:T(8,128)(2,1)S(1)}, u32[]{:S(2)}, u32[]{:S(2)}) collective-permute-start(bf16[2,512,256]{2,1,0:T(8,128)(2,1)S(1)} %pad_maximum_fusion.3), channel_id=1, source_target_pairs={{32,0},{49,1},{34,2},{51,3},{36,4},{53,5},{38,6},{55,7},{40,8},{57... | collective-permute-start | bytes 1572872 | tf_op jit(solution)/shard_map/ppermute | solution.py:38
  51.4 0.0 collective-permute-done.3
  51.4 0.1 pad_maximum_fusion.1.refs_0_
  51.5 3.6 %collective-permute-start.4 = (bf16[4,512,256]{2,1,0:T(8,128)(2,1)S(1)}, bf16[4,512,256]{2,1,0:T(8,128)(2,1)S(1)}, u32[]{:S(2)}, u32[]{:S(2)}) collective-permute-start(bf16[4,512,256]{2,1,0:T(8,128)(2,1)S(1)} %pad_maximum_fusion.1.refs_0_), channel_id=1, source_target_pairs={{64,0},{449,1},{66,2},{451,3},{68,4},{453,5},{70,6},{455,7},{72,8}... | collective-permute-start | bytes 3145736 | tf_op jit(solution)/shard_map/ppermute | solution.py:38
  55.1 3.5 %collective-permute-start.5 = (bf16[4,512,256]{2,1,0:T(8,128)(2,1)S(1)}, bf16[4,512,256]{2,1,0:T(8,128)(2,1)S(1)}, u32[]{:S(2)}, u32[]{:S(2)}) collective-permute-start(bf16[4,512,256]{2,1,0:T(8,128)(2,1)S(1)} %pad_maximum_fusion.1.refs_0_), channel_id=1, source_target_pairs={{2,0},{15,1},{4,2},{1,3},{6,4},{3,5},{8,6},{5,7},{10,8},{7,9},{12,... | collective-permute-start | bytes 3145736 | tf_op jit(solution)/shard_map/ppermute | solution.py:38
  58.5 0.5 collective-permute-done.2.refs_1_
  59.0 0.1 pad_maximum_fusion.2
  59.1 3.1 %collective-permute-start.7 = (bf16[4,512,256]{2,1,0:T(8,128)(2,1)S(1)}, bf16[4,512,256]{2,1,0:T(8,128)(2,1)S(1)}, u32[]{:S(2)}, u32[]{:S(2)}) collective-permute-start(bf16[4,512,256]{2,1,0:T(8,128)(2,1)S(1)} %pad_maximum_fusion.2), channel_id=1, source_target_pairs={{32,0},{49,1},{34,2},{51,3},{36,4},{53,5},{38,6},{55,7},{40,8},{57... | collective-permute-start | bytes 3145736 | tf_op jit(solution)/shard_map/ppermute | solution.py:38
  62.2 1.2 %shard_map.88.refs_0_ = bf16[16,2,512,256]{3,2,1,0:T(8,128)(2,1)} custom-call(bf16[4,512,256]{2,1,0:T(8,128)(2,1)S(1)} %pad_maximum_fusion.1.refs_0_, bf16[2,512,256]{2,1,0:T(8,128)(2,1)S(1)} %collective-permute-done.2.refs_1_), custom_call_target="tpu_custom_call" | custom-call | bytes 3145728 | tf_op jit(solution)/shard_map/pallas_call | solution.py:250
  63.5 4.7 %collective-permute-done.4.refs_1_ = bf16[4,512,256]{2,1,0:T(8,128)(2,1)S(1)} collective-permute-done((bf16[4,512,256]{2,1,0:T(8,128)(2,1)S(1)}, bf16[4,512,256]{2,1,0:T(8,128)(2,1)S(1)}, u32[]{:S(2)}, u32[]{:S(2)}) %collective-permute-start.4) | collective-permute-done | bytes 1048608 | tf_op jit(solution)/shard_map/ppermute | solution.py:38
  68.3 3.4 %collective-permute-start.8 = (bf16[2,512,256]{2,1,0:T(8,128)(2,1)S(1)}, bf16[2,512,256]{2,1,0:T(8,128)(2,1)S(1)}, u32[]{:S(2)}, u32[]{:S(2)}) collective-permute-start(bf16[2,512,256]{2,1,0:T(8,128)(2,1)S(1)} %slice.13), channel_id=1, source_target_pairs={{1,0},{0,1},{3,2},{2,3},{5,4},{4,5},{7,6},{6,7},{9,8},{8,9},{11,10... | collective-permute-start | bytes 1572872 | tf_op jit(solution)/shard_map/ppermute | solution.py:43
  71.7 0.1 collective-permute-done.5.refs_3_
  71.8 4.8 %collective-permute-start.6 = (bf16[2,512,256]{2,1,0:T(8,128)(2,1)S(1)}, bf16[2,512,256]{2,1,0:T(8,128)(2,1)S(1)}, u32[]{:S(2)}, u32[]{:S(2)}) collective-permute-start(bf16[2,512,256]{2,1,0:T(8,128)(2,1)S(1)} %slice.16), channel_id=1, source_target_pairs={{1,0},{0,1},{3,2},{2,3},{5,4},{4,5},{7,6},{6,7},{9,8},{8,9},{11,10... | collective-permute-start | bytes 1572872 | tf_op jit(solution)/shard_map/ppermute | solution.py:43
  76.6 0.0 collective-permute-done.8.refs_2_
  76.6 1.6 %shard_map.89.refs_0_ = bf16[16,2,512,256]{3,2,1,0:T(8,128)(2,1)} custom-call(bf16[16,2,512,256]{3,2,1,0:T(8,128)(2,1)} %shard_map.88.refs_0_, bf16[4,512,256]{2,1,0:T(8,128)(2,1)S(1)} %collective-permute-done.4.refs_1_, bf16[2,512,256]{2,1,0:T(8,128)(2,1)S(1)} %collective-permute-done.8.refs_2_, ...), custom_call_target="tpu_custom_call", output_to_operand_aliasing={{}: (0, {})} | custom-call | bytes 5242880 | tf_op jit(solution)/shard_map/pallas_call | solution.py:250
  78.3 0.0 collective-permute-done.7.refs_1_
  78.3 0.0 collective-permute-done.6.refs_2_
  78.4 0.2 pad_maximum_fusion
  78.6 2.8 %collective-permute-start.9 = (bf16[6,512,256]{2,1,0:T(8,128)(2,1)S(1)}, bf16[6,512,256]{2,1,0:T(8,128)(2,1)S(1)}, u32[]{:S(2)}, u32[]{:S(2)}) collective-permute-start(bf16[6,512,256]{2,1,0:T(8,128)(2,1)S(1)} %pad_maximum_fusion), channel_id=1, source_target_pairs={{1,0},{0,1},{3,2},{2,3},{5,4},{4,5},{7,6},{6,7},{9,8},{8,9},{11,10... | collective-permute-start | bytes 4718600 | tf_op jit(solution)/shard_map/ppermute | solution.py:43
  81.4 1.9 %collective-permute-start.10 = (bf16[4,512,256]{2,1,0:T(8,128)(2,1)S(1)}, bf16[4,512,256]{2,1,0:T(8,128)(2,1)S(1)}, u32[]{:S(2)}, u32[]{:S(2)}) collective-permute-start(bf16[4,512,256]{2,1,0:T(8,128)(2,1)S(1)} %collective-permute-done.7.refs_1_), channel_id=1, source_target_pairs={{1,0},{0,1},{3,2},{2,3},{5,4},{4,5},{7,6},{6,7},{9,8},{8,9},{11,10... | collective-permute-start | bytes 3145736 | tf_op jit(solution)/shard_map/ppermute | solution.py:43
  83.3 1.2 %shard_map.90.refs_0_ = bf16[16,2,512,256]{3,2,1,0:T(8,128)(2,1)} custom-call(bf16[16,2,512,256]{3,2,1,0:T(8,128)(2,1)} %shard_map.89.refs_0_, bf16[4,512,256]{2,1,0:T(8,128)(2,1)S(1)} %collective-permute-done.7.refs_1_, bf16[2,512,256]{2,1,0:T(8,128)(2,1)S(1)} %collective-permute-done.6.refs_2_), custom_call_target="tpu_custom_call", output_to_operand_aliasing={{}: (0, {})} | custom-call | bytes 3145728 | tf_op jit(solution)/shard_map/pallas_call | solution.py:250
  84.5 0.0 collective-permute-done.9.refs_1_
  84.6 1.2 %shard_map.91.refs_0_ = bf16[16,2,512,256]{3,2,1,0:T(8,128)(2,1)} custom-call(bf16[16,2,512,256]{3,2,1,0:T(8,128)(2,1)} %shard_map.90.refs_0_, bf16[6,512,256]{2,1,0:T(8,128)(2,1)S(1)} %collective-permute-done.9.refs_1_), custom_call_target="tpu_custom_call", output_to_operand_aliasing={{}: (0, {})} | custom-call | bytes 3145728 | tf_op jit(solution)/shard_map/pallas_call | solution.py:250
  85.8 0.1 collective-permute-done.10.refs_1_
  85.9 1.0 %shard_map.92 = bf16[16,2,512,256]{3,2,1,0:T(8,128)(2,1)} custom-call(bf16[16,2,512,256]{3,2,1,0:T(8,128)(2,1)} %shard_map.91.refs_0_, bf16[4,512,256]{2,1,0:T(8,128)(2,1)S(1)} %collective-permute-done.10.refs_1_), custom_call_target="tpu_custom_call", output_to_operand_aliasing={{}: (0, {})} | custom-call | bytes 2097152 | tf_op jit(solution)/shard_map/pallas_call | solution.py:250
  (4 shorter events, 0.1 us)
Async XLA Ops:
  20.6 16.3 %collective-permute-start = (bf16[512,256]{1,0:T(8,128)(2,1)S(1)}, bf16[512,256]{1,0:T(8,128)(2,1)S(1)}, u32[]{:S(2)}, u32[]{:S(2)}) collective-permute-start(bf16[512,256]{1,0:T(8,128)(2,1)S(1)} %shard_map.85), channel_id=1, source_target_pairs={{2,0},{11,1},{8,2},{1,3},{14,4},{7,5},{4,6},{13,7},{10,8},{3,9},{0... | collective-permute-start | bytes 786440 | tf_op jit(solution)/shard_map/ppermute | solution.py:52
  24.7 17.4 %collective-permute-start.1 = (bf16[512,256]{1,0:T(8,128)(2,1)S(1)}, bf16[512,256]{1,0:T(8,128)(2,1)S(1)}, u32[]{:S(2)}, u32[]{:S(2)}) collective-permute-start(bf16[512,256]{1,0:T(8,128)(2,1)S(1)} %shard_map.85), channel_id=1, source_target_pairs={{48,0},{57,1},{54,2},{63,3},{60,4},{53,5},{50,6},{59,7},{56,8},{49... | collective-permute-start | bytes 786440 | tf_op jit(solution)/shard_map/ppermute | solution.py:52
  42.1 9.2 %collective-permute-start.3 = (bf16[2,512,256]{2,1,0:T(8,128)(2,1)S(1)}, bf16[2,512,256]{2,1,0:T(8,128)(2,1)S(1)}, u32[]{:S(2)}, u32[]{:S(2)}) collective-permute-start(bf16[2,512,256]{2,1,0:T(8,128)(2,1)S(1)} %pad_maximum_fusion.3), channel_id=1, source_target_pairs={{1,0},{0,1},{3,2},{2,3},{5,4},{4,5},{7,6},{6,7},{9,8},{8,9},{11,10... | collective-permute-start | bytes 1572872 | tf_op jit(solution)/shard_map/ppermute | solution.py:43
  47.4 11.6 %collective-permute-start.2 = (bf16[2,512,256]{2,1,0:T(8,128)(2,1)S(1)}, bf16[2,512,256]{2,1,0:T(8,128)(2,1)S(1)}, u32[]{:S(2)}, u32[]{:S(2)}) collective-permute-start(bf16[2,512,256]{2,1,0:T(8,128)(2,1)S(1)} %pad_maximum_fusion.3), channel_id=1, source_target_pairs={{32,0},{49,1},{34,2},{51,3},{36,4},{53,5},{38,6},{55,7},{40,8},{57... | collective-permute-start | bytes 1572872 | tf_op jit(solution)/shard_map/ppermute | solution.py:38
  51.5 16.8 %collective-permute-start.4 = (bf16[4,512,256]{2,1,0:T(8,128)(2,1)S(1)}, bf16[4,512,256]{2,1,0:T(8,128)(2,1)S(1)}, u32[]{:S(2)}, u32[]{:S(2)}) collective-permute-start(bf16[4,512,256]{2,1,0:T(8,128)(2,1)S(1)} %pad_maximum_fusion.1.refs_0_), channel_id=1, source_target_pairs={{64,0},{449,1},{66,2},{451,3},{68,4},{453,5},{70,6},{455,7},{72,8}... | collective-permute-start | bytes 3145736 | tf_op jit(solution)/shard_map/ppermute | solution.py:38
  55.1 16.8 %collective-permute-start.5 = (bf16[4,512,256]{2,1,0:T(8,128)(2,1)S(1)}, bf16[4,512,256]{2,1,0:T(8,128)(2,1)S(1)}, u32[]{:S(2)}, u32[]{:S(2)}) collective-permute-start(bf16[4,512,256]{2,1,0:T(8,128)(2,1)S(1)} %pad_maximum_fusion.1.refs_0_), channel_id=1, source_target_pairs={{2,0},{15,1},{4,2},{1,3},{6,4},{3,5},{8,6},{5,7},{10,8},{7,9},{12,... | collective-permute-start | bytes 3145736 | tf_op jit(solution)/shard_map/ppermute | solution.py:38
  59.1 19.2 %collective-permute-start.7 = (bf16[4,512,256]{2,1,0:T(8,128)(2,1)S(1)}, bf16[4,512,256]{2,1,0:T(8,128)(2,1)S(1)}, u32[]{:S(2)}, u32[]{:S(2)}) collective-permute-start(bf16[4,512,256]{2,1,0:T(8,128)(2,1)S(1)} %pad_maximum_fusion.2), channel_id=1, source_target_pairs={{32,0},{49,1},{34,2},{51,3},{36,4},{53,5},{38,6},{55,7},{40,8},{57... | collective-permute-start | bytes 3145736 | tf_op jit(solution)/shard_map/ppermute | solution.py:38
  68.3 8.4 %collective-permute-start.8 = (bf16[2,512,256]{2,1,0:T(8,128)(2,1)S(1)}, bf16[2,512,256]{2,1,0:T(8,128)(2,1)S(1)}, u32[]{:S(2)}, u32[]{:S(2)}) collective-permute-start(bf16[2,512,256]{2,1,0:T(8,128)(2,1)S(1)} %slice.13), channel_id=1, source_target_pairs={{1,0},{0,1},{3,2},{2,3},{5,4},{4,5},{7,6},{6,7},{9,8},{8,9},{11,10... | collective-permute-start | bytes 1572872 | tf_op jit(solution)/shard_map/ppermute | solution.py:43
  71.8 6.4 %collective-permute-start.6 = (bf16[2,512,256]{2,1,0:T(8,128)(2,1)S(1)}, bf16[2,512,256]{2,1,0:T(8,128)(2,1)S(1)}, u32[]{:S(2)}, u32[]{:S(2)}) collective-permute-start(bf16[2,512,256]{2,1,0:T(8,128)(2,1)S(1)} %slice.16), channel_id=1, source_target_pairs={{1,0},{0,1},{3,2},{2,3},{5,4},{4,5},{7,6},{6,7},{9,8},{8,9},{11,10... | collective-permute-start | bytes 1572872 | tf_op jit(solution)/shard_map/ppermute | solution.py:43
  78.6 6.0 %collective-permute-start.9 = (bf16[6,512,256]{2,1,0:T(8,128)(2,1)S(1)}, bf16[6,512,256]{2,1,0:T(8,128)(2,1)S(1)}, u32[]{:S(2)}, u32[]{:S(2)}) collective-permute-start(bf16[6,512,256]{2,1,0:T(8,128)(2,1)S(1)} %pad_maximum_fusion), channel_id=1, source_target_pairs={{1,0},{0,1},{3,2},{2,3},{5,4},{4,5},{7,6},{6,7},{9,8},{8,9},{11,10... | collective-permute-start | bytes 4718600 | tf_op jit(solution)/shard_map/ppermute | solution.py:43
  81.4 4.6 %collective-permute-start.10 = (bf16[4,512,256]{2,1,0:T(8,128)(2,1)S(1)}, bf16[4,512,256]{2,1,0:T(8,128)(2,1)S(1)}, u32[]{:S(2)}, u32[]{:S(2)}) collective-permute-start(bf16[4,512,256]{2,1,0:T(8,128)(2,1)S(1)} %collective-permute-done.7.refs_1_), channel_id=1, source_target_pairs={{1,0},{0,1},{3,2},{2,3},{5,4},{4,5},{7,6},{6,7},{9,8},{8,9},{11,10... | collective-permute-start | bytes 3145736 | tf_op jit(solution)/shard_map/ppermute | solution.py:43
